TPU v7x, 32 devices: a whole 2x2x4 slice. The times are simulated.
32 devices in a mesh: expert: 16 (over z, y, core), tensor: 2 (over x).
Axes of the slice: x: 2, y: 2, z: 4, core: 2. Of those that a mesh axis runs over, the one named last changes fastest.
Arguments:
- tokens: bfloat16 [2048, 2048], P('expert', 'tensor'), may hold values from -6 to 6
- grad_out: bfloat16 [2048, 2048], P('expert', 'tensor'), may hold values from -6 to 6
- gates: float32 [2048, 6], P('expert'), may hold values from 0.1 to 1
- expert_ids: int32 [2048, 6], P('expert'), may hold values from 0 to 15, all different within a row; in each aligned block of 128 rows (0 to 127, 128 to 255, ...) at most 64 rows name the same one
- w_gate: bfloat16 [16, 2048, 1408], P('expert', None, 'tensor'), may hold values from -0.125 to 0.125
- w_up: bfloat16 [16, 2048, 1408], P('expert', None, 'tensor'), may hold values from -0.125 to 0.125
- w_down: bfloat16 [16, 1408, 2048], P('expert', 'tensor'), may hold values from -0.15625 to 0.15625
Outputs:
- mixed: bfloat16 [2048, 2048], P('expert', 'tensor')
- grad_tokens: bfloat16 [2048, 2048], P('expert', 'tensor')
- grad_gates: float32 [2048, 6], P('expert')
- grad_w_gate: bfloat16 [16, 2048, 1408], P('expert', None, 'tensor')
- grad_w_up: bfloat16 [16, 2048, 1408], P('expert', None, 'tensor')
- grad_w_down: bfloat16 [16, 1408, 2048], P('expert', 'tensor')
Inputs may be any that keep to these rules, and one draw needn't show every extreme that they name: `expert_ids`: each row names 6 different experts. In each aligned block of 128 rows (the tokens of one index of expert) no expert is named by more than 64 rows, and some block names some expert exactly 64 times.
All inputs are finite; a program needn't handle non-finite values.
Results may differ from a plain program's by a relative error of at most 0.0064.
Values may be sent and summed in bfloat16 or wider, within the bound.
No kernel may reach another device: no remote copies, remote signals or barrier semaphores. Data moves between devices by JAX's collectives and lax.ppermute only.
A program may use at most 128 MiB of HBM per device.

v0:
```python
import jax
import jax.numpy as jnp
from jax import lax
from jax.sharding import PartitionSpec as P


def body(tokens, grad_out, gates, expert_ids, w_gate, w_up, w_down):
    expert_count = lax.axis_size("expert")
    tok_count = expert_ids.shape[0]
    top_count = expert_ids.shape[1]
    capacity = tok_count * top_count * 4 // (3 * expert_count)
    slot_total = expert_count * capacity
    flat_ids = expert_ids.reshape(-1)
    member = (flat_ids[:, None] == jnp.arange(expert_count, dtype=jnp.int32)[None, :]).astype(
        jnp.int32
    )
    earlier = jnp.cumsum(member, axis=0) - member
    position = jnp.sum(earlier * member, axis=1)
    slot_index = flat_ids * capacity + position
    pair_token = jnp.arange(tok_count * top_count, dtype=jnp.int32) // top_count
    pair_gate = gates.reshape(-1)[:, None]

    def pack(rows, scaled):
        picked = rows[pair_token]
        if scaled:
            picked = (pair_gate * picked.astype(jnp.float32)).astype(jnp.bfloat16)
        buffer = jnp.zeros((slot_total, rows.shape[1]), jnp.bfloat16).at[slot_index].set(picked)
        return buffer.reshape(expert_count, capacity, rows.shape[1])

    def dispatch(rows, scaled):
        arrived = lax.all_to_all(
            pack(rows, scaled), "expert", split_axis=0, concat_axis=0, tiled=True
        )
        arrived = arrived.reshape(slot_total, rows.shape[1])
        return lax.all_gather(arrived, "tensor", axis=1, tiled=True)

    def give_back(partial_value):
        shares = lax.psum_scatter(partial_value, "tensor", scatter_dimension=1, tiled=True).astype(
            jnp.bfloat16
        )
        width = shares.shape[1]
        shares = shares.reshape(expert_count, capacity, width)
        returned = lax.all_to_all(shares, "expert", split_axis=0, concat_axis=0, tiled=True)
        return returned.reshape(slot_total, width)[slot_index].reshape(tok_count, top_count, width)

    weight_gate = w_gate[0]
    weight_up = w_up[0]
    weight_down = w_down[0]
    full_rows = dispatch(tokens, False)
    gate_pre = jnp.dot(full_rows, weight_gate, preferred_element_type=jnp.float32)
    up_pre = jnp.dot(full_rows, weight_up, preferred_element_type=jnp.float32)
    sig = jax.nn.sigmoid(gate_pre)
    act = (gate_pre * sig * up_pre).astype(jnp.bfloat16)
    outputs = give_back(jnp.dot(act, weight_down, preferred_element_type=jnp.float32)).astype(
        jnp.float32
    )
    mixed = jnp.sum(gates[:, :, None] * outputs, axis=1).astype(jnp.bfloat16)
    gate_terms = jnp.sum(grad_out.astype(jnp.float32)[:, None, :] * outputs, axis=2)
    grad_gates = lax.psum(gate_terms, "tensor")
    grad_rows = dispatch(grad_out, True)
    contract_last = (((1,), (1,)), ((), ()))
    contract_first = (((0,), (0,)), ((), ()))
    grad_act = lax.dot_general(
        grad_rows, weight_down, contract_last, preferred_element_type=jnp.float32
    )
    grad_gate_pre = (grad_act * up_pre * sig * (1.0 + gate_pre * (1.0 - sig))).astype(jnp.bfloat16)
    grad_up_pre = (grad_act * gate_pre * sig).astype(jnp.bfloat16)
    grad_down = lax.dot_general(
        act, grad_rows, contract_first, preferred_element_type=jnp.float32
    ).astype(jnp.bfloat16)
    grad_gate = lax.dot_general(
        full_rows, grad_gate_pre, contract_first, preferred_element_type=jnp.float32
    ).astype(jnp.bfloat16)
    grad_up = lax.dot_general(
        full_rows, grad_up_pre, contract_first, preferred_element_type=jnp.float32
    ).astype(jnp.bfloat16)
    input_terms = lax.dot_general(
        grad_gate_pre, weight_gate, contract_last, preferred_element_type=jnp.float32
    ) + lax.dot_general(grad_up_pre, weight_up, contract_last, preferred_element_type=jnp.float32)
    input_pairs = give_back(input_terms).astype(jnp.float32)
    grad_tokens = jnp.sum(input_pairs, axis=1).astype(jnp.bfloat16)
    return (mixed, grad_tokens, grad_gates, grad_gate[None], grad_up[None], grad_down[None])


def solution(mesh):
    placed = (
        P("expert", "tensor"),
        P("expert", "tensor"),
        P("expert", None),
        P("expert", None),
        P("expert", None, "tensor"),
        P("expert", None, "tensor"),
        P("expert", "tensor", None),
    )
    return jax.shard_map(
        body,
        mesh=mesh,
        in_specs=placed,
        out_specs=(
            P("expert", "tensor"),
            P("expert", "tensor"),
            P("expert", None),
            P("expert", None, "tensor"),
            P("expert", None, "tensor"),
            P("expert", "tensor", None),
        ),
        check_vma=False,
    )
```

profile of v0, /device:TPU:18, one launch (start us, length us, event | category | flops | bytes accessed | tf_op | source)
XLA Modules:
  0.0 523.3 jit_solution(18409795312587027390)
XLA Ops:
  7.2 0.0 all-gather.3.cloned.1.call-start
  7.3 0.8 broadcast_multiply_fusion
  8.1 0.8 copy.22
  8.9 0.1 eq.29
  9.0 0.1 eq.25
  9.2 0.1 copy.21
  9.3 0.1 mul.76
  9.5 1.7 reduce-window.6
  11.2 0.3 slice_reduce_fusion
  11.5 0.1 fusion.22
  11.6 24.7 %scatter_custom_fusion = bf16[1024,1024]{1,0:T(8,128)(2,1)} fusion(s32[768]{0:T(1024)S(1)} %fusion.24, bf16[128,1024]{1,0:T(8,128)(2,1)} %param.7, s32[1024]{0:T(1024)S(1)} %pad_clamp_fusion.1, bf16[]{:T(256)} %constant.8.clone.1), kind=kCustom, calls=%fused_computation.32 | custom fusion | bytes 2097664 | tf_op jit(solution)/shard_map/scatter | solution.py:27
  36.3 54.0 %all_to_all.20 = bf16[16,64,1024]{2,1,0:T(8,128)(2,1)} all-to-all(bf16[16,64,1024]{2,1,0:T(8,128)(2,1)} %bitcast.71), channel_id=1, replica_groups=mesh['expert'=16,'tensor'=2] {'expert'}, dimensions={0} | all-to-all | bytes 4194304 | tf_op jit(solution)/shard_map/all_to_all | solution.py:31
  90.3 0.0 all-gather.3.cloned.1.call-update
  90.3 0.2 all-gather.5.cloned.1.call-start
  90.6 0.1 copy.20
  90.7 0.1 mul.81
  90.8 15.4 %scatter_custom_fusion.1 = bf16[1024,1024]{1,0:T(8,128)(2,1)} fusion(s32[768]{0:T(1024)S(1)} %fusion.24, f32[768]{0:T(1024)S(1)} %mul.81, bf16[]{:T(256)} %constant.8.clone.1, bf16[128,1024]{1,0:T(8,128)(2,1)S(1)} %copy-done.2, s32[1024]{0:T(1024)S(1)} %pad_clamp_fusion.1), kind=kCustom, calls=%fused_computation.31 | custom fusion | flops 2359296 | bytes 2367490 | tf_op jit(solution)/shard_map/scatter | solution.py:27
  106.2 52.5 %all_to_all.21 = bf16[16,64,1024]{2,1,0:T(8,128)(2,1)} all-to-all(bf16[16,64,1024]{2,1,0:T(8,128)(2,1)} %bitcast.70), channel_id=1, replica_groups=mesh['expert'=16,'tensor'=2] {'expert'}, dimensions={0} | all-to-all | bytes 4194304 | tf_op jit(solution)/shard_map/all_to_all | solution.py:31
  158.8 0.0 all-gather.5.cloned.1.call-update
  158.8 0.0 reduce-scatter.5.cloned.1.call-start
  158.8 0.0 all-gather.3.cloned.1.call-done
  158.9 8.0 %fusion.8 = f32[1024,704]{0,1:T(8,128)} fusion(bf16[1024,2048]{1,0:T(8,128)(2,1)} %all-gather.3.cloned.1.call-done, bf16[1,2048,704]{1,2,0:T(8,128)(2,1)} %param.12), kind=kOutput, calls=%fused_computation.21 | convolution fusion | flops 2952790016 | bytes 9961472 | tf_op jit(solution)/shard_map/dot_general | solution.py:51
  166.9 4.8 fusion.12
  171.6 42.8 %all-gather.5.cloned.1.call-done = bf16[1024,2048]{1,0:T(8,128)(2,1)} async-done(((bf16[1024,1024]{1,0:T(8,128)(2,1)}), bf16[1024,2048]{1,0:T(8,128)(2,1)}) %all-gather.5.cloned.1.call-update) | async-done | bytes 4194320 | tf_op jit(solution)/shard_map/all_gather | solution.py:35
  214.5 8.7 %multiply_convert_fusion.1 = (bf16[1024,704]{0,1:T(8,128)(2,1)S(1)}, bf16[1024,704]{0,1:T(8,128)(2,1)S(1)}, bf16[1024,704]{0,1:T(8,128)(2,1)}) fusion(f32[1024,704]{0,1:T(8,128)} %fusion.12, f32[1024,704]{0,1:T(8,128)} %fusion.8, bf16[1024,2048]{1,0:T(8,128)(2,1)} %all-gather.5.cloned.1.call-done, bf16[1,704,2048]{2,1,0:T(8,128)(2,1)S(1)} %copy-done), kind=kOutput, calls=%fused_computation.27 | convolution fusion | flops 2964324352 | bytes 17170432 | tf_op jit(solution)/shard_map/dot_general | solution.py:63
  223.1 3.5 fusion.10
  226.7 5.9 %convolution_add_fusion = f32[1024,2048]{1,0:T(8,128)} fusion(f32[1024,2048]{1,0:T(8,128)S(1)} %fusion.10, bf16[1024,704]{0,1:T(8,128)(2,1)S(1)} %get-tuple-element.14, bf16[1,2048,704]{1,2,0:T(8,128)(2,1)S(1)} %copy-done.9), kind=kOutput, calls=%fused_computation.8 | convolution fusion | flops 2954887168 | bytes 21102592 | tf_op jit(solution)/shard_map/dot_general | solution.py:79
  232.6 0.0 reduce-scatter.5.cloned.1.call-update
  232.6 0.0 reduce-scatter.3.cloned.1.call-start
  232.7 7.0 %fusion.5 = f32[1024,2048]{1,0:T(8,128)} fusion(bf16[1024,704]{0,1:T(8,128)(2,1)} %get-tuple-element.16, bf16[1,704,2048]{2,1,0:T(8,128)(2,1)S(1)} %copy-done), kind=kOutput, calls=%fused_computation.18 | convolution fusion | flops 2952790016 | bytes 12713984 | tf_op jit(solution)/shard_map/dot_general | solution.py:54
  239.7 92.3 %reduce-scatter.5.cloned.1.call-done = f32[1024,1024]{1,0:T(8,128)} async-done(((f32[1024,2048]{1,0:T(8,128)}), f32[1024,1024]{1,0:T(8,128)}) %reduce-scatter.5.cloned.1.call-update) | async-done | bytes 4194320 | tf_op jit(solution)/shard_map/reduce_scatter | solution.py:38
  332.0 3.8 convert_element_type.66
  335.9 6.0 %all-to-all-start.3 = ((bf16[16,64,1024]{2,1,0:T(8,128)(2,1)}), bf16[16,64,1024]{2,1,0:T(8,128)(2,1)S(1)}, u32[]{:S(2)}, u32[]{:S(2)}) async-start(bf16[16,64,1024]{2,1,0:T(8,128)(2,1)} %bitcast.67), calls=%async_computation.5 | async-start | bytes 4194304 | tf_op jit(solution)/shard_map/all_to_all | solution.py:43
  341.9 91.7 %reduce-scatter.3.cloned.1.call-done = f32[1024,1024]{1,0:T(8,128)} async-done(((f32[1024,2048]{1,0:T(8,128)}), f32[1024,1024]{1,0:T(8,128)}) %reduce-scatter.3.cloned.1.call-update) | async-done | bytes 4194320 | tf_op jit(solution)/shard_map/reduce_scatter | solution.py:38
  433.5 3.8 convert_element_type.58
  437.4 6.6 %all-to-all-start.1 = ((bf16[16,64,1024]{2,1,0:T(8,128)(2,1)}), bf16[16,64,1024]{2,1,0:T(8,128)(2,1)}, u32[]{:S(2)}, u32[]{:S(2)}) async-start(bf16[16,64,1024]{2,1,0:T(8,128)(2,1)} %bitcast.66), calls=%async_computation.2 | async-start | bytes 4194304 | tf_op jit(solution)/shard_map/all_to_all | solution.py:43
  444.1 7.5 %fusion = bf16[1,704,2048]{2,1,0:T(8,128)(2,1)} fusion(bf16[1024,704]{0,1:T(8,128)(2,1)} %get-tuple-element.16, bf16[1024,2048]{1,0:T(8,128)(2,1)} %all-gather.5.cloned.1.call-done), kind=kOutput, calls=%fused_computation.13 | convolution fusion | flops 2954231808 | bytes 8519680 | tf_op jit(solution)/shard_map/dot_general | solution.py:68
  451.6 4.5 fusion.2
  456.0 4.5 fusion.1
  460.5 3.6 gather_fusion.1
  464.0 2.5 reshape.153
  466.5 2.2 reduce_sum.44
  468.7 22.8 %all-to-all-done.1 = bf16[16,64,1024]{2,1,0:T(8,128)(2,1)} async-done(((bf16[16,64,1024]{2,1,0:T(8,128)(2,1)}), bf16[16,64,1024]{2,1,0:T(8,128)(2,1)}, u32[]{:S(2)}, u32[]{:S(2)}) %all-to-all-start.1) | async-done | bytes 2097184 | tf_op jit(solution)/shard_map/all_to_all | solution.py:43
  491.5 6.4 %gather_fusion = bf16[768,1024]{1,0:T(8,128)(2,1)} fusion(bf16[1024,1024]{1,0:T(8,128)(2,1)} %bitcast.7, s32[1024]{0:T(1024)S(1)} %pad_clamp_fusion), kind=kCustom, calls=%fused_computation.1 | custom fusion | bytes 3148800 | tf_op jit(solution)/shard_map/gather | solution.py:44
  498.0 4.0 reshape.154
  502.0 4.8 multiply_reduce_fusion
  506.8 8.9 %psum.7 = f32[128,6]{1,0:T(8,128)S(1)} all-reduce(f32[128,6]{1,0:T(8,128)S(1)} %get-tuple-element.12), channel_id=1, replica_groups=mesh['expert'=16,'tensor'=2] {'tensor'}, use_global_device_ids=true, to_apply=%region_10.11 | all-reduce | flops 768 | bytes 6144 | tf_op jit(solution)/shard_map/psum | solution.py:59
  515.6 0.7 copy.26
  (37 shorter events, 0.2 us)
Async XLA Ops:
  7.2 207.3 %copy-start = (bf16[1,704,2048]{2,1,0:T(8,128)(2,1)S(1)}, bf16[1,704,2048]{2,1,0:T(8,128)(2,1)}, u32[]{:S(2)}) copy-start(bf16[1,704,2048]{2,1,0:T(8,128)(2,1)} %param.13) | copy-start | bytes 8650756
  7.2 151.7 %all-gather.3.cloned.1.call-start = ((), (), s32[]{:S(2)}) async-start(), calls=%async_computation.6 | async-start | bytes 6291456 | tf_op jit(solution)/shard_map/all_gather | solution.py:35
  36.3 54.3 %copy-start.4 = (f32[128,6]{0,1:T(8,128)S(1)}, f32[128,6]{0,1:T(8,128)}, u32[]{:S(2)}) copy-start(f32[128,6]{0,1:T(8,128)} %param.9) | copy-start | bytes 9220
  36.3 54.5 %copy-start.2 = (bf16[128,1024]{1,0:T(8,128)(2,1)S(1)}, bf16[128,1024]{1,0:T(8,128)(2,1)}, u32[]{:S(2)}) copy-start(bf16[128,1024]{1,0:T(8,128)(2,1)} %param.8) | copy-start | bytes 786436
  90.3 124.1 %all-gather.5.cloned.1.call-start = ((), (), s32[]{:S(2)}) async-start(), calls=%async_computation.8 | async-start | bytes 6291456 | tf_op jit(solution)/shard_map/all_gather | solution.py:35
  158.8 173.2 %reduce-scatter.5.cloned.1.call-start = ((), (), s32[]{:S(2)}) async-start(), calls=%async_computation.9 | async-start | bytes 12582912 | tf_op jit(solution)/shard_map/reduce_scatter | solution.py:38
  158.9 8.0 %copy-start.5 = (bf16[1024,2048]{1,0:T(8,128)(2,1)S(1)}, bf16[1024,2048]{1,0:T(8,128)(2,1)}, u32[]{:S(2)}) copy-start(bf16[1024,2048]{1,0:T(8,128)(2,1)} %all-gather.3.cloned.1.call-done) | copy-start | bytes 12582916
  158.9 8.0 %copy-start.7 = (bf16[1,2048,704]{1,2,0:T(8,128)(2,1)S(1)}, bf16[1,2048,704]{1,2,0:T(8,128)(2,1)}, u32[]{:S(2)}) copy-start(bf16[1,2048,704]{1,2,0:T(8,128)(2,1)} %param.11) | copy-start | bytes 8650756
  214.5 8.7 %copy-start.8 = (bf16[1,2048,704]{1,2,0:T(8,128)(2,1)S(1)}, bf16[1,2048,704]{1,2,0:T(8,128)(2,1)}, u32[]{:S(2)}) copy-start(bf16[1,2048,704]{1,2,0:T(8,128)(2,1)} %param.11) | copy-start | bytes 8650756
  223.1 3.5 copy-start.12
  223.1 3.6 copy-start.10
  223.1 3.6 copy-start.9
  232.6 200.9 %reduce-scatter.3.cloned.1.call-start = ((), (), s32[]{:S(2)}) async-start(), calls=%async_computation.7 | async-start | bytes 12582912 | tf_op jit(solution)/shard_map/reduce_scatter | solution.py:38
  335.9 101.5 %all-to-all-start.3 = ((bf16[16,64,1024]{2,1,0:T(8,128)(2,1)}), bf16[16,64,1024]{2,1,0:T(8,128)(2,1)S(1)}, u32[]{:S(2)}, u32[]{:S(2)}) async-start(bf16[16,64,1024]{2,1,0:T(8,128)(2,1)} %bitcast.67), calls=%async_computation.5 | async-start | bytes 4194304 | tf_op jit(solution)/shard_map/all_to_all | solution.py:43
  437.3 6.6 %copy-start.3 = (bf16[128,1024]{1,0:T(8,128)(2,1)S(1)}, bf16[128,1024]{1,0:T(8,128)(2,1)}, u32[]{:S(2)}) copy-start(bf16[128,1024]{1,0:T(8,128)(2,1)} %param.8) | copy-start | bytes 786436
  437.4 54.2 %all-to-all-start.1 = ((bf16[16,64,1024]{2,1,0:T(8,128)(2,1)}), bf16[16,64,1024]{2,1,0:T(8,128)(2,1)}, u32[]{:S(2)}, u32[]{:S(2)}) async-start(bf16[16,64,1024]{2,1,0:T(8,128)(2,1)} %bitcast.66), calls=%async_computation.2 | async-start | bytes 4194304 | tf_op jit(solution)/shard_map/all_to_all | solution.py:43
  444.0 7.5 %copy-start.6 = (bf16[1024,2048]{1,0:T(8,128)(2,1)S(1)}, bf16[1024,2048]{1,0:T(8,128)(2,1)}, u32[]{:S(2)}) copy-start(bf16[1024,2048]{1,0:T(8,128)(2,1)} %all-gather.3.cloned.1.call-done) | copy-start | bytes 12582916
  444.0 7.5 %copy-start.11 = (bf16[1024,704]{0,1:T(8,128)(2,1)S(1)}, bf16[1024,704]{0,1:T(8,128)(2,1)}, u32[]{:S(2)}) copy-start(bf16[1024,704]{0,1:T(8,128)(2,1)} %copy-done.10) | copy-start | bytes 4325380
  451.6 4.5 copy-start.13
  498.0 18.3 %copy-start.1 = (bf16[1,704,2048]{2,1,0:T(8,128)(2,1)S(1)}, bf16[1,704,2048]{2,1,0:T(8,128)(2,1)}, u32[]{:S(2)}) copy-start(bf16[1,704,2048]{2,1,0:T(8,128)(2,1)} %param.13) | copy-start | bytes 8650756
Sparse Core Ops, SparseCore 0:
  90.4 55.5 all-gather.2
  158.9 55.5 all-gather.4
  232.7 99.2 reduce-scatter.4
  334.3 99.2 reduce-scatter.2
where the time goes:
time: 530 us; the launch traced here: 523 us
  waiting for transfers between devices  250 us (47%)
  blocking collectives  115 us (22%)
  matrix products  54.3 us (10%)
  local copies, waits for them, and re-layouts  43.7 us (8%)
  other arithmetic  32.8 us (6%)
  between operations  14.4 us (3%)
  starting transfers between devices  13 us (2%)
    reduce_scatter x2, waiting for transfers between devices, give_back(): lax.psum_scatter(partial_value, 'tensor', scatter_dimension=1, tiled=True)  184 us
    all_to_all x2, blocking collectives, dispatch(): lax.all_to_all(pack(rows, scaled), 'expert', split_axis=0, concat_axis=0,...  107 us
    all_gather x2, waiting for transfers between devices, dispatch(): return lax.all_gather(arrived, 'tensor', axis=1, tiled=True)  42.9 us
    scatter x1, local copies, waits for them, and re-layouts, pack(): jnp.zeros((slot_total, rows.shape[1]), jnp.bfloat16).at[slot_index]  24.7 us
    all_to_all x2, waiting for transfers between devices, give_back(): lax.all_to_all(shares, 'expert', split_axis=0, concat_axis=0, tiled=True)  22.8 us
    scatter x1, other arithmetic, pack(): jnp.zeros((slot_total, rows.shape[1]), jnp.bfloat16).at[slot_index]  15.4 us
    all_to_all x2, starting transfers between devices, give_back(): lax.all_to_all(shares, 'expert', split_axis=0, concat_axis=0, tiled=True)  12.6 us
  transfers between devices with their start and end apart: 6, of which 4 were waited for; matrix products, arithmetic and copies ran while one was open for 13% of the time, Pallas kernels for 0%

commit v1 on v0

--- a/solution.py
+++ b/solution.py
@@ -3,8 +3,11 @@
 from jax import lax
 from jax.sharding import PartitionSpec as P
 
-
-def body(tokens, grad_out, gates, expert_ids, w_gate, w_up, w_down):
+F32 = jnp.float32
+BF16 = jnp.bfloat16
+
+
+def slots_body(tokens, grad_out, gates, expert_ids, w_gate, w_up, w_down):
     expert_count = lax.axis_size("expert")
     tok_count = expert_ids.shape[0]
     top_count = expert_ids.shape[1]
@@ -82,6 +85,152 @@
     return (mixed, grad_tokens, grad_gates, grad_gate[None], grad_up[None], grad_down[None])
 
 
+def after(value, *others):
+    return lax.optimization_barrier((value, *others))[0]
+
+
+def gather_body(tokens, grad_out, gates, expert_ids, w_gate, w_up, w_down):
+    expert_count = lax.axis_size("expert")
+    tok_count, top_count = expert_ids.shape
+    capacity = tok_count * top_count * 4 // (3 * expert_count)
+    width = tokens.shape[1]
+    half = width // 2
+    column = expert_count // 4
+    me = lax.axis_index("expert")
+    side = lax.axis_index("tensor")
+
+    core_pairs = [(e, e ^ 1) for e in range(expert_count)]
+    chip_pairs = [(e, e ^ 2) for e in range(expert_count)]
+
+    def swap_core(value):
+        return lax.ppermute(value, "expert", core_pairs)
+
+    def swap_pair(value):
+        return lax.ppermute(value, "expert", chip_pairs)
+
+    def swap_side(value):
+        return lax.ppermute(value, "tensor", [(0, 1), (1, 0)])
+
+    def shift(value, step):
+        return lax.ppermute(
+            value, "expert", [(e, (e + 4 * step) % expert_count) for e in range(expert_count)]
+        )
+
+    rel_core, rel_pair, rel_step = jnp.meshgrid(
+        jnp.arange(2), jnp.arange(2), jnp.arange(column), indexing="ij"
+    )
+    block_of = (
+        ((me // 4 - rel_step) % column) * 4 + (((me // 2) % 2) ^ rel_pair) * 2 + ((me % 2) ^ rel_core)
+    ).reshape(-1)
+
+    routing = jnp.concatenate([expert_ids.astype(F32), gates], axis=1)
+    routing = lax.all_gather(routing, "expert")[block_of]
+    named = routing[:, :, :top_count] == me.astype(F32)
+    gate_of_token = jnp.sum(jnp.where(named, routing[:, :, top_count:], 0.0), axis=2)
+    member = jnp.any(named, axis=2).astype(jnp.int32)
+    position = jnp.where(member > 0, jnp.cumsum(member, axis=1) - 1, -1)
+    pick = position[:, None, :] == jnp.arange(capacity, dtype=jnp.int32)[None, :, None]
+    gate_row = jnp.sum(jnp.where(pick, gate_of_token[:, None, :], 0.0), axis=2).reshape(-1, 1)
+    pick_bf = pick.astype(BF16)
+
+    def spread(rows, start):
+        own = after(jnp.stack([rows[:, :half], rows[:, half:]]), *start)
+        parts = [own] + [shift(own, step) for step in range(1, column)]
+        a = jnp.stack([part[0] for part in parts])
+        b = jnp.stack([part[1] for part in parts])
+        a = jnp.stack([a, swap_side(a)], axis=1)
+        b = jnp.stack([b, swap_pair(b)])
+        a = jnp.stack([a, swap_pair(a)])
+        b = jnp.stack([b, swap_side(b)], axis=2)
+        return (a, swap_core(a)), (b, swap_core(b)), parts
+
+    def pick_rows(a, b):
+        halves = []
+        for piece in (a, b):
+            blocks = jnp.stack(piece).reshape(4 * column, 2, tok_count, half)
+            halves.append(
+                jnp.einsum("bst,bxth->bsxh", pick_bf, blocks, preferred_element_type=F32).astype(BF16)
+            )
+        rows = jnp.concatenate(halves, axis=3)
+        rows = jnp.where(side == 0, rows, rows[:, :, ::-1])
+        return rows.reshape(-1, 2 * width)
+
+    def put_back(values):
+        values = values.astype(BF16).reshape(4 * column, capacity, 2, width)
+        values = jnp.where(side == 0, values, values[:, :, ::-1])
+        blocks = jnp.einsum("bst,bsxh->bxth", pick_bf, values, preferred_element_type=F32)
+        return blocks.astype(BF16).reshape(2, 2, column, 2, tok_count, width)
+
+    def add(mine, theirs):
+        return (mine.astype(F32) + theirs.astype(F32)).astype(BF16)
+
+    def collect(blocks):
+        halves = blocks[..., :half], blocks[..., half:]
+        a, b = (add(piece[0], swap_core(piece[1])) for piece in halves)
+        a = add(a[0], swap_pair(a[1]))
+        b = add(b[:, :, 0], swap_side(b[:, :, 1]))
+        a = add(a[:, 0], swap_side(a[:, 1]))
+        b = add(b[0], swap_pair(b[1]))
+        both = jnp.stack([a, b], axis=1)
+        total = both[0].astype(F32)
+        for step in range(1, column):
+            total = total + shift(both[step], column - step).astype(F32)
+        return jnp.concatenate([total[0], total[1]], axis=1).astype(BF16)
+
+    weight_gate, weight_up, weight_down = w_gate[0], w_up[0], w_down[0]
+    contract_last = (((1,), (1,)), ((), ()))
+    contract_first = (((0,), (0,)), ((), ()))
+
+    token_a, token_b, token_parts = spread(tokens, ())
+    grad_a, grad_b, _ = spread(grad_out, token_parts)
+
+    full_rows = pick_rows(token_a, token_b)
+    gate_pre = jnp.dot(full_rows, weight_gate, preferred_element_type=F32)
+    up_pre = jnp.dot(full_rows, weight_up, preferred_element_type=F32)
+    sig = jax.nn.sigmoid(gate_pre)
+    act = gate_pre * sig * up_pre
+    scaled_act = (gate_row * act).astype(BF16)
+    mixed = collect(put_back(jnp.dot(scaled_act, weight_down, preferred_element_type=F32)))
+
+    grad_rows = pick_rows(grad_a, grad_b)
+    plain = lax.dot_general(grad_rows, weight_down, contract_last, preferred_element_type=F32)
+    gate_sums = jnp.sum(act * plain, axis=1)
+    grad_act = gate_row * plain
+    grad_gate_pre = (grad_act * up_pre * sig * (1.0 + gate_pre * (1.0 - sig))).astype(BF16)
+    grad_up_pre = (grad_act * gate_pre * sig).astype(BF16)
+    input_terms = lax.dot_general(
+        grad_gate_pre, weight_gate, contract_last, preferred_element_type=F32
+    ) + lax.dot_general(grad_up_pre, weight_up, contract_last, preferred_element_type=F32)
+    grad_tokens = collect(put_back(input_terms))
+
+    token_sums = jnp.sum(
+        jnp.where(pick, gate_sums.reshape(4 * column, capacity, 1), 0.0), axis=1
+    )
+    token_sums = token_sums + swap_side(token_sums)
+    token_sums = jnp.zeros_like(token_sums).at[block_of].set(token_sums)
+    expert_sums = lax.all_to_all(token_sums, "expert", split_axis=0, concat_axis=0, tiled=True)
+    chosen = expert_ids[None] == jnp.arange(expert_count, dtype=jnp.int32)[:, None, None]
+    grad_gates = jnp.sum(jnp.where(chosen, expert_sums[:, :, None], 0.0), axis=0)
+
+    def weight_grad(left, right):
+        return lax.dot_general(left, right, contract_first, preferred_element_type=F32).astype(BF16)[None]
+
+    grad_down = weight_grad(scaled_act, grad_rows)
+    grad_gate = weight_grad(full_rows, grad_gate_pre)
+    grad_up = weight_grad(full_rows, grad_up_pre)
+    return (mixed, grad_tokens, grad_gates, grad_gate, grad_up, grad_down)
+
+
+def body(tokens, grad_out, gates, expert_ids, w_gate, w_up, w_down):
+    expert_count = lax.axis_size("expert")
+    tok_count, top_count = expert_ids.shape
+    slot_total = tok_count * top_count * 4 // (3 * expert_count) * expert_count
+    gathers = expert_count * tok_count <= 2 * slot_total
+    shaped = lax.axis_size("tensor") == 2 and expert_count % 4 == 0
+    plan = gather_body if gathers and shaped else slots_body
+    return plan(tokens, grad_out, gates, expert_ids, w_gate, w_up, w_down)
+
+
 def solution(mesh):
     placed = (
         P("expert", "tensor"),

time: 530 us -> 444 us (0.84)
  the two profiles are of different devices: /device:TPU:18 before, /device:TPU:0 now
where the time goes in v1:
time: 444 us; the launch traced here: 439 us
  waiting for transfers between devices  142 us (32%)
  local copies, waits for them, and re-layouts  97.1 us (22%)
  matrix products  64.7 us (15%)
  other arithmetic  63.2 us (14%)
  starting transfers between devices  49.7 us (11%)
  blocking collectives  21 us (5%)
    ppermute x12, waiting for transfers between devices, shift(): lax.ppermute(value, 'expert', [(e, (e + 4 * step) % expert_count) for e i...  60.2 us
    ppermute x8, waiting for transfers between devices, swap_pair(): return lax.ppermute(value, 'expert', chip_pairs)  41.2 us
    ppermute x9, waiting for transfers between devices, swap_side(): return lax.ppermute(value, 'tensor', [(0, 1), (1, 0)])  40.6 us
    unnamed x71, local copies, waits for them, and re-layouts  39.9 us
    reshape x4, local copies, waits for them, and re-layouts, put_back(): values = values.astype(BF16).reshape(4 * column, capacity, 2, width)  25.5 us
    dot_general x3, matrix products, weight_grad(): lax.dot_general(left, right, contract_first, preferred_element_type=F32)  23.6 us
    ppermute x12, starting transfers between devices, shift(): lax.ppermute(value, 'expert', [(e, (e + 4 * step) % expert_count) for e i...  23.5 us
    all_gather x1, blocking collectives, gather_body(): routing = lax.all_gather(routing, 'expert')[block_of]  21 us
  transfers between devices with their start and end apart: 38, of which 16 were waited for; matrix products, arithmetic and copies ran while one was open for 29% of the time, Pallas kernels for 0%

profile of v1, /device:TPU:0, one launch (start us, length us, event | category | flops | bytes accessed | tf_op | source)
XLA Modules:
  0.0 439.5 jit_solution(14471695372177881075)
XLA Ops:
  1.9 5.1 %collective-permute-start.2 = (bf16[2,128,512]{2,1,0:T(8,128)(2,1)S(1)}, bf16[2,128,512]{2,1,0:T(8,128)(2,1)S(1)}, u32[]{:S(2)}, u32[]{:S(2)}) collective-permute-start(bf16[2,128,512]{2,1,0:T(8,128)(2,1)S(1)} %pad_maximum_fusion.20), channel_id=1, source_target_pairs={{0,24},{2,26},{4,28},{6,30},{8,0},{10,2},{12,4},{14,6},{16,8},{18,... | collective-permute-start | bytes 786440 | tf_op jit(solution)/shard_map/ppermute | solution.py:115
  8.0 5.7 %collective-permute-done.2 = bf16[2,128,512]{2,1,0:T(8,128)(2,1)S(1)} collective-permute-done((bf16[2,128,512]{2,1,0:T(8,128)(2,1)S(1)}, bf16[2,128,512]{2,1,0:T(8,128)(2,1)S(1)}, u32[]{:S(2)}, u32[]{:S(2)}) %collective-permute-start.2) | collective-permute-done | bytes 262176 | tf_op jit(solution)/shard_map/ppermute | solution.py:115
  14.4 14.9 %collective-permute-done.1 = bf16[2,128,512]{2,1,0:T(8,128)(2,1)S(1)} collective-permute-done((bf16[2,128,512]{2,1,0:T(8,128)(2,1)S(1)}, bf16[2,128,512]{2,1,0:T(8,128)(2,1)S(1)}, u32[]{:S(2)}, u32[]{:S(2)}) %collective-permute-start.1) | collective-permute-done | bytes 262176 | tf_op jit(solution)/shard_map/ppermute | solution.py:115
  38.5 6.1 %collective-permute-done.3 = bf16[4,128,512]{2,1,0:T(8,128)(2,1)} collective-permute-done((bf16[4,128,512]{2,1,0:T(8,128)(2,1)}, bf16[4,128,512]{2,1,0:T(8,128)(2,1)}, u32[]{:S(2)}, u32[]{:S(2)}) %collective-permute-start.3) | collective-permute-done | bytes 524320 | tf_op jit(solution)/shard_map/ppermute | solution.py:112
  52.6 13.0 %collective-permute-done.19 = bf16[2,128,512]{2,1,0:T(8,128)(2,1)S(1)} collective-permute-done((bf16[2,128,512]{2,1,0:T(8,128)(2,1)S(1)}, bf16[2,128,512]{2,1,0:T(8,128)(2,1)S(1)}, u32[]{:S(2)}, u32[]{:S(2)}) %collective-permute-start.19) | collective-permute-done | bytes 262176 | tf_op jit(solution)/shard_map/ppermute | solution.py:115
  80.3 21.0 %all-gather = f32[2048,12]{0,1:T(8,128)S(1)} all-gather(f32[128,12]{0,1:T(8,128)S(1)} %pad_maximum_fusion.24), channel_id=2, replica_groups=mesh['expert'=16,'tensor'=2] {'expert'}, dimensions={0}, use_global_device_ids=true | all-gather | bytes 104448 | tf_op jit(solution)/shard_map/all_gather | solution.py:127
  109.7 20.7 %collective-permute-done.22 = bf16[4,2,128,512]{3,2,0,1:T(8,128)(2,1)} collective-permute-done((bf16[4,2,128,512]{3,2,0,1:T(8,128)(2,1)}, bf16[4,2,128,512]{3,2,0,1:T(8,128)(2,1)}, u32[]{:S(2)}, u32[]{:S(2)}) %collective-permute-start.22) | collective-permute-done | bytes 1048608 | tf_op jit(solution)/shard_map/ppermute | solution.py:109
  130.4 3.2 fusion.80
  133.6 3.6 fusion.79
  145.7 3.4 reverse_select_fusion.3
  149.1 8.5 %copy.65 = bf16[16,64,2,1024]{3,2,1,0:T(2,128)(2,1)} copy(bf16[16,64,2,1024]{3,1,2,0:T(8,128)(2,1)} %reverse_select_fusion.3) | data formatting | bytes 8388608 | tf_op jit(solution)/shard_map/jit(_where)/select_n | solution.py:155
  157.6 4.0 copy.91
  161.6 4.8 %fusion.11 = f32[1024,704]{0,1:T(8,128)} fusion(bf16[1024,2048]{1,0:T(8,128)(2,1)S(1)} %bitcast.238, bf16[1,2048,704]{1,2,0:T(8,128)(2,1)S(1)} %copy-done.28), kind=kOutput, calls=%fused_computation.34 | convolution fusion | flops 2952790016 | bytes 9961472 | tf_op jit(solution)/shard_map/dot_general | solution.py:189
  166.4 4.8 %fusion.15 = f32[1024,704]{0,1:T(8,128)} fusion(bf16[1024,2048]{1,0:T(8,128)(2,1)S(1)} %bitcast.239, bf16[1,2048,704]{1,2,0:T(8,128)(2,1)S(1)} %copy-done.26), kind=kOutput, calls=%fused_computation.38 | convolution fusion | flops 2952790016 | bytes 9961472 | tf_op jit(solution)/shard_map/dot_general | solution.py:188
  178.8 3.4 reverse_select_fusion.1
  182.2 9.0 %copy.74 = bf16[16,64,2,1024]{3,2,1,0:T(2,128)(2,1)} copy(bf16[16,64,2,1024]{3,1,2,0:T(8,128)(2,1)} %reverse_select_fusion.1) | data formatting | bytes 8388608 | tf_op jit(solution)/shard_map/jit(_where)/select_n | solution.py:155
  191.3 3.8 copy.92
  195.2 5.1 %multiply_reduce_fusion = (f32[1024]{0:T(1024)S(1)}, f32[1024,704]{0,1:T(8,128)}) fusion(f32[1024,704]{0,1:T(8,128)S(1)} %copy-done.13, f32[1024,704]{0,1:T(8,128)S(1)} %copy-done.15, bf16[1024,2048]{1,0:T(8,128)(2,1)S(1)} %bitcast.242, bf16[1,704,2048]{2,1,0:T(8,128)(2,1)S(1)} %copy-done), kind=kOutput, calls=%fused_computation.40 | convolution fusion | flops 2957835264 | bytes 15732736 | tf_op jit(solution)/shard_map/dot_general | solution.py:196
  200.9 8.9 %fusion.4 = bf16[1,704,2048]{2,1,0:T(8,128)(2,1)} fusion(bf16[1024,2048]{1,0:T(8,128)(2,1)} %bitcast.243, f32[1024]{0:T(1024)S(1)} %mul.72, f32[1024,704]{0,1:T(8,128)} %fusion.11, f32[1024,704]{0,1:T(8,128)} %fusion.15), kind=kOutput, calls=%fused_computation.27 | convolution fusion | flops 2959278080 | bytes 12849152 | tf_op jit(solution)/shard_map/dot_general | solution.py:216
  209.8 5.5 %convolution_convert_fusion.2 = bf16[1024,2048]{1,0:T(8,128)(2,1)} fusion(bf16[1,704,2048]{2,1,0:T(8,128)(2,1)S(1)} %copy-done, f32[1024]{0:T(1024)S(1)} %mul.72, f32[1024,704]{0,1:T(8,128)S(1)} %copy-done.14, f32[1024,704]{0,1:T(8,128)S(1)} %copy-done.16), kind=kOutput, calls=%fused_computation.23 | convolution fusion | flops 2959933440 | bytes 12849152 | tf_op jit(solution)/shard_map/dot_general | solution.py:193
  216.8 8.2 %reshape.190 = bf16[16,64,2,1024]{3,2,1,0:T(2,128)(2,1)} reshape(bf16[1024,2048]{1,0:T(8,128)(2,1)} %convolution_convert_fusion.2) | data formatting | bytes 8388608 | tf_op jit(solution)/shard_map/reshape | solution.py:159
  225.0 5.8 %copy.67 = bf16[16,64,2,1024]{3,1,2,0:T(8,128)(2,1)} copy(bf16[16,64,2,1024]{3,2,1,0:T(2,128)(2,1)} %reshape.190) | data formatting | bytes 8388608 | tf_op jit(solution)/shard_map/reshape | solution.py:159
  230.8 3.5 fusion.13
  234.3 5.2 %add_convert_fusion = bf16[1024,2048]{1,0:T(8,128)(2,1)} fusion(f32[1024,2048]{1,0:T(8,128)S(1)} %fusion.13, bf16[1024,704]{0,1:T(8,128)(2,1)S(1)} %get-tuple-element.20, bf16[1,2048,704]{1,2,0:T(8,128)(2,1)S(1)} %copy-done.29), kind=kOutput, calls=%fused_computation.2 | convolution fusion | flops 2956984320 | bytes 16908288 | tf_op jit(solution)/shard_map/dot_general | solution.py:203
  239.6 7.8 %reshape.195 = bf16[16,64,2,1024]{3,2,1,0:T(2,128)(2,1)} reshape(bf16[1024,2048]{1,0:T(8,128)(2,1)} %add_convert_fusion) | data formatting | bytes 8388608 | tf_op jit(solution)/shard_map/reshape | solution.py:159
  247.4 3.7 copy.76
  251.1 5.0 %reverse_select_fusion = (bf16[16,64,2,1024]{3,1,2,0:T(8,128)(2,1)}, bf16[16,64,2,1024]{3,1,2,0:T(8,128)(2,1)}) fusion(bf16[16,64,2,1024]{3,1,2,0:T(8,128)(2,1)S(1)} %copy.76, pred[]{:T(512)S(6)} %eq.23, bf16[16,64,2,1024]{3,1,2,0:T(8,128)(2,1)S(1)} %copy-done.2), kind=kLoop, calls=%fused_computation.5 | loop fusion | flops 4194304 | bytes 16777216 | tf_op jit(solution)/shard_map/jit(_where)/select_n | solution.py:160
  256.2 4.7 %convolution_convert_fusion = bf16[16,2,1024,128]{3,2,1,0:T(8,128)(2,1)S(1)} fusion(bf16[16,64,2,1024]{3,1,2,0:T(8,128)(2,1)} %get-tuple-element.78, s32[16,128]{1,0:T(8,128)S(1)} %add_select_fusion), kind=kOutput, calls=%fused_computation.3 | convolution fusion | flops 541196288 | bytes 12591104 | tf_op jit(solution)/shard_map/bst,bsxh->bxth/dot_general | solution.py:161
  263.6 4.2 copy.89
  267.8 7.4 %fusion.6 = bf16[1,2048,704]{1,2,0:T(8,128)(2,1)} fusion(bf16[1024,704]{0,1:T(8,128)(2,1)} %copy-done.20, bf16[1024,2048]{1,0:T(8,128)(2,1)} %bitcast.240), kind=kOutput, calls=%fused_computation.29 | convolution fusion | flops 2954231808 | bytes 8519680 | tf_op jit(solution)/shard_map/dot_general | solution.py:216
  276.2 4.1 copy.87
  280.6 4.7 %convolution_convert_fusion.1 = bf16[16,2,1024,128]{3,2,1,0:T(8,128)(2,1)S(1)} fusion(bf16[16,64,2,1024]{3,1,2,0:T(8,128)(2,1)} %get-tuple-element.79, s32[16,128]{1,0:T(8,128)S(1)} %add_select_fusion), kind=kOutput, calls=%fused_computation.4 | convolution fusion | flops 541196288 | bytes 12591104 | tf_op jit(solution)/shard_map/bst,bsxh->bxth/dot_general | solution.py:161
  285.3 3.4 fusion.84
  288.7 4.2 copy.83
  292.9 4.2 copy.85
  298.7 3.7 all-to-all-start
  302.5 7.4 %fusion.5 = bf16[1,2048,704]{1,2,0:T(8,128)(2,1)} fusion(bf16[1024,704]{0,1:T(8,128)(2,1)} %copy-done.19, bf16[1024,2048]{1,0:T(8,128)(2,1)} %bitcast.241), kind=kOutput, calls=%fused_computation.28 | convolution fusion | flops 2954231808 | bytes 8519680 | tf_op jit(solution)/shard_map/dot_general | solution.py:216
  309.8 4.1 copy.86
  316.4 4.3 copy.82
  338.3 14.6 %collective-permute-done.31 = bf16[2,4,128,512]{3,2,1,0:T(8,128)(2,1)S(1)} collective-permute-done((bf16[2,4,128,512]{3,2,1,0:T(8,128)(2,1)S(1)}, bf16[2,4,128,512]{3,2,1,0:T(8,128)(2,1)S(1)}, u32[]{:S(2)}, u32[]{:S(2)}) %collective-permute-start.31) | collective-permute-done | bytes 1048608 | tf_op jit(solution)/shard_map/ppermute | solution.py:112
  357.8 17.6 %collective-permute-done.13 = bf16[2,4,128,512]{3,2,1,0:T(8,128)(2,1)S(1)} collective-permute-done((bf16[2,4,128,512]{3,2,1,0:T(8,128)(2,1)S(1)}, bf16[2,4,128,512]{3,2,1,0:T(8,128)(2,1)S(1)}, u32[]{:S(2)}, u32[]{:S(2)}) %collective-permute-start.13) | collective-permute-done | bytes 1048608 | tf_op jit(solution)/shard_map/ppermute | solution.py:112
  380.3 9.7 %collective-permute-done.32 = bf16[4,128,512]{2,1,0:T(8,128)(2,1)S(1)} collective-permute-done((bf16[4,128,512]{2,1,0:T(8,128)(2,1)S(1)}, bf16[4,128,512]{2,1,0:T(8,128)(2,1)S(1)}, u32[]{:S(2)}, u32[]{:S(2)}) %collective-permute-start.32) | collective-permute-done | bytes 524320 | tf_op jit(solution)/shard_map/ppermute | solution.py:109
  390.4 3.9 collective-permute-start.33
  395.4 5.1 %collective-permute-done.14 = bf16[4,128,512]{2,1,0:T(8,128)(2,1)S(1)} collective-permute-done((bf16[4,128,512]{2,1,0:T(8,128)(2,1)S(1)}, bf16[4,128,512]{2,1,0:T(8,128)(2,1)S(1)}, u32[]{:S(2)}, u32[]{:S(2)}) %collective-permute-start.14) | collective-permute-done | bytes 524320 | tf_op jit(solution)/shard_map/ppermute | solution.py:109
  400.9 3.5 collective-permute-start.15
  404.5 6.3 %collective-permute-start.16 = (bf16[2,128,512]{2,1,0:T(8,128)(2,1)S(1)}, bf16[2,128,512]{2,1,0:T(8,128)(2,1)S(1)}, u32[]{:S(2)}, u32[]{:S(2)}) collective-permute-start(bf16[2,128,512]{2,1,0:T(8,128)(2,1)S(1)} %get-tuple-element.35), channel_id=1, source_target_pairs={{0,16},{2,18},{4,20},{6,22},{8,24},{10,26},{12,28},{14,30},{16,0},... | collective-permute-start | bytes 786440 | tf_op jit(solution)/shard_map/ppermute | solution.py:115
  410.7 18.5 %collective-permute-done.34 = bf16[2,128,512]{2,1,0:T(8,128)(2,1)S(1)} collective-permute-done((bf16[2,128,512]{2,1,0:T(8,128)(2,1)S(1)}, bf16[2,128,512]{2,1,0:T(8,128)(2,1)S(1)}, u32[]{:S(2)}, u32[]{:S(2)}) %collective-permute-start.34) | collective-permute-done | bytes 262176 | tf_op jit(solution)/shard_map/ppermute | solution.py:115
  429.4 8.2 %collective-permute-done.16 = bf16[2,128,512]{2,1,0:T(8,128)(2,1)S(1)} collective-permute-done((bf16[2,128,512]{2,1,0:T(8,128)(2,1)S(1)}, bf16[2,128,512]{2,1,0:T(8,128)(2,1)S(1)}, u32[]{:S(2)}, u32[]{:S(2)}) %collective-permute-start.16) | collective-permute-done | bytes 262176 | tf_op jit(solution)/shard_map/ppermute | solution.py:115
  (215 shorter events, 100.3 us)
Async XLA Ops:
  0.6 194.4 %copy-start = (bf16[1,704,2048]{2,1,0:T(8,128)(2,1)S(1)}, bf16[1,704,2048]{2,1,0:T(8,128)(2,1)}, u32[]{:S(2)}) copy-start(bf16[1,704,2048]{2,1,0:T(8,128)(2,1)} %param.13) | copy-start | bytes 8650756
  0.6 32.3 %copy-start.22 = (bf16[128,1024]{1,0:T(8,128)(2,1)S(1)}, bf16[128,1024]{1,0:T(8,128)(2,1)}, u32[]{:S(2)}) copy-start(bf16[128,1024]{1,0:T(8,128)(2,1)} %param.8) | copy-start | bytes 786436
  0.7 33.0 %copy-start.23 = (s32[128,6]{0,1:T(8,128)S(1)}, s32[128,6]{0,1:T(8,128)}, u32[]{:S(2)}) copy-start(s32[128,6]{0,1:T(8,128)} %param.10) | copy-start | bytes 9220
  0.7 33.0 %copy-start.25 = (f32[128,6]{0,1:T(8,128)S(1)}, f32[128,6]{0,1:T(8,128)}, u32[]{:S(2)}) copy-start(f32[128,6]{0,1:T(8,128)} %param.9) | copy-start | bytes 9220
  1.9 11.9 %collective-permute-start.2 = (bf16[2,128,512]{2,1,0:T(8,128)(2,1)S(1)}, bf16[2,128,512]{2,1,0:T(8,128)(2,1)S(1)}, u32[]{:S(2)}, u32[]{:S(2)}) collective-permute-start(bf16[2,128,512]{2,1,0:T(8,128)(2,1)S(1)} %pad_maximum_fusion.20), channel_id=1, source_target_pairs={{0,24},{2,26},{4,28},{6,30},{8,0},{10,2},{12,4},{14,6},{16,8},{18,... | collective-permute-start | bytes 786440 | tf_op jit(solution)/shard_map/ppermute | solution.py:115
  7.0 22.3 %collective-permute-start.1 = (bf16[2,128,512]{2,1,0:T(8,128)(2,1)S(1)}, bf16[2,128,512]{2,1,0:T(8,128)(2,1)S(1)}, u32[]{:S(2)}, u32[]{:S(2)}) collective-permute-start(bf16[2,128,512]{2,1,0:T(8,128)(2,1)S(1)} %pad_maximum_fusion.20), channel_id=1, source_target_pairs={{0,16},{2,18},{4,20},{6,22},{8,24},{10,26},{12,28},{14,30},{16,0},... | collective-permute-start | bytes 786440 | tf_op jit(solution)/shard_map/ppermute | solution.py:115
  7.0 23.0 %collective-permute-start = (bf16[2,128,512]{2,1,0:T(8,128)(2,1)S(1)}, bf16[2,128,512]{2,1,0:T(8,128)(2,1)S(1)}, u32[]{:S(2)}, u32[]{:S(2)}) collective-permute-start(bf16[2,128,512]{2,1,0:T(8,128)(2,1)S(1)} %pad_maximum_fusion.20), channel_id=1, source_target_pairs={{0,8},{2,10},{4,12},{6,14},{8,16},{10,18},{12,20},{14,22},{16,24},... | collective-permute-start | bytes 786440 | tf_op jit(solution)/shard_map/ppermute | solution.py:115
  31.5 13.1 %collective-permute-start.3 = (bf16[4,128,512]{2,1,0:T(8,128)(2,1)}, bf16[4,128,512]{2,1,0:T(8,128)(2,1)}, u32[]{:S(2)}, u32[]{:S(2)}) collective-permute-start(bf16[4,128,512]{2,1,0:T(8,128)(2,1)} %get-tuple-element.45), channel_id=1, source_target_pairs={{0,1},{1,0},{2,3},{3,2},{4,5},{5,4},{6,7},{7,6},{8,9},{9,8},{10,11... | collective-permute-start | bytes 1572872 | tf_op jit(solution)/shard_map/ppermute | solution.py:112
  35.8 14.8 %collective-permute-start.6 = (bf16[4,128,512]{2,1,0:T(8,128)(2,1)}, bf16[4,128,512]{2,1,0:T(8,128)(2,1)}, u32[]{:S(2)}, u32[]{:S(2)}) collective-permute-start(bf16[4,128,512]{2,1,0:T(8,128)(2,1)} %get-tuple-element.47), channel_id=1, source_target_pairs={{0,4},{2,6},{4,0},{6,2},{8,12},{10,14},{12,8},{14,10},{16,20},{18,... | collective-permute-start | bytes 1572872 | tf_op jit(solution)/shard_map/ppermute | solution.py:109
  37.3 13.3 %copy-start.18 = (bf16[1,4,128,512]{3,2,1,0:T(8,128)(2,1)S(1)}, bf16[1,4,128,512]{3,2,1,0:T(8,128)(2,1)}, u32[]{:S(2)}) copy-start(bf16[1,4,128,512]{3,2,1,0:T(8,128)(2,1)} %get-tuple-element.46) | copy-start | bytes 1572868
  38.4 14.2 %collective-permute-start.20 = (bf16[2,128,512]{2,1,0:T(8,128)(2,1)S(1)}, bf16[2,128,512]{2,1,0:T(8,128)(2,1)S(1)}, u32[]{:S(2)}, u32[]{:S(2)}) collective-permute-start(bf16[2,128,512]{2,1,0:T(8,128)(2,1)S(1)} %pad_maximum_fusion.22), channel_id=1, source_target_pairs={{0,24},{2,26},{4,28},{6,30},{8,0},{10,2},{12,4},{14,6},{16,8},{18,... | collective-permute-start | bytes 786440 | tf_op jit(solution)/shard_map/ppermute | solution.py:115
  45.8 25.2 %collective-permute-start.4 = (bf16[4,2,128,512]{3,2,0,1:T(8,128)(2,1)S(1)}, bf16[4,2,128,512]{3,2,0,1:T(8,128)(2,1)S(1)}, u32[]{:S(2)}, u32[]{:S(2)}) collective-permute-start(bf16[4,2,128,512]{3,2,0,1:T(8,128)(2,1)S(1)} %get-tuple-element.37), channel_id=1, source_target_pairs={{0,4},{2,6},{4,0},{6,2},{8,12},{10,14},{12,8},{14,10},{16,20},{18,... | collective-permute-start | bytes 3145736 | tf_op jit(solution)/shard_map/ppermute | solution.py:109
  47.4 18.2 %collective-permute-start.19 = (bf16[2,128,512]{2,1,0:T(8,128)(2,1)S(1)}, bf16[2,128,512]{2,1,0:T(8,128)(2,1)S(1)}, u32[]{:S(2)}, u32[]{:S(2)}) collective-permute-start(bf16[2,128,512]{2,1,0:T(8,128)(2,1)S(1)} %pad_maximum_fusion.22), channel_id=1, source_target_pairs={{0,16},{2,18},{4,20},{6,22},{8,24},{10,26},{12,28},{14,30},{16,0},... | collective-permute-start | bytes 786440 | tf_op jit(solution)/shard_map/ppermute | solution.py:115
  49.8 15.8 %collective-permute-start.18 = (bf16[2,128,512]{2,1,0:T(8,128)(2,1)S(1)}, bf16[2,128,512]{2,1,0:T(8,128)(2,1)S(1)}, u32[]{:S(2)}, u32[]{:S(2)}) collective-permute-start(bf16[2,128,512]{2,1,0:T(8,128)(2,1)S(1)} %pad_maximum_fusion.22), channel_id=1, source_target_pairs={{0,8},{2,10},{4,12},{6,14},{8,16},{10,18},{12,20},{14,22},{16,24},... | collective-permute-start | bytes 786440 | tf_op jit(solution)/shard_map/ppermute | solution.py:115
  51.8 26.2 %collective-permute-start.7 = (bf16[2,4,128,512]{3,2,1,0:T(8,128)(2,1)S(1)}, bf16[2,4,128,512]{3,2,1,0:T(8,128)(2,1)S(1)}, u32[]{:S(2)}, u32[]{:S(2)}) collective-permute-start(bf16[2,4,128,512]{3,2,1,0:T(8,128)(2,1)S(1)} %get-tuple-element.39), channel_id=1, source_target_pairs={{0,1},{1,0},{2,3},{3,2},{4,5},{5,4},{6,7},{7,6},{8,9},{9,8},{10,11... | collective-permute-start | bytes 3145736 | tf_op jit(solution)/shard_map/ppermute | solution.py:112
  66.7 35.2 %collective-permute-start.21 = (bf16[4,128,512]{2,1,0:T(8,128)(2,1)}, bf16[4,128,512]{2,1,0:T(8,128)(2,1)}, u32[]{:S(2)}, u32[]{:S(2)}) collective-permute-start(bf16[4,128,512]{2,1,0:T(8,128)(2,1)} %get-tuple-element.49), channel_id=1, source_target_pairs={{0,1},{1,0},{2,3},{3,2},{4,5},{5,4},{6,7},{7,6},{8,9},{9,8},{10,11... | collective-permute-start | bytes 1572872 | tf_op jit(solution)/shard_map/ppermute | solution.py:112
  73.3 64.4 %collective-permute-start.5 = (bf16[2,4,2,128,512]{4,3,1,2,0:T(8,128)(2,1)}, bf16[2,4,2,128,512]{4,3,1,2,0:T(8,128)(2,1)}, u32[]{:S(2)}, u32[]{:S(2)}) collective-permute-start(bf16[2,4,2,128,512]{4,3,1,2,0:T(8,128)(2,1)} %get-tuple-element.23), channel_id=1, source_target_pairs={{0,2},{2,0},{4,6},{6,4},{8,10},{10,8},{12,14},{14,12},{16,18},{18,... | collective-permute-start | bytes 6291464 | tf_op jit(solution)/shard_map/ppermute | solution.py:106
  74.2 31.1 %collective-permute-start.24 = (bf16[4,128,512]{2,1,0:T(8,128)(2,1)}, bf16[4,128,512]{2,1,0:T(8,128)(2,1)}, u32[]{:S(2)}, u32[]{:S(2)}) collective-permute-start(bf16[4,128,512]{2,1,0:T(8,128)(2,1)} %get-tuple-element.51), channel_id=1, source_target_pairs={{0,4},{2,6},{4,0},{6,2},{8,12},{10,14},{12,8},{14,10},{16,20},{18,... | collective-permute-start | bytes 1572872 | tf_op jit(solution)/shard_map/ppermute | solution.py:109
  80.3 59.9 %collective-permute-start.8 = (bf16[2,4,2,128,512]{4,3,1,0,2:T(8,128)(2,1)}, bf16[2,4,2,128,512]{4,3,1,0,2:T(8,128)(2,1)}, u32[]{:S(2)}, u32[]{:S(2)}) collective-permute-start(bf16[2,4,2,128,512]{4,3,1,0,2:T(8,128)(2,1)} %get-tuple-element.25), channel_id=1, source_target_pairs={{0,2},{2,0},{4,6},{6,4},{8,10},{10,8},{12,14},{14,12},{16,18},{18,... | collective-permute-start | bytes 6291464 | tf_op jit(solution)/shard_map/ppermute | solution.py:106
  104.7 25.7 %collective-permute-start.22 = (bf16[4,2,128,512]{3,2,0,1:T(8,128)(2,1)}, bf16[4,2,128,512]{3,2,0,1:T(8,128)(2,1)}, u32[]{:S(2)}, u32[]{:S(2)}) collective-permute-start(bf16[4,2,128,512]{3,2,0,1:T(8,128)(2,1)} %get-tuple-element.41), channel_id=1, source_target_pairs={{0,4},{2,6},{4,0},{6,2},{8,12},{10,14},{12,8},{14,10},{16,20},{18,... | collective-permute-start | bytes 3145736 | tf_op jit(solution)/shard_map/ppermute | solution.py:109
  107.8 25.9 %collective-permute-start.25 = (bf16[2,4,128,512]{3,2,1,0:T(8,128)(2,1)}, bf16[2,4,128,512]{3,2,1,0:T(8,128)(2,1)}, u32[]{:S(2)}, u32[]{:S(2)}) collective-permute-start(bf16[2,4,128,512]{3,2,1,0:T(8,128)(2,1)} %get-tuple-element.43), channel_id=1, source_target_pairs={{0,1},{1,0},{2,3},{3,2},{4,5},{5,4},{6,7},{7,6},{8,9},{9,8},{10,11... | collective-permute-start | bytes 3145736 | tf_op jit(solution)/shard_map/ppermute | solution.py:112
  133.6 37.5 %collective-permute-start.23 = (bf16[2,4,2,128,512]{4,3,1,2,0:T(8,128)(2,1)}, bf16[2,4,2,128,512]{4,3,1,2,0:T(8,128)(2,1)}, u32[]{:S(2)}, u32[]{:S(2)}) collective-permute-start(bf16[2,4,2,128,512]{4,3,1,2,0:T(8,128)(2,1)} %get-tuple-element.27), channel_id=1, source_target_pairs={{0,2},{2,0},{4,6},{6,4},{8,10},{10,8},{12,14},{14,12},{16,18},{18,... | collective-permute-start | bytes 6291464 | tf_op jit(solution)/shard_map/ppermute | solution.py:106
  137.2 37.1 %collective-permute-start.26 = (bf16[2,4,2,128,512]{4,3,1,0,2:T(8,128)(2,1)}, bf16[2,4,2,128,512]{4,3,1,0,2:T(8,128)(2,1)}, u32[]{:S(2)}, u32[]{:S(2)}) collective-permute-start(bf16[2,4,2,128,512]{4,3,1,0,2:T(8,128)(2,1)} %get-tuple-element.29), channel_id=1, source_target_pairs={{0,2},{2,0},{4,6},{6,4},{8,10},{10,8},{12,14},{14,12},{16,18},{18,... | collective-permute-start | bytes 6291464 | tf_op jit(solution)/shard_map/ppermute | solution.py:106
  200.9 8.9 %copy-start.14 = (f32[1024,704]{0,1:T(8,128)S(1)}, f32[1024,704]{0,1:T(8,128)}, u32[]{:S(2)}) copy-start(f32[1024,704]{0,1:T(8,128)} %fusion.11) | copy-start | bytes 8650756
  200.9 8.9 %copy-start.16 = (f32[1024,704]{0,1:T(8,128)S(1)}, f32[1024,704]{0,1:T(8,128)}, u32[]{:S(2)}) copy-start(f32[1024,704]{0,1:T(8,128)} %fusion.15) | copy-start | bytes 8650756
  216.8 14.0 %copy-start.19 = (bf16[1024,704]{0,1:T(8,128)(2,1)}, bf16[1024,704]{0,1:T(8,128)(2,1)S(1)}, u32[]{:S(2)}) copy-start(bf16[1024,704]{0,1:T(8,128)(2,1)S(1)} %get-tuple-element.21) | copy-start | bytes 4325380
  216.8 17.5 %copy-start.20 = (bf16[1024,704]{0,1:T(8,128)(2,1)}, bf16[1024,704]{0,1:T(8,128)(2,1)S(1)}, u32[]{:S(2)}) copy-start(bf16[1024,704]{0,1:T(8,128)(2,1)S(1)} %get-tuple-element.20) | copy-start | bytes 4325380
  267.8 55.9 %collective-permute-start.30 = (bf16[2,4,2,128,512]{4,3,1,0,2:T(8,128)(2,1)}, bf16[2,4,2,128,512]{4,3,1,0,2:T(8,128)(2,1)}, u32[]{:S(2)}, u32[]{:S(2)}) collective-permute-start(bf16[2,4,2,128,512]{4,3,1,0,2:T(8,128)(2,1)} %bitcast.245), channel_id=1, source_target_pairs={{0,2},{2,0},{4,6},{6,4},{8,10},{10,8},{12,14},{14,12},{16,18},{18,... | collective-permute-start | bytes 6291464 | tf_op jit(solution)/shard_map/ppermute | solution.py:106
  275.2 22.4 %collective-permute-start.36 = (f32[16,128]{1,0:T(8,128)S(1)}, f32[16,128]{1,0:T(8,128)S(1)}, u32[]{:S(2)}, u32[]{:S(2)}) collective-permute-start(f32[16,128]{1,0:T(8,128)S(1)} %get-tuple-element.8), channel_id=1, source_target_pairs={{0,1},{1,0},{2,3},{3,2},{4,5},{5,4},{6,7},{7,6},{8,9},{9,8},{10,11... | collective-permute-start | bytes 24584 | tf_op jit(solution)/shard_map/ppermute | solution.py:112
  280.4 47.5 %collective-permute-start.27 = (bf16[2,4,2,128,512]{4,3,1,2,0:T(8,128)(2,1)}, bf16[2,4,2,128,512]{4,3,1,2,0:T(8,128)(2,1)}, u32[]{:S(2)}, u32[]{:S(2)}) collective-permute-start(bf16[2,4,2,128,512]{4,3,1,2,0:T(8,128)(2,1)} %bitcast.246), channel_id=1, source_target_pairs={{0,2},{2,0},{4,6},{6,4},{8,10},{10,8},{12,14},{14,12},{16,18},{18,... | collective-permute-start | bytes 6291464 | tf_op jit(solution)/shard_map/ppermute | solution.py:106
  297.0 35.3 %collective-permute-start.12 = (bf16[2,4,2,128,512]{4,3,1,0,2:T(8,128)(2,1)}, bf16[2,4,2,128,512]{4,3,1,0,2:T(8,128)(2,1)}, u32[]{:S(2)}, u32[]{:S(2)}) collective-permute-start(bf16[2,4,2,128,512]{4,3,1,0,2:T(8,128)(2,1)} %bitcast.247), channel_id=1, source_target_pairs={{0,2},{2,0},{4,6},{6,4},{8,10},{10,8},{12,14},{14,12},{16,18},{18,... | collective-permute-start | bytes 6291464 | tf_op jit(solution)/shard_map/ppermute | solution.py:106
  297.3 38.3 %collective-permute-start.9 = (bf16[2,4,2,128,512]{4,3,1,2,0:T(8,128)(2,1)}, bf16[2,4,2,128,512]{4,3,1,2,0:T(8,128)(2,1)}, u32[]{:S(2)}, u32[]{:S(2)}) collective-permute-start(bf16[2,4,2,128,512]{4,3,1,2,0:T(8,128)(2,1)} %bitcast.244), channel_id=1, source_target_pairs={{0,2},{2,0},{4,6},{6,4},{8,10},{10,8},{12,14},{14,12},{16,18},{18,... | collective-permute-start | bytes 6291464 | tf_op jit(solution)/shard_map/ppermute | solution.py:106
  298.7 24.3 %all-to-all-start = ((f32[16,1,128]{2,1,0:T(1,128)}), f32[16,1,128]{2,1,0:T(1,128)S(1)}, u32[]{:S(2)}, u32[]{:S(2)}) async-start(f32[16,1,128]{2,1,0:T(1,128)} %bitcast.85), calls=%async_computation | async-start | bytes 16384 | tf_op jit(solution)/shard_map/all_to_all | solution.py:211
  326.9 26.1 %collective-permute-start.31 = (bf16[2,4,128,512]{3,2,1,0:T(8,128)(2,1)S(1)}, bf16[2,4,128,512]{3,2,1,0:T(8,128)(2,1)S(1)}, u32[]{:S(2)}, u32[]{:S(2)}) collective-permute-start(bf16[2,4,128,512]{3,2,1,0:T(8,128)(2,1)S(1)} %slice_bitcast_fusion), channel_id=1, source_target_pairs={{0,1},{1,0},{2,3},{3,2},{4,5},{5,4},{6,7},{7,6},{8,9},{9,8},{10,11... | collective-permute-start | bytes 3145736 | tf_op jit(solution)/shard_map/ppermute | solution.py:112
  330.3 26.1 %collective-permute-start.28 = (bf16[4,2,128,512]{3,2,0,1:T(8,128)(2,1)S(1)}, bf16[4,2,128,512]{3,2,0,1:T(8,128)(2,1)S(1)}, u32[]{:S(2)}, u32[]{:S(2)}) collective-permute-start(bf16[4,2,128,512]{3,2,0,1:T(8,128)(2,1)S(1)} %slice_bitcast_fusion.2), channel_id=1, source_target_pairs={{0,4},{2,6},{4,0},{6,2},{8,12},{10,14},{12,8},{14,10},{16,20},{18,... | collective-permute-start | bytes 3145736 | tf_op jit(solution)/shard_map/ppermute | solution.py:109
  334.7 40.7 %collective-permute-start.13 = (bf16[2,4,128,512]{3,2,1,0:T(8,128)(2,1)S(1)}, bf16[2,4,128,512]{3,2,1,0:T(8,128)(2,1)S(1)}, u32[]{:S(2)}, u32[]{:S(2)}) collective-permute-start(bf16[2,4,128,512]{3,2,1,0:T(8,128)(2,1)S(1)} %slice_bitcast_fusion.4), channel_id=1, source_target_pairs={{0,1},{1,0},{2,3},{3,2},{4,5},{5,4},{6,7},{7,6},{8,9},{9,8},{10,11... | collective-permute-start | bytes 3145736 | tf_op jit(solution)/shard_map/ppermute | solution.py:112
  338.0 40.8 %collective-permute-start.10 = (bf16[4,2,128,512]{3,2,0,1:T(8,128)(2,1)S(1)}, bf16[4,2,128,512]{3,2,0,1:T(8,128)(2,1)S(1)}, u32[]{:S(2)}, u32[]{:S(2)}) collective-permute-start(bf16[4,2,128,512]{3,2,0,1:T(8,128)(2,1)S(1)} %slice_bitcast_fusion.6), channel_id=1, source_target_pairs={{0,4},{2,6},{4,0},{6,2},{8,12},{10,14},{12,8},{14,10},{16,20},{18,... | collective-permute-start | bytes 3145736 | tf_op jit(solution)/shard_map/ppermute | solution.py:109
  353.3 36.8 %collective-permute-start.32 = (bf16[4,128,512]{2,1,0:T(8,128)(2,1)S(1)}, bf16[4,128,512]{2,1,0:T(8,128)(2,1)S(1)}, u32[]{:S(2)}, u32[]{:S(2)}) collective-permute-start(bf16[4,128,512]{2,1,0:T(8,128)(2,1)S(1)} %slice_bitcast_fusion.8), channel_id=1, source_target_pairs={{0,4},{2,6},{4,0},{6,2},{8,12},{10,14},{12,8},{14,10},{16,20},{18,... | collective-permute-start | bytes 1572872 | tf_op jit(solution)/shard_map/ppermute | solution.py:109
  356.7 33.5 %collective-permute-start.29 = (bf16[4,128,512]{2,1,0:T(8,128)(2,1)S(1)}, bf16[4,128,512]{2,1,0:T(8,128)(2,1)S(1)}, u32[]{:S(2)}, u32[]{:S(2)}) collective-permute-start(bf16[4,128,512]{2,1,0:T(8,128)(2,1)S(1)} %slice_bitcast_fusion.10), channel_id=1, source_target_pairs={{0,1},{1,0},{2,3},{3,2},{4,5},{5,4},{6,7},{7,6},{8,9},{9,8},{10,11... | collective-permute-start | bytes 1572872 | tf_op jit(solution)/shard_map/ppermute | solution.py:112
  375.8 24.8 %collective-permute-start.14 = (bf16[4,128,512]{2,1,0:T(8,128)(2,1)S(1)}, bf16[4,128,512]{2,1,0:T(8,128)(2,1)S(1)}, u32[]{:S(2)}, u32[]{:S(2)}) collective-permute-start(bf16[4,128,512]{2,1,0:T(8,128)(2,1)S(1)} %slice_bitcast_fusion.12), channel_id=1, source_target_pairs={{0,4},{2,6},{4,0},{6,2},{8,12},{10,14},{12,8},{14,10},{16,20},{18,... | collective-permute-start | bytes 1572872 | tf_op jit(solution)/shard_map/ppermute | solution.py:109
  379.1 21.6 %collective-permute-start.11 = (bf16[4,128,512]{2,1,0:T(8,128)(2,1)S(1)}, bf16[4,128,512]{2,1,0:T(8,128)(2,1)S(1)}, u32[]{:S(2)}, u32[]{:S(2)}) collective-permute-start(bf16[4,128,512]{2,1,0:T(8,128)(2,1)S(1)} %slice_bitcast_fusion.14), channel_id=1, source_target_pairs={{0,1},{1,0},{2,3},{3,2},{4,5},{5,4},{6,7},{7,6},{8,9},{9,8},{10,11... | collective-permute-start | bytes 1572872 | tf_op jit(solution)/shard_map/ppermute | solution.py:112
  390.4 14.1 %collective-permute-start.33 = (bf16[2,128,512]{2,1,0:T(8,128)(2,1)S(1)}, bf16[2,128,512]{2,1,0:T(8,128)(2,1)S(1)}, u32[]{:S(2)}, u32[]{:S(2)}) collective-permute-start(bf16[2,128,512]{2,1,0:T(8,128)(2,1)S(1)} %get-tuple-element.30), channel_id=1, source_target_pairs={{0,24},{2,26},{4,28},{6,30},{8,0},{10,2},{12,4},{14,6},{16,8},{18,... | collective-permute-start | bytes 786440 | tf_op jit(solution)/shard_map/ppermute | solution.py:115
  394.3 16.4 %collective-permute-start.35 = (bf16[2,128,512]{2,1,0:T(8,128)(2,1)S(1)}, bf16[2,128,512]{2,1,0:T(8,128)(2,1)S(1)}, u32[]{:S(2)}, u32[]{:S(2)}) collective-permute-start(bf16[2,128,512]{2,1,0:T(8,128)(2,1)S(1)} %get-tuple-element.31), channel_id=1, source_target_pairs={{0,8},{2,10},{4,12},{6,14},{8,16},{10,18},{12,20},{14,22},{16,24},... | collective-permute-start | bytes 786440 | tf_op jit(solution)/shard_map/ppermute | solution.py:115
  394.3 34.9 %collective-permute-start.34 = (bf16[2,128,512]{2,1,0:T(8,128)(2,1)S(1)}, bf16[2,128,512]{2,1,0:T(8,128)(2,1)S(1)}, u32[]{:S(2)}, u32[]{:S(2)}) collective-permute-start(bf16[2,128,512]{2,1,0:T(8,128)(2,1)S(1)} %get-tuple-element.32), channel_id=1, source_target_pairs={{0,16},{2,18},{4,20},{6,22},{8,24},{10,26},{12,28},{14,30},{16,0},... | collective-permute-start | bytes 786440 | tf_op jit(solution)/shard_map/ppermute | solution.py:115
  400.9 28.5 %collective-permute-start.15 = (bf16[2,128,512]{2,1,0:T(8,128)(2,1)S(1)}, bf16[2,128,512]{2,1,0:T(8,128)(2,1)S(1)}, u32[]{:S(2)}, u32[]{:S(2)}) collective-permute-start(bf16[2,128,512]{2,1,0:T(8,128)(2,1)S(1)} %get-tuple-element.33), channel_id=1, source_target_pairs={{0,24},{2,26},{4,28},{6,30},{8,0},{10,2},{12,4},{14,6},{16,8},{18,... | collective-permute-start | bytes 786440 | tf_op jit(solution)/shard_map/ppermute | solution.py:115
  404.5 25.0 %collective-permute-start.17 = (bf16[2,128,512]{2,1,0:T(8,128)(2,1)S(1)}, bf16[2,128,512]{2,1,0:T(8,128)(2,1)S(1)}, u32[]{:S(2)}, u32[]{:S(2)}) collective-permute-start(bf16[2,128,512]{2,1,0:T(8,128)(2,1)S(1)} %get-tuple-element.34), channel_id=1, source_target_pairs={{0,8},{2,10},{4,12},{6,14},{8,16},{10,18},{12,20},{14,22},{16,24},... | collective-permute-start | bytes 786440 | tf_op jit(solution)/shard_map/ppermute | solution.py:115
  404.5 34.7 %copy-start.1 = (bf16[1,704,2048]{2,1,0:T(8,128)(2,1)S(1)}, bf16[1,704,2048]{2,1,0:T(8,128)(2,1)}, u32[]{:S(2)}) copy-start(bf16[1,704,2048]{2,1,0:T(8,128)(2,1)} %param.13) | copy-start | bytes 8650756
  404.5 33.1 %collective-permute-start.16 = (bf16[2,128,512]{2,1,0:T(8,128)(2,1)S(1)}, bf16[2,128,512]{2,1,0:T(8,128)(2,1)S(1)}, u32[]{:S(2)}, u32[]{:S(2)}) collective-permute-start(bf16[2,128,512]{2,1,0:T(8,128)(2,1)S(1)} %get-tuple-element.35), channel_id=1, source_target_pairs={{0,16},{2,18},{4,20},{6,22},{8,24},{10,26},{12,28},{14,30},{16,0},... | collective-permute-start | bytes 786440 | tf_op jit(solution)/shard_map/ppermute | solution.py:115
  (20 other events, 84.3 us)

commit v2 on v0

--- a/solution.py
+++ b/solution.py
@@ -1,10 +1,17 @@
+import functools
+
 import jax
 import jax.numpy as jnp
 from jax import lax
+from jax.experimental import pallas as pl
+from jax.experimental.pallas import tpu as pltpu
 from jax.sharding import PartitionSpec as P
 
-
-def body(tokens, grad_out, gates, expert_ids, w_gate, w_up, w_down):
+F32 = jnp.float32
+BF16 = jnp.bfloat16
+
+
+def slots_body(tokens, grad_out, gates, expert_ids, w_gate, w_up, w_down):
     expert_count = lax.axis_size("expert")
     tok_count = expert_ids.shape[0]
     top_count = expert_ids.shape[1]
@@ -82,6 +89,272 @@
     return (mixed, grad_tokens, grad_gates, grad_gate[None], grad_up[None], grad_down[None])
 
 
+LAST = (((1,), (1,)), ((), ()))
+FIRST = (((0,), (0,)), ((), ()))
+
+
+def dot(left, right, dims=(((1,), (0,)), ((), ()))):
+    return lax.dot_general(left, right, dims, preferred_element_type=F32)
+
+
+def after(value, *others):
+    return lax.optimization_barrier((value, *others))[0]
+
+
+def picks(pos, place, capacity):
+    row = pos[0, place : place + 1, :]
+    slot = lax.broadcasted_iota(jnp.int32, (capacity, row.shape[1]), 0).astype(F32)
+    return row == slot
+
+
+def gather_rows(side, pos, pieces, rows, capacity):
+    half = pieces[0].shape[-1]
+    for core in range(2):
+        for pair in range(2):
+            place = 2 * core + pair
+            pick = picks(pos, place, capacity).astype(BF16)
+            at = pl.ds(place * capacity, capacity)
+            for far in range(2):
+                column = pl.multiple_of((side ^ far) * 2 * half, half)
+                a = pieces[2 * core + pair][far, 0]
+                b = pieces[4 + 2 * core + far][pair, 0]
+                rows[at, pl.ds(column, half)] = dot(pick, a).astype(BF16)
+                rows[at, pl.ds(column + half, half)] = dot(pick, b).astype(BF16)
+
+
+def gate_rows(pos, gate, capacity):
+    out = []
+    for place in range(4):
+        pick = picks(pos, place, capacity)
+        out.append(jnp.sum(jnp.where(pick, gate[0, place : place + 1, :], 0.0), axis=1, keepdims=True))
+    return jnp.concatenate(out, axis=0)
+
+
+def scatter_rows(side, pos, values, outs, capacity):
+    half = outs[0].shape[-1]
+    for core in range(2):
+        for pair in range(2):
+            place = 2 * core + pair
+            pick = picks(pos, place, capacity).astype(BF16)
+            at = pl.ds(place * capacity, capacity)
+            for far in range(2):
+                column = pl.multiple_of((side ^ far) * 2 * half, half)
+                a = dot(pick, values[at, pl.ds(column, half)], FIRST)
+                outs[core][pair, far, 0] = a.astype(BF16)
+                b = dot(pick, values[at, pl.ds(column + half, half)], FIRST)
+                outs[2 + core][far, pair, 0] = b.astype(BF16)
+
+
+def up_kernel(capacity, side, pos, gate, *refs):
+    pieces, (weight_gate, weight_up, rows, gate_pre, up_pre, scaled) = refs[:8], refs[8:]
+    gather_rows(side[0], pos, pieces, rows, capacity)
+    gates = gate_rows(pos, gate, capacity)
+    got = rows[...]
+    pre = dot(got, weight_gate[...])
+    up = dot(got, weight_up[...])
+    gate_pre[...] = pre
+    up_pre[...] = up
+    scaled[...] = (gates * (pre * jax.nn.sigmoid(pre) * up)).astype(BF16)
+
+
+def mix_kernel(capacity, side, pos, scaled, weight_down, *refs):
+    outs, values = refs[:4], refs[4]
+    values[...] = dot(scaled[...], weight_down[...]).astype(BF16)
+    scatter_rows(side[0], pos, values, outs, capacity)
+
+
+def back_kernel(capacity, side, pos, gate, *refs):
+    pieces, (weight_down, gate_pre, up_pre, rows, grad_gate_pre, grad_up_pre, sums) = refs[:8], refs[8:]
+    gather_rows(side[0], pos, pieces, rows, capacity)
+    gates = gate_rows(pos, gate, capacity)
+    plain = dot(rows[...], weight_down[...], LAST)
+    pre, up = gate_pre[...], up_pre[...]
+    sig = jax.nn.sigmoid(pre)
+    silu = pre * sig
+    row_sums = jnp.sum(silu * up * plain, axis=1, keepdims=True)
+    grad_act = gates * plain
+    grad_gate_pre[...] = (grad_act * up * sig * (1.0 + pre * (1.0 - sig))).astype(BF16)
+    grad_up_pre[...] = (grad_act * silu).astype(BF16)
+    for place in range(4):
+        pick = picks(pos, place, capacity)
+        own = row_sums[place * capacity : (place + 1) * capacity]
+        sums[0, place : place + 1, :] = jnp.sum(jnp.where(pick, own, 0.0), axis=0, keepdims=True)
+
+
+def input_kernel(capacity, side, pos, grad_gate_pre, grad_up_pre, weight_gate, weight_up, *refs):
+    outs, values = refs[:4], refs[4]
+    terms = dot(grad_gate_pre[...], weight_gate[...], LAST)
+    values[...] = (terms + dot(grad_up_pre[...], weight_up[...], LAST)).astype(BF16)
+    scatter_rows(side[0], pos, values, outs, capacity)
+
+
+def gather_body(tokens, grad_out, gates, expert_ids, w_gate, w_up, w_down):
+    expert_count = lax.axis_size("expert")
+    tok_count, top_count = expert_ids.shape
+    capacity = tok_count * top_count * 4 // (3 * expert_count)
+    width = tokens.shape[1]
+    half = width // 2
+    column = expert_count // 4
+    features = 2 * width
+    hidden = w_gate.shape[2]
+    step_rows = 4 * capacity
+    slots = column * step_rows
+    me = lax.axis_index("expert")
+    side = lax.axis_index("tensor").astype(jnp.int32).reshape(1)
+
+    core_pairs = [(e, e ^ 1) for e in range(expert_count)]
+    chip_pairs = [(e, e ^ 2) for e in range(expert_count)]
+
+    def swap_core(value):
+        return lax.ppermute(value, "expert", core_pairs)
+
+    def swap_pair(value):
+        return lax.ppermute(value, "expert", chip_pairs)
+
+    def swap_side(value):
+        return lax.ppermute(value, "tensor", [(0, 1), (1, 0)])
+
+    def shift(value, step):
+        return lax.ppermute(
+            value, "expert", [(e, (e + 4 * step) % expert_count) for e in range(expert_count)]
+        )
+
+    def spread(rows, start):
+        own = after(jnp.stack([rows[:, :half], rows[:, half:]]), *start)
+        parts = [own] + [shift(own, step) for step in range(1, column)]
+        a = jnp.stack([part[0] for part in parts])
+        b = jnp.stack([part[1] for part in parts])
+        a = jnp.stack([a, swap_side(a)])
+        b = jnp.stack([b, swap_pair(b)])
+        far_a = swap_pair(a)
+        far_b = swap_side(b)
+        pieces = (a, far_a, swap_core(a), swap_core(far_a), b, far_b, swap_core(b), swap_core(far_b))
+        return pieces, parts
+
+    def spread_routing():
+        own = jnp.concatenate([expert_ids.astype(F32), gates], axis=1).T
+        all_parts = jnp.stack([own] + [shift(own, step) for step in range(1, column)])
+        all_parts = jnp.stack([all_parts, swap_pair(all_parts)], axis=1)
+        all_parts = jnp.concatenate([all_parts, swap_core(all_parts)], axis=1)
+        named = all_parts[:, :, :top_count] == me.astype(F32)
+        gate = jnp.sum(jnp.where(named, all_parts[:, :, top_count:], 0.0), axis=2)
+        member = jnp.any(named, axis=2)
+        upto = jnp.triu(jnp.ones((tok_count, tok_count), BF16))
+        count = jnp.dot(member.astype(BF16), upto, preferred_element_type=F32)
+        return jnp.where(member, count - 1.0, -1.0), gate
+
+    def add(*terms):
+        return sum(term.astype(F32) for term in terms)
+
+    def collect(outs):
+        own_a, other_a, own_b, other_b = outs
+        core_a, core_b = swap_core(other_a), swap_core(other_b)
+        first_a = swap_pair(add(own_a[1], core_a[1]).astype(BF16))
+        first_b = swap_side(add(own_b[1], core_b[1]).astype(BF16))
+        second_a = swap_side(add(own_a[0, 1], core_a[0, 1], first_a[1]).astype(BF16))
+        second_b = swap_pair(add(own_b[0, 1], core_b[0, 1], first_b[1]).astype(BF16))
+        a = add(own_a[0, 0], core_a[0, 0], first_a[0], second_a)
+        b = add(own_b[0, 0], core_b[0, 0], first_b[0], second_b)
+        both = jnp.stack([a, b], axis=1)
+        total = both[0]
+        for step in range(1, column):
+            total = total + shift(both[step].astype(BF16), column - step).astype(F32)
+        return jnp.concatenate([total[0], total[1]], axis=1).astype(BF16)
+
+    table = pl.BlockSpec((1, 4, tok_count), lambda i, s: (i, 0, 0))
+    piece = pl.BlockSpec((2, 1, tok_count, half), lambda i, s: (0, i, 0, 0))
+    out_piece = pl.BlockSpec((2, 2, 1, tok_count, half), lambda i, s: (0, 0, i, 0, 0))
+
+    def rows_of(size):
+        return pl.BlockSpec((step_rows, size), lambda i, s: (i, 0))
+
+    def whole(*shape):
+        return pl.BlockSpec(shape, lambda i, s: (0, 0), pipeline_mode=pl.Buffered(1))
+
+    def kernel(run, macs, in_specs, outs, scratch=()):
+        return pl.pallas_call(
+            functools.partial(run, capacity),
+            out_shape=[shape for shape, _ in outs],
+            grid_spec=pltpu.PrefetchScalarGridSpec(
+                num_scalar_prefetch=1,
+                grid=(column,),
+                in_specs=in_specs,
+                out_specs=[spec for _, spec in outs],
+                scratch_shapes=scratch,
+            ),
+            compiler_params=pltpu.CompilerParams(vmem_limit_bytes=40 * 1024 * 1024),
+            cost_estimate=pl.CostEstimate(
+                flops=2 * macs, bytes_accessed=16 * 1024 * 1024, transcendentals=0
+            ),
+        )
+
+    def shaped(shape, dtype):
+        return jax.ShapeDtypeStruct(shape, dtype)
+
+    row_out = (shaped((slots, features), BF16), rows_of(features))
+    hidden_f32 = (shaped((slots, hidden), F32), rows_of(hidden))
+    hidden_bf = (shaped((slots, hidden), BF16), rows_of(hidden))
+    piece_outs = [(shaped((2, 2, column, tok_count, half), BF16), out_piece)] * 4
+    macs = slots * features * hidden
+    values = [pltpu.VMEM((step_rows, features), BF16)]
+
+    weight_gate, weight_up, weight_down = w_gate[0], w_up[0], w_down[0]
+    wide = whole(features, hidden)
+    tall = whole(hidden, features)
+
+    token_pieces, token_parts = spread(tokens, ())
+    pos, gate = spread_routing()
+    grad_pieces, _ = spread(grad_out, token_parts)
+
+    rows, gate_pre, up_pre, scaled = kernel(
+        up_kernel,
+        2 * macs,
+        [table, table] + [piece] * 8 + [wide, wide],
+        [row_out, hidden_f32, hidden_f32, hidden_bf],
+    )(side, pos, gate, *token_pieces, weight_gate, weight_up)
+    mix_out = kernel(
+        mix_kernel, macs, [table, rows_of(hidden), tall], piece_outs, values
+    )(side, pos, scaled, weight_down)
+    mixed = collect(mix_out)
+    grad_rows, grad_gate_pre, grad_up_pre, token_sums = kernel(
+        back_kernel,
+        macs,
+        [table, table] + [piece] * 8 + [tall, rows_of(hidden), rows_of(hidden)],
+        [row_out, hidden_bf, hidden_bf, (shaped((column, 4, tok_count), F32), table)],
+    )(side, pos, gate, *grad_pieces, weight_down, gate_pre, up_pre)
+    input_out = kernel(
+        input_kernel,
+        2 * macs,
+        [table, rows_of(hidden), rows_of(hidden), wide, wide],
+        piece_outs,
+        values,
+    )(side, pos, grad_gate_pre, grad_up_pre, weight_gate, weight_up)
+    grad_tokens = collect(input_out)
+
+    token_sums = token_sums + swap_side(token_sums)
+    block = jnp.arange(expert_count)
+    place = (me // 4 - block // 4) % column * 4 + ((me ^ block) % 2) * 2 + ((me ^ block) // 2) % 2
+    token_sums = token_sums.reshape(expert_count, tok_count)[place]
+    expert_sums = lax.all_to_all(token_sums, "expert", split_axis=0, concat_axis=0, tiled=True)
+    chosen = expert_ids[None] == jnp.arange(expert_count, dtype=jnp.int32)[:, None, None]
+    grad_gates = jnp.sum(jnp.where(chosen, expert_sums[:, :, None], 0.0), axis=0)
+
+    grad_down = dot(scaled, grad_rows, FIRST).astype(BF16)[None]
+    grad_gate = dot(rows, grad_gate_pre, FIRST).astype(BF16)[None]
+    grad_up = dot(rows, grad_up_pre, FIRST).astype(BF16)[None]
+    return (mixed, grad_tokens, grad_gates, grad_gate, grad_up, grad_down)
+
+
+def body(tokens, grad_out, gates, expert_ids, w_gate, w_up, w_down):
+    expert_count = lax.axis_size("expert")
+    tok_count, top_count = expert_ids.shape
+    slot_total = tok_count * top_count * 4 // (3 * expert_count) * expert_count
+    gathers = expert_count * tok_count <= 2 * slot_total
+    shaped = lax.axis_size("tensor") == 2 and expert_count % 4 == 0
+    plan = gather_body if gathers and shaped else slots_body
+    return plan(tokens, grad_out, gates, expert_ids, w_gate, w_up, w_down)
+
+
 def solution(mesh):
     placed = (
         P("expert", "tensor"),

time: 530 us -> 308 us (0.58)
  the two profiles are of different devices: /device:TPU:18 before, /device:TPU:0 now
where the time goes in v2:
time: 308 us; the launch traced here: 307 us
  waiting for transfers between devices  131 us (43%)
  starting transfers between devices  65.2 us (21%)
  Pallas kernels  44.4 us (14%)
  other arithmetic  27.1 us (9%)
  local copies, waits for them, and re-layouts  21.9 us (7%)
  matrix products  16.2 us (5%)
    ppermute x15, waiting for transfers between devices, shift(): lax.ppermute(value, 'expert', [(e, (e + 4 * step) % expert_count) for e i...  54.7 us
    ppermute x9, waiting for transfers between devices, swap_pair(): return lax.ppermute(value, 'expert', chip_pairs)  49.7 us
    ppermute x15, starting transfers between devices, shift(): lax.ppermute(value, 'expert', [(e, (e + 4 * step) % expert_count) for e i...  34.1 us
    ppermute x9, waiting for transfers between devices, swap_side(): return lax.ppermute(value, 'tensor', [(0, 1), (1, 0)])  26.8 us
    unnamed x42, local copies, waits for them, and re-layouts  18.4 us
    dot_general x3, matrix products, dot(): return lax.dot_general(left, right, dims, preferred_element_type=F32)  16 us
    pallas_call x1, Pallas kernels, gather_body(): kernel(input_kernel, 2 * macs, [table, rows_of(hidden), rows_of(hidden),...  14.3 us
    pallas_call x1, Pallas kernels, gather_body(): kernel(up_kernel, 2 * macs, [table, table] + [piece] * 8 + [wide, wide],...  13.4 us
  transfers between devices with their start and end apart: 47, of which 16 were waited for; matrix products, arithmetic and copies ran while one was open for 18% of the time, Pallas kernels for 14%

profile of v2, /device:TPU:0, one launch (start us, length us, event | category | flops | bytes accessed | tf_op | source)
XLA Modules:
  0.0 307.1 jit_solution(12882776419445993348)
XLA Ops:
  1.7 3.1 %collective-permute-start.5 = (bf16[2,128,512]{2,1,0:T(8,128)(2,1)S(1)}, bf16[2,128,512]{2,1,0:T(8,128)(2,1)S(1)}, u32[]{:S(2)}, u32[]{:S(2)}) collective-permute-start(bf16[2,128,512]{2,1,0:T(8,128)(2,1)S(1)} %pad_maximum_fusion.10), channel_id=1, source_target_pairs={{0,8},{2,10},{4,12},{6,14},{8,16},{10,18},{12,20},{14,22},{16,24},... | collective-permute-start | bytes 786440 | tf_op jit(solution)/shard_map/ppermute | solution.py:218
  4.7 2.6 collective-permute-start.6
  12.1 1.9 collective-permute-done.5
  14.0 10.6 %collective-permute-done.6 = bf16[2,128,512]{2,1,0:T(8,128)(2,1)S(1)} collective-permute-done((bf16[2,128,512]{2,1,0:T(8,128)(2,1)S(1)}, bf16[2,128,512]{2,1,0:T(8,128)(2,1)S(1)}, u32[]{:S(2)}, u32[]{:S(2)}) %collective-permute-start.6) | collective-permute-done | bytes 262176 | tf_op jit(solution)/shard_map/ppermute | solution.py:218
  24.6 6.3 %collective-permute-start.25 = (bf16[2,128,512]{2,1,0:T(8,128)(2,1)S(1)}, bf16[2,128,512]{2,1,0:T(8,128)(2,1)S(1)}, u32[]{:S(2)}, u32[]{:S(2)}) collective-permute-start(bf16[2,128,512]{2,1,0:T(8,128)(2,1)S(1)} %pad_maximum_fusion.12), channel_id=1, source_target_pairs={{0,8},{2,10},{4,12},{6,14},{8,16},{10,18},{12,20},{14,22},{16,24},... | collective-permute-start | bytes 786440 | tf_op jit(solution)/shard_map/ppermute | solution.py:218
  32.6 1.6 collective-permute-start.12
  34.3 4.9 %collective-permute-done.25 = bf16[2,128,512]{2,1,0:T(8,128)(2,1)S(1)} collective-permute-done((bf16[2,128,512]{2,1,0:T(8,128)(2,1)S(1)}, bf16[2,128,512]{2,1,0:T(8,128)(2,1)S(1)}, u32[]{:S(2)}, u32[]{:S(2)}) %collective-permute-start.25) | collective-permute-done | bytes 262176 | tf_op jit(solution)/shard_map/ppermute | solution.py:218
  40.7 7.7 %collective-permute-done.26 = bf16[2,128,512]{2,1,0:T(8,128)(2,1)S(1)} collective-permute-done((bf16[2,128,512]{2,1,0:T(8,128)(2,1)S(1)}, bf16[2,128,512]{2,1,0:T(8,128)(2,1)S(1)}, u32[]{:S(2)}, u32[]{:S(2)}) %collective-permute-start.26) | collective-permute-done | bytes 262176 | tf_op jit(solution)/shard_map/ppermute | solution.py:218
  48.4 2.6 collective-permute-start.2
  51.2 1.6 collective-permute-start.13
  53.8 4.6 %collective-permute-done.27 = bf16[2,128,512]{2,1,0:T(8,128)(2,1)S(1)} collective-permute-done((bf16[2,128,512]{2,1,0:T(8,128)(2,1)S(1)}, bf16[2,128,512]{2,1,0:T(8,128)(2,1)S(1)}, u32[]{:S(2)}, u32[]{:S(2)}) %collective-permute-start.27) | collective-permute-done | bytes 262176 | tf_op jit(solution)/shard_map/ppermute | solution.py:218
  58.4 1.5 collective-permute-start.9
  60.0 1.6 collective-permute-start.28
  62.3 20.4 %collective-permute-done.3 = f32[4,12,128]{2,1,0:T(8,128)S(1)} collective-permute-done((f32[4,12,128]{2,1,0:T(8,128)S(1)}, f32[4,12,128]{2,1,0:T(8,128)S(1)}, u32[]{:S(2)}, u32[]{:S(2)}) %collective-permute-start.3) | collective-permute-done | bytes 24608 | tf_op jit(solution)/shard_map/ppermute | solution.py:212
  84.2 2.5 collective-permute-done.28
  86.8 7.2 %collective-permute-done.32 = bf16[4,128,512]{2,1,0:T(8,128)(2,1)S(1)} collective-permute-done((bf16[4,128,512]{2,1,0:T(8,128)(2,1)S(1)}, bf16[4,128,512]{2,1,0:T(8,128)(2,1)S(1)}, u32[]{:S(2)}, u32[]{:S(2)}) %collective-permute-start.32) | collective-permute-done | bytes 524320 | tf_op jit(solution)/shard_map/ppermute | solution.py:212
  94.1 1.6 collective-permute-start.29
  98.6 4.6 %copy.38 = bf16[1,2048,704]{2,1,0:T(8,128)(2,1)} copy(bf16[1,2048,704]{1,2,0:T(8,128)(2,1)} %param.11) | data formatting | bytes 5767168 | tf_op args[4]
  103.2 4.7 %copy.39 = bf16[1,2048,704]{2,1,0:T(8,128)(2,1)} copy(bf16[1,2048,704]{1,2,0:T(8,128)(2,1)} %param.12) | data formatting | bytes 5767168 | tf_op args[5]
  108.1 11.6 %collective-permute-done.29.refs_1_ = bf16[2,4,128,512]{3,2,1,0:T(8,128)(2,1)S(1)} collective-permute-done((bf16[2,4,128,512]{3,2,1,0:T(8,128)(2,1)S(1)}, bf16[2,4,128,512]{3,2,1,0:T(8,128)(2,1)S(1)}, u32[]{:S(2)}, u32[]{:S(2)}) %collective-permute-start.29) | collective-permute-done | bytes 1048608 | tf_op jit(solution)/shard_map/ppermute | solution.py:212
  124.2 13.4 %shard_map.118 = (bf16[1024,2048]{1,0:T(8,128)(2,1)}, f32[1024,704]{1,0:T(8,128)S(1)}, f32[1024,704]{1,0:T(8,128)}, bf16[1024,704]{1,0:T(8,128)(2,1)S(1)}) custom-call(s32[1]{0:T(128)} %bitcast.side, f32[4,4,128]{2,1,0:T(4,128)S(1)} %fusion.5.pos, f32[4,4,128]{2,1,0:T(4,128)S(1)} %copy.40.gate, bf16[2,4,128,512]{3,2,1,0:T(8,128)(2,1)} %pad_maximum_fusion.2.refs_0_, ...), custom_call_target="tpu_custom_call" | custom-call | flops 5905580032 | bytes 16777216 | tf_op jit(solution)/shard_map/pallas_call | solution.py:309
  137.6 1.7 copy-done
  141.9 7.9 %shard_map.119 = (bf16[2,2,4,128,512]{4,3,2,1,0:T(8,128)(2,1)S(1)}, bf16[2,2,4,128,512]{4,3,2,1,0:T(8,128)(2,1)}, bf16[2,2,4,128,512]{4,3,2,1,0:T(8,128)(2,1)S(1)}, bf16[2,2,4,128,512]{4,3,2,1,0:T(8,128)(2,1)}) custom-call(s32[1]{0:T(128)} %bitcast.side, f32[4,4,128]{2,1,0:T(4,128)S(1)} %fusion.5.pos, bf16[1024,704]{1,0:T(8,128)(2,1)S(1)} %copy-done.16, ...), custom_call_target="tpu_custom_call" | custom-call | flops 2952790016 | bytes 16777216 | tf_op jit(solution)/shard_map/pallas_call | solution.py:315
  151.7 8.8 %shard_map.120 = (bf16[1024,2048]{1,0:T(8,128)(2,1)}, bf16[1024,704]{1,0:T(8,128)(2,1)S(1)}, bf16[1024,704]{1,0:T(8,128)(2,1)S(1)}, f32[4,4,128]{2,1,0:T(4,128)S(1)}) custom-call(s32[1]{0:T(128)} %bitcast.side, f32[4,4,128]{2,1,0:T(4,128)S(1)} %fusion.5.pos, f32[4,4,128]{2,1,0:T(4,128)S(1)} %copy.40.gate, ...), custom_call_target="tpu_custom_call" | custom-call | flops 2952790016 | bytes 16777216 | tf_op jit(solution)/shard_map/pallas_call | solution.py:319
  160.6 14.3 %shard_map.121 = (bf16[2,2,4,128,512]{4,3,2,1,0:T(8,128)(2,1)S(1)}, bf16[2,2,4,128,512]{4,3,2,1,0:T(8,128)(2,1)}, bf16[2,2,4,128,512]{4,3,2,1,0:T(8,128)(2,1)S(1)}, bf16[2,2,4,128,512]{4,3,2,1,0:T(8,128)(2,1)}) custom-call(s32[1]{0:T(128)} %bitcast.side, f32[4,4,128]{2,1,0:T(4,128)S(1)} %fusion.5.pos, bf16[1024,704]{1,0:T(8,128)(2,1)S(1)} %get-tuple-element.31.grad_gate_pre, ...), custom_call_target="tpu_custom_call" | custom-call | flops 5905580032 | bytes 16777216 | tf_op jit(solution)/shard_map/pallas_call | solution.py:325
  174.9 1.6 collective-permute-start.45
  176.6 4.5 %fusion.1 = bf16[1,2048,704]{1,2,0:T(8,128)(2,1)} fusion(bf16[1024,2048]{1,0:T(8,128)(2,1)S(1)} %copy-done.19, bf16[1024,704]{1,0:T(8,128)(2,1)S(1)} %get-tuple-element.32.grad_up_pre), kind=kOutput, calls=%fused_computation.5 | convolution fusion | flops 2954231808 | bytes 8519680 | tf_op jit(solution)/shard_map/dot_general | solution.py:97
  181.2 4.5 %fusion = bf16[1,2048,704]{1,2,0:T(8,128)(2,1)} fusion(bf16[1024,2048]{1,0:T(8,128)(2,1)S(1)} %copy-done.19, bf16[1024,704]{1,0:T(8,128)(2,1)S(1)} %get-tuple-element.31.grad_gate_pre), kind=kOutput, calls=%fused_computation.4 | convolution fusion | flops 2954231808 | bytes 8519680 | tf_op jit(solution)/shard_map/dot_general | solution.py:97
  186.8 3.9 %all-to-all-start = ((f32[16,1,128]{2,1,0:T(1,128)}), f32[16,1,128]{2,1,0:T(1,128)S(1)}, u32[]{:S(2)}, u32[]{:S(2)}) async-start(f32[16,1,128]{2,1,0:T(1,128)} %bitcast.63), calls=%async_computation | async-start | bytes 16384 | tf_op jit(solution)/shard_map/all_to_all | solution.py:338
  190.8 1.8 fusion.7
  193.2 2.5 fusion.6
  195.8 1.9 collective-permute-start.17
  197.7 2.5 fusion.9
  201.7 2.5 fusion.8
  204.4 7.0 %fusion.2 = bf16[1,704,2048]{2,1,0:T(8,128)(2,1)} fusion(bf16[1024,704]{1,0:T(8,128)(2,1)S(1)} %copy-done.17, bf16[1024,2048]{1,0:T(8,128)(2,1)} %get-tuple-element.39), kind=kOutput, calls=%fused_computation.6 | convolution fusion | flops 2954231808 | bytes 8519680 | tf_op jit(solution)/shard_map/dot_general | solution.py:97
  212.1 6.7 %collective-permute-done.20 = bf16[2,4,128,512]{3,2,1,0:T(8,128)(2,1)} collective-permute-done((bf16[2,4,128,512]{3,2,1,0:T(8,128)(2,1)S(1)}, bf16[2,4,128,512]{3,2,1,0:T(8,128)(2,1)}, u32[]{:S(2)}, u32[]{:S(2)}) %collective-permute-start.20) | collective-permute-done | bytes 1048608 | tf_op jit(solution)/shard_map/ppermute | solution.py:215
  218.8 1.6 fusion.16
  220.3 2.0 collective-permute-start.21
  225.0 16.2 %collective-permute-done.40 = bf16[2,4,128,512]{3,2,1,0:T(8,128)(2,1)} collective-permute-done((bf16[2,4,128,512]{3,2,1,0:T(8,128)(2,1)}, bf16[2,4,128,512]{3,2,1,0:T(8,128)(2,1)}, u32[]{:S(2)}, u32[]{:S(2)}) %collective-permute-start.40) | collective-permute-done | bytes 1048608 | tf_op jit(solution)/shard_map/ppermute | solution.py:215
  242.6 2.0 collective-permute-start.41
  247.5 8.2 %collective-permute-done.21 = bf16[4,128,512]{2,1,0:T(8,128)(2,1)S(1)} collective-permute-done((bf16[4,128,512]{2,1,0:T(8,128)(2,1)S(1)}, bf16[4,128,512]{2,1,0:T(8,128)(2,1)S(1)}, u32[]{:S(2)}, u32[]{:S(2)}) %collective-permute-start.21) | collective-permute-done | bytes 524320 | tf_op jit(solution)/shard_map/ppermute | solution.py:212
  255.7 1.6 fusion.18
  259.0 3.8 %collective-permute-start.22 = (bf16[2,128,512]{2,1,0:T(8,128)(2,1)S(1)}, bf16[2,128,512]{2,1,0:T(8,128)(2,1)S(1)}, u32[]{:S(2)}, u32[]{:S(2)}) collective-permute-start(bf16[2,128,512]{2,1,0:T(8,128)(2,1)S(1)} %get-tuple-element.45), channel_id=1, source_target_pairs={{0,24},{2,26},{4,28},{6,30},{8,0},{10,2},{12,4},{14,6},{16,8},{18,... | collective-permute-start | bytes 786440 | tf_op jit(solution)/shard_map/ppermute | solution.py:218
  263.9 2.4 collective-permute-done.41
  269.5 3.5 %collective-permute-start.42 = (bf16[2,128,512]{2,1,0:T(8,128)(2,1)S(1)}, bf16[2,128,512]{2,1,0:T(8,128)(2,1)S(1)}, u32[]{:S(2)}, u32[]{:S(2)}) collective-permute-start(bf16[2,128,512]{2,1,0:T(8,128)(2,1)S(1)} %get-tuple-element.42), channel_id=1, source_target_pairs={{0,24},{2,26},{4,28},{6,30},{8,0},{10,2},{12,4},{14,6},{16,8},{18,... | collective-permute-start | bytes 786440 | tf_op jit(solution)/shard_map/ppermute | solution.py:218
  272.9 7.2 %collective-permute-start.44 = (bf16[2,128,512]{2,1,0:T(8,128)(2,1)S(1)}, bf16[2,128,512]{2,1,0:T(8,128)(2,1)S(1)}, u32[]{:S(2)}, u32[]{:S(2)}) collective-permute-start(bf16[2,128,512]{2,1,0:T(8,128)(2,1)S(1)} %get-tuple-element.43), channel_id=1, source_target_pairs={{0,8},{2,10},{4,12},{6,14},{8,16},{10,18},{12,20},{14,22},{16,24},... | collective-permute-start | bytes 786440 | tf_op jit(solution)/shard_map/ppermute | solution.py:218
  280.2 17.4 %collective-permute-done.23 = bf16[2,128,512]{2,1,0:T(8,128)(2,1)S(1)} collective-permute-done((bf16[2,128,512]{2,1,0:T(8,128)(2,1)S(1)}, bf16[2,128,512]{2,1,0:T(8,128)(2,1)S(1)}, u32[]{:S(2)}, u32[]{:S(2)}) %collective-permute-start.23) | collective-permute-done | bytes 262176 | tf_op jit(solution)/shard_map/ppermute | solution.py:218
  298.5 7.7 %collective-permute-done.43 = bf16[2,128,512]{2,1,0:T(8,128)(2,1)S(1)} collective-permute-done((bf16[2,128,512]{2,1,0:T(8,128)(2,1)S(1)}, bf16[2,128,512]{2,1,0:T(8,128)(2,1)S(1)}, u32[]{:S(2)}, u32[]{:S(2)}) %collective-permute-start.43) | collective-permute-done | bytes 262176 | tf_op jit(solution)/shard_map/ppermute | solution.py:218
  (152 shorter events, 44.0 us)
Async XLA Ops:
  1.7 12.4 %collective-permute-start.5 = (bf16[2,128,512]{2,1,0:T(8,128)(2,1)S(1)}, bf16[2,128,512]{2,1,0:T(8,128)(2,1)S(1)}, u32[]{:S(2)}, u32[]{:S(2)}) collective-permute-start(bf16[2,128,512]{2,1,0:T(8,128)(2,1)S(1)} %pad_maximum_fusion.10), channel_id=1, source_target_pairs={{0,8},{2,10},{4,12},{6,14},{8,16},{10,18},{12,20},{14,22},{16,24},... | collective-permute-start | bytes 786440 | tf_op jit(solution)/shard_map/ppermute | solution.py:218
  4.7 19.9 %collective-permute-start.6 = (bf16[2,128,512]{2,1,0:T(8,128)(2,1)S(1)}, bf16[2,128,512]{2,1,0:T(8,128)(2,1)S(1)}, u32[]{:S(2)}, u32[]{:S(2)}) collective-permute-start(bf16[2,128,512]{2,1,0:T(8,128)(2,1)S(1)} %pad_maximum_fusion.10), channel_id=1, source_target_pairs={{0,16},{2,18},{4,20},{6,22},{8,24},{10,26},{12,28},{14,30},{16,0},... | collective-permute-start | bytes 786440 | tf_op jit(solution)/shard_map/ppermute | solution.py:218
  7.3 17.3 %collective-permute-start.7 = (bf16[2,128,512]{2,1,0:T(8,128)(2,1)S(1)}, bf16[2,128,512]{2,1,0:T(8,128)(2,1)S(1)}, u32[]{:S(2)}, u32[]{:S(2)}) collective-permute-start(bf16[2,128,512]{2,1,0:T(8,128)(2,1)S(1)} %pad_maximum_fusion.10), channel_id=1, source_target_pairs={{0,24},{2,26},{4,28},{6,30},{8,0},{10,2},{12,4},{14,6},{16,8},{18,... | collective-permute-start | bytes 786440 | tf_op jit(solution)/shard_map/ppermute | solution.py:218
  10.1 50.0 %collective-permute-start = (f32[12,128]{1,0:T(8,128)S(1)}, f32[12,128]{1,0:T(8,128)S(1)}, u32[]{:S(2)}, u32[]{:S(2)}) collective-permute-start(f32[12,128]{1,0:T(8,128)S(1)} %get-tuple-element.83), channel_id=1, source_target_pairs={{0,8},{2,10},{4,12},{6,14},{8,16},{10,18},{12,20},{14,22},{16,24},... | collective-permute-start | bytes 18440 | tf_op jit(solution)/shard_map/ppermute | solution.py:218
  10.7 50.8 %collective-permute-start.1 = (f32[12,128]{1,0:T(8,128)S(1)}, f32[12,128]{1,0:T(8,128)S(1)}, u32[]{:S(2)}, u32[]{:S(2)}) collective-permute-start(f32[12,128]{1,0:T(8,128)S(1)} %get-tuple-element.83), channel_id=1, source_target_pairs={{0,16},{2,18},{4,20},{6,22},{8,24},{10,26},{12,28},{14,30},{16,0},... | collective-permute-start | bytes 18440 | tf_op jit(solution)/shard_map/ppermute | solution.py:218
  24.6 14.6 %collective-permute-start.25 = (bf16[2,128,512]{2,1,0:T(8,128)(2,1)S(1)}, bf16[2,128,512]{2,1,0:T(8,128)(2,1)S(1)}, u32[]{:S(2)}, u32[]{:S(2)}) collective-permute-start(bf16[2,128,512]{2,1,0:T(8,128)(2,1)S(1)} %pad_maximum_fusion.12), channel_id=1, source_target_pairs={{0,8},{2,10},{4,12},{6,14},{8,16},{10,18},{12,20},{14,22},{16,24},... | collective-permute-start | bytes 786440 | tf_op jit(solution)/shard_map/ppermute | solution.py:218
  31.0 17.4 %collective-permute-start.26 = (bf16[2,128,512]{2,1,0:T(8,128)(2,1)S(1)}, bf16[2,128,512]{2,1,0:T(8,128)(2,1)S(1)}, u32[]{:S(2)}, u32[]{:S(2)}) collective-permute-start(bf16[2,128,512]{2,1,0:T(8,128)(2,1)S(1)} %pad_maximum_fusion.12), channel_id=1, source_target_pairs={{0,16},{2,18},{4,20},{6,22},{8,24},{10,26},{12,28},{14,30},{16,0},... | collective-permute-start | bytes 786440 | tf_op jit(solution)/shard_map/ppermute | solution.py:218
  32.6 18.3 %collective-permute-start.12 = (bf16[4,128,512]{2,1,0:T(8,128)(2,1)S(1)}, bf16[4,128,512]{2,1,0:T(8,128)(2,1)S(1)}, u32[]{:S(2)}, u32[]{:S(2)}) collective-permute-start(bf16[4,128,512]{2,1,0:T(8,128)(2,1)S(1)} %get-tuple-element.53), channel_id=1, source_target_pairs={{0,4},{2,6},{4,0},{6,2},{8,12},{10,14},{12,8},{14,10},{16,20},{18,... | collective-permute-start | bytes 1572872 | tf_op jit(solution)/shard_map/ppermute | solution.py:212
  39.2 12.0 %collective-permute-start.8 = (bf16[4,128,512]{2,1,0:T(8,128)(2,1)S(1)}, bf16[4,128,512]{2,1,0:T(8,128)(2,1)S(1)}, u32[]{:S(2)}, u32[]{:S(2)}) collective-permute-start(bf16[4,128,512]{2,1,0:T(8,128)(2,1)S(1)} %get-tuple-element.55), channel_id=1, source_target_pairs={{0,1},{1,0},{2,3},{3,2},{4,5},{5,4},{6,7},{7,6},{8,9},{9,8},{10,11... | collective-permute-start | bytes 1572872 | tf_op jit(solution)/shard_map/ppermute | solution.py:215
  48.4 13.2 %collective-permute-start.2 = (f32[12,128]{1,0:T(8,128)S(1)}, f32[12,128]{1,0:T(8,128)S(1)}, u32[]{:S(2)}, u32[]{:S(2)}) collective-permute-start(f32[12,128]{1,0:T(8,128)S(1)} %get-tuple-element.83), channel_id=1, source_target_pairs={{0,24},{2,26},{4,28},{6,30},{8,0},{10,2},{12,4},{14,6},{16,8},{18,... | collective-permute-start | bytes 18440 | tf_op jit(solution)/shard_map/ppermute | solution.py:218
  51.0 7.4 %collective-permute-start.27 = (bf16[2,128,512]{2,1,0:T(8,128)(2,1)S(1)}, bf16[2,128,512]{2,1,0:T(8,128)(2,1)S(1)}, u32[]{:S(2)}, u32[]{:S(2)}) collective-permute-start(bf16[2,128,512]{2,1,0:T(8,128)(2,1)S(1)} %pad_maximum_fusion.12), channel_id=1, source_target_pairs={{0,24},{2,26},{4,28},{6,30},{8,0},{10,2},{12,4},{14,6},{16,8},{18,... | collective-permute-start | bytes 786440 | tf_op jit(solution)/shard_map/ppermute | solution.py:218
  51.2 44.5 %collective-permute-start.13 = (bf16[2,4,128,512]{3,2,1,0:T(8,128)(2,1)S(1)}, bf16[2,4,128,512]{3,2,1,0:T(8,128)(2,1)}, u32[]{:S(2)}, u32[]{:S(2)}) collective-permute-start(bf16[2,4,128,512]{3,2,1,0:T(8,128)(2,1)S(1)} %pad_maximum_fusion.3.refs_4_), channel_id=1, source_target_pairs={{0,1},{1,0},{2,3},{3,2},{4,5},{5,4},{6,7},{7,6},{8,9},{9,8},{10,11... | collective-permute-start | bytes 3145736 | tf_op jit(solution)/shard_map/ppermute | solution.py:215
  58.4 38.8 %collective-permute-start.9 = (bf16[2,4,128,512]{3,2,1,0:T(8,128)(2,1)}, bf16[2,4,128,512]{3,2,1,0:T(8,128)(2,1)}, u32[]{:S(2)}, u32[]{:S(2)}) collective-permute-start(bf16[2,4,128,512]{3,2,1,0:T(8,128)(2,1)} %pad_maximum_fusion.2.refs_0_), channel_id=1, source_target_pairs={{0,4},{2,6},{4,0},{6,2},{8,12},{10,14},{12,8},{14,10},{16,20},{18,... | collective-permute-start | bytes 3145736 | tf_op jit(solution)/shard_map/ppermute | solution.py:212
  60.0 26.6 %collective-permute-start.28 = (bf16[4,128,512]{2,1,0:T(8,128)(2,1)S(1)}, bf16[4,128,512]{2,1,0:T(8,128)(2,1)S(1)}, u32[]{:S(2)}, u32[]{:S(2)}) collective-permute-start(bf16[4,128,512]{2,1,0:T(8,128)(2,1)S(1)} %get-tuple-element.51), channel_id=1, source_target_pairs={{0,1},{1,0},{2,3},{3,2},{4,5},{5,4},{6,7},{7,6},{8,9},{9,8},{10,11... | collective-permute-start | bytes 1572872 | tf_op jit(solution)/shard_map/ppermute | solution.py:215
  61.6 35.6 %collective-permute-start.14 = (bf16[2,4,128,512]{3,2,1,0:T(8,128)(2,1)S(1)}, bf16[2,4,128,512]{3,2,1,0:T(8,128)(2,1)S(1)}, u32[]{:S(2)}, u32[]{:S(2)}) collective-permute-start(bf16[2,4,128,512]{3,2,1,0:T(8,128)(2,1)S(1)} %pad_maximum_fusion.3.refs_4_), channel_id=1, source_target_pairs={{0,2},{2,0},{4,6},{6,4},{8,10},{10,8},{12,14},{14,12},{16,18},{18,... | collective-permute-start | bytes 3145736 | tf_op jit(solution)/shard_map/ppermute | solution.py:209
  61.6 21.0 %collective-permute-start.3 = (f32[4,12,128]{2,1,0:T(8,128)S(1)}, f32[4,12,128]{2,1,0:T(8,128)S(1)}, u32[]{:S(2)}, u32[]{:S(2)}) collective-permute-start(f32[4,12,128]{2,1,0:T(8,128)S(1)} %get-tuple-element.81), channel_id=1, source_target_pairs={{0,4},{2,6},{4,0},{6,2},{8,12},{10,14},{12,8},{14,10},{16,20},{18,... | collective-permute-start | bytes 73736 | tf_op jit(solution)/shard_map/ppermute | solution.py:212
  82.6 11.3 %collective-permute-start.32 = (bf16[4,128,512]{2,1,0:T(8,128)(2,1)S(1)}, bf16[4,128,512]{2,1,0:T(8,128)(2,1)S(1)}, u32[]{:S(2)}, u32[]{:S(2)}) collective-permute-start(bf16[4,128,512]{2,1,0:T(8,128)(2,1)S(1)} %get-tuple-element.49), channel_id=1, source_target_pairs={{0,4},{2,6},{4,0},{6,2},{8,12},{10,14},{12,8},{14,10},{16,20},{18,... | collective-permute-start | bytes 1572872 | tf_op jit(solution)/shard_map/ppermute | solution.py:212
  86.7 7.4 %collective-permute-start.4 = (f32[4,2,12,128]{3,2,0,1:T(8,128)S(1)}, f32[4,2,12,128]{3,2,0,1:T(8,128)S(1)}, u32[]{:S(2)}, u32[]{:S(2)}) collective-permute-start(f32[4,2,12,128]{3,2,0,1:T(8,128)S(1)} %pad_maximum_fusion.15), channel_id=1, source_target_pairs={{0,2},{2,0},{4,6},{6,4},{8,10},{10,8},{12,14},{14,12},{16,18},{18,... | collective-permute-start | bytes 147464 | tf_op jit(solution)/shard_map/ppermute | solution.py:209
  93.9 14.1 %collective-permute-start.10 = (bf16[2,4,128,512]{3,2,1,0:T(8,128)(2,1)}, bf16[2,4,128,512]{3,2,1,0:T(8,128)(2,1)}, u32[]{:S(2)}, u32[]{:S(2)}) collective-permute-start(bf16[2,4,128,512]{3,2,1,0:T(8,128)(2,1)} %pad_maximum_fusion.2.refs_0_), channel_id=1, source_target_pairs={{0,2},{2,0},{4,6},{6,4},{8,10},{10,8},{12,14},{14,12},{16,18},{18,... | collective-permute-start | bytes 3145736 | tf_op jit(solution)/shard_map/ppermute | solution.py:209
  94.1 25.6 %collective-permute-start.29 = (bf16[2,4,128,512]{3,2,1,0:T(8,128)(2,1)S(1)}, bf16[2,4,128,512]{3,2,1,0:T(8,128)(2,1)S(1)}, u32[]{:S(2)}, u32[]{:S(2)}) collective-permute-start(bf16[2,4,128,512]{3,2,1,0:T(8,128)(2,1)S(1)} %pad_maximum_fusion.4.refs_0_), channel_id=1, source_target_pairs={{0,4},{2,6},{4,0},{6,2},{8,12},{10,14},{12,8},{14,10},{16,20},{18,... | collective-permute-start | bytes 3145736 | tf_op jit(solution)/shard_map/ppermute | solution.py:212
  95.6 25.4 %collective-permute-start.33 = (bf16[2,4,128,512]{3,2,1,0:T(8,128)(2,1)S(1)}, bf16[2,4,128,512]{3,2,1,0:T(8,128)(2,1)}, u32[]{:S(2)}, u32[]{:S(2)}) collective-permute-start(bf16[2,4,128,512]{3,2,1,0:T(8,128)(2,1)S(1)} %pad_maximum_fusion.5.refs_4_), channel_id=1, source_target_pairs={{0,1},{1,0},{2,3},{3,2},{4,5},{5,4},{6,7},{7,6},{8,9},{9,8},{10,11... | collective-permute-start | bytes 3145736 | tf_op jit(solution)/shard_map/ppermute | solution.py:215
  97.1 23.9 %collective-permute-start.15 = (bf16[2,4,128,512]{3,2,1,0:T(8,128)(2,1)}, bf16[2,4,128,512]{3,2,1,0:T(8,128)(2,1)}, u32[]{:S(2)}, u32[]{:S(2)}) collective-permute-start(bf16[2,4,128,512]{3,2,1,0:T(8,128)(2,1)} %collective-permute-done.13.refs_5_), channel_id=1, source_target_pairs={{0,2},{2,0},{4,6},{6,4},{8,10},{10,8},{12,14},{14,12},{16,18},{18,... | collective-permute-start | bytes 3145736 | tf_op jit(solution)/shard_map/ppermute | solution.py:209
  98.1 23.6 %collective-permute-start.11 = (bf16[2,4,128,512]{3,2,1,0:T(8,128)(2,1)}, bf16[2,4,128,512]{3,2,1,0:T(8,128)(2,1)}, u32[]{:S(2)}, u32[]{:S(2)}) collective-permute-start(bf16[2,4,128,512]{3,2,1,0:T(8,128)(2,1)} %collective-permute-done.9.refs_1_), channel_id=1, source_target_pairs={{0,2},{2,0},{4,6},{6,4},{8,10},{10,8},{12,14},{14,12},{16,18},{18,... | collective-permute-start | bytes 3145736 | tf_op jit(solution)/shard_map/ppermute | solution.py:209
  108.0 43.2 %collective-permute-start.30 = (bf16[2,4,128,512]{3,2,1,0:T(8,128)(2,1)S(1)}, bf16[2,4,128,512]{3,2,1,0:T(8,128)(2,1)S(1)}, u32[]{:S(2)}, u32[]{:S(2)}) collective-permute-start(bf16[2,4,128,512]{3,2,1,0:T(8,128)(2,1)S(1)} %pad_maximum_fusion.4.refs_0_), channel_id=1, source_target_pairs={{0,2},{2,0},{4,6},{6,4},{8,10},{10,8},{12,14},{14,12},{16,18},{18,... | collective-permute-start | bytes 3145736 | tf_op jit(solution)/shard_map/ppermute | solution.py:209
  119.7 32.0 %collective-permute-start.34 = (bf16[2,4,128,512]{3,2,1,0:T(8,128)(2,1)S(1)}, bf16[2,4,128,512]{3,2,1,0:T(8,128)(2,1)S(1)}, u32[]{:S(2)}, u32[]{:S(2)}) collective-permute-start(bf16[2,4,128,512]{3,2,1,0:T(8,128)(2,1)S(1)} %pad_maximum_fusion.5.refs_4_), channel_id=1, source_target_pairs={{0,2},{2,0},{4,6},{6,4},{8,10},{10,8},{12,14},{14,12},{16,18},{18,... | collective-permute-start | bytes 3145736 | tf_op jit(solution)/shard_map/ppermute | solution.py:209
  121.0 30.7 %collective-permute-start.31 = (bf16[2,4,128,512]{3,2,1,0:T(8,128)(2,1)S(1)}, bf16[2,4,128,512]{3,2,1,0:T(8,128)(2,1)S(1)}, u32[]{:S(2)}, u32[]{:S(2)}) collective-permute-start(bf16[2,4,128,512]{3,2,1,0:T(8,128)(2,1)S(1)} %collective-permute-done.29.refs_1_), channel_id=1, source_target_pairs={{0,2},{2,0},{4,6},{6,4},{8,10},{10,8},{12,14},{14,12},{16,18},{18,... | collective-permute-start | bytes 3145736 | tf_op jit(solution)/shard_map/ppermute | solution.py:209
  121.0 30.7 %collective-permute-start.35 = (bf16[2,4,128,512]{3,2,1,0:T(8,128)(2,1)}, bf16[2,4,128,512]{3,2,1,0:T(8,128)(2,1)S(1)}, u32[]{:S(2)}, u32[]{:S(2)}) collective-permute-start(bf16[2,4,128,512]{3,2,1,0:T(8,128)(2,1)} %collective-permute-done.33.refs_5_), channel_id=1, source_target_pairs={{0,2},{2,0},{4,6},{6,4},{8,10},{10,8},{12,14},{14,12},{16,18},{18,... | collective-permute-start | bytes 3145736 | tf_op jit(solution)/shard_map/ppermute | solution.py:209
  151.2 39.6 %collective-permute-start.19 = (bf16[2,2,4,128,512]{4,3,2,1,0:T(8,128)(2,1)}, bf16[2,2,4,128,512]{4,3,2,1,0:T(8,128)(2,1)}, u32[]{:S(2)}, u32[]{:S(2)}) collective-permute-start(bf16[2,2,4,128,512]{4,3,2,1,0:T(8,128)(2,1)} %get-tuple-element.27), channel_id=1, source_target_pairs={{0,2},{2,0},{4,6},{6,4},{8,10},{10,8},{12,14},{14,12},{16,18},{18,... | collective-permute-start | bytes 6291464 | tf_op jit(solution)/shard_map/ppermute | solution.py:209
  151.2 42.0 %collective-permute-start.16 = (bf16[2,2,4,128,512]{4,3,2,1,0:T(8,128)(2,1)}, bf16[2,2,4,128,512]{4,3,2,1,0:T(8,128)(2,1)}, u32[]{:S(2)}, u32[]{:S(2)}) collective-permute-start(bf16[2,2,4,128,512]{4,3,2,1,0:T(8,128)(2,1)} %get-tuple-element.25), channel_id=1, source_target_pairs={{0,2},{2,0},{4,6},{6,4},{8,10},{10,8},{12,14},{14,12},{16,18},{18,... | collective-permute-start | bytes 6291464 | tf_op jit(solution)/shard_map/ppermute | solution.py:209
  174.9 22.8 %collective-permute-start.39 = (bf16[2,2,4,128,512]{4,3,2,1,0:T(8,128)(2,1)}, bf16[2,2,4,128,512]{4,3,2,1,0:T(8,128)(2,1)}, u32[]{:S(2)}, u32[]{:S(2)}) collective-permute-start(bf16[2,2,4,128,512]{4,3,2,1,0:T(8,128)(2,1)} %get-tuple-element.36), channel_id=1, source_target_pairs={{0,2},{2,0},{4,6},{6,4},{8,10},{10,8},{12,14},{14,12},{16,18},{18,... | collective-permute-start | bytes 6291464 | tf_op jit(solution)/shard_map/ppermute | solution.py:209
  174.9 10.8 %collective-permute-start.45 = (f32[4,4,128]{2,1,0:T(4,128)S(1)}, f32[4,4,128]{2,1,0:T(4,128)S(1)}, u32[]{:S(2)}, u32[]{:S(2)}) collective-permute-start(f32[4,4,128]{2,1,0:T(4,128)S(1)} %get-tuple-element.37), channel_id=1, source_target_pairs={{0,1},{1,0},{2,3},{3,2},{4,5},{5,4},{6,7},{7,6},{8,9},{9,8},{10,11... | collective-permute-start | bytes 24584 | tf_op jit(solution)/shard_map/ppermute | solution.py:215
  176.5 25.2 %collective-permute-start.36 = (bf16[2,2,4,128,512]{4,3,2,1,0:T(8,128)(2,1)}, bf16[2,2,4,128,512]{4,3,2,1,0:T(8,128)(2,1)}, u32[]{:S(2)}, u32[]{:S(2)}) collective-permute-start(bf16[2,2,4,128,512]{4,3,2,1,0:T(8,128)(2,1)} %get-tuple-element.34), channel_id=1, source_target_pairs={{0,2},{2,0},{4,6},{6,4},{8,10},{10,8},{12,14},{14,12},{16,18},{18,... | collective-permute-start | bytes 6291464 | tf_op jit(solution)/shard_map/ppermute | solution.py:209
  186.8 24.6 %all-to-all-start = ((f32[16,1,128]{2,1,0:T(1,128)}), f32[16,1,128]{2,1,0:T(1,128)S(1)}, u32[]{:S(2)}, u32[]{:S(2)}) async-start(f32[16,1,128]{2,1,0:T(1,128)} %bitcast.63), calls=%async_computation | async-start | bytes 16384 | tf_op jit(solution)/shard_map/all_to_all | solution.py:338
  192.6 26.1 %collective-permute-start.20 = (bf16[2,4,128,512]{3,2,1,0:T(8,128)(2,1)S(1)}, bf16[2,4,128,512]{3,2,1,0:T(8,128)(2,1)}, u32[]{:S(2)}, u32[]{:S(2)}) collective-permute-start(bf16[2,4,128,512]{3,2,1,0:T(8,128)(2,1)S(1)} %fusion.7), channel_id=1, source_target_pairs={{0,1},{1,0},{2,3},{3,2},{4,5},{5,4},{6,7},{7,6},{8,9},{9,8},{10,11... | collective-permute-start | bytes 3145736 | tf_op jit(solution)/shard_map/ppermute | solution.py:215
  195.8 26.6 %collective-permute-start.17 = (bf16[2,4,128,512]{3,2,1,0:T(8,128)(2,1)}, bf16[2,4,128,512]{3,2,1,0:T(8,128)(2,1)}, u32[]{:S(2)}, u32[]{:S(2)}) collective-permute-start(bf16[2,4,128,512]{3,2,1,0:T(8,128)(2,1)} %fusion.6), channel_id=1, source_target_pairs={{0,4},{2,6},{4,0},{6,2},{8,12},{10,14},{12,8},{14,10},{16,20},{18,... | collective-permute-start | bytes 3145736 | tf_op jit(solution)/shard_map/ppermute | solution.py:212
  200.2 41.0 %collective-permute-start.40 = (bf16[2,4,128,512]{3,2,1,0:T(8,128)(2,1)}, bf16[2,4,128,512]{3,2,1,0:T(8,128)(2,1)}, u32[]{:S(2)}, u32[]{:S(2)}) collective-permute-start(bf16[2,4,128,512]{3,2,1,0:T(8,128)(2,1)} %fusion.9), channel_id=1, source_target_pairs={{0,1},{1,0},{2,3},{3,2},{4,5},{5,4},{6,7},{7,6},{8,9},{9,8},{10,11... | collective-permute-start | bytes 3145736 | tf_op jit(solution)/shard_map/ppermute | solution.py:215
  204.2 40.5 %collective-permute-start.37 = (bf16[2,4,128,512]{3,2,1,0:T(8,128)(2,1)}, bf16[2,4,128,512]{3,2,1,0:T(8,128)(2,1)}, u32[]{:S(2)}, u32[]{:S(2)}) collective-permute-start(bf16[2,4,128,512]{3,2,1,0:T(8,128)(2,1)} %fusion.8), channel_id=1, source_target_pairs={{0,4},{2,6},{4,0},{6,2},{8,12},{10,14},{12,8},{14,10},{16,20},{18,... | collective-permute-start | bytes 3145736 | tf_op jit(solution)/shard_map/ppermute | solution.py:212
  212.1 29.2 %copy-start.10 = (bf16[2,2,4,128,512]{4,3,2,1,0:T(8,128)(2,1)S(1)}, bf16[2,2,4,128,512]{4,3,2,1,0:T(8,128)(2,1)}, u32[]{:S(2)}) copy-start(bf16[2,2,4,128,512]{4,3,2,1,0:T(8,128)(2,1)} %copy-done.8) | copy-start | bytes 6291460
  220.3 35.3 %collective-permute-start.21 = (bf16[4,128,512]{2,1,0:T(8,128)(2,1)S(1)}, bf16[4,128,512]{2,1,0:T(8,128)(2,1)S(1)}, u32[]{:S(2)}, u32[]{:S(2)}) collective-permute-start(bf16[4,128,512]{2,1,0:T(8,128)(2,1)S(1)} %fusion.16), channel_id=1, source_target_pairs={{0,4},{2,6},{4,0},{6,2},{8,12},{10,14},{12,8},{14,10},{16,20},{18,... | collective-permute-start | bytes 1572872 | tf_op jit(solution)/shard_map/ppermute | solution.py:212
  223.8 33.5 %collective-permute-start.18 = (bf16[4,128,512]{2,1,0:T(8,128)(2,1)S(1)}, bf16[4,128,512]{2,1,0:T(8,128)(2,1)S(1)}, u32[]{:S(2)}, u32[]{:S(2)}) collective-permute-start(bf16[4,128,512]{2,1,0:T(8,128)(2,1)S(1)} %fusion.19), channel_id=1, source_target_pairs={{0,1},{1,0},{2,3},{3,2},{4,5},{5,4},{6,7},{7,6},{8,9},{9,8},{10,11... | collective-permute-start | bytes 1572872 | tf_op jit(solution)/shard_map/ppermute | solution.py:215
  242.6 23.7 %collective-permute-start.41 = (bf16[4,128,512]{2,1,0:T(8,128)(2,1)S(1)}, bf16[4,128,512]{2,1,0:T(8,128)(2,1)S(1)}, u32[]{:S(2)}, u32[]{:S(2)}) collective-permute-start(bf16[4,128,512]{2,1,0:T(8,128)(2,1)S(1)} %fusion.10), channel_id=1, source_target_pairs={{0,4},{2,6},{4,0},{6,2},{8,12},{10,14},{12,8},{14,10},{16,20},{18,... | collective-permute-start | bytes 1572872 | tf_op jit(solution)/shard_map/ppermute | solution.py:212
  246.1 21.7 %collective-permute-start.38 = (bf16[4,128,512]{2,1,0:T(8,128)(2,1)S(1)}, bf16[4,128,512]{2,1,0:T(8,128)(2,1)S(1)}, u32[]{:S(2)}, u32[]{:S(2)}) collective-permute-start(bf16[4,128,512]{2,1,0:T(8,128)(2,1)S(1)} %fusion.13), channel_id=1, source_target_pairs={{0,1},{1,0},{2,3},{3,2},{4,5},{5,4},{6,7},{7,6},{8,9},{9,8},{10,11... | collective-permute-start | bytes 1572872 | tf_op jit(solution)/shard_map/ppermute | solution.py:215
  259.0 13.9 %collective-permute-start.22 = (bf16[2,128,512]{2,1,0:T(8,128)(2,1)S(1)}, bf16[2,128,512]{2,1,0:T(8,128)(2,1)S(1)}, u32[]{:S(2)}, u32[]{:S(2)}) collective-permute-start(bf16[2,128,512]{2,1,0:T(8,128)(2,1)S(1)} %get-tuple-element.45), channel_id=1, source_target_pairs={{0,24},{2,26},{4,28},{6,30},{8,0},{10,2},{12,4},{14,6},{16,8},{18,... | collective-permute-start | bytes 786440 | tf_op jit(solution)/shard_map/ppermute | solution.py:218
  262.8 34.8 %collective-permute-start.23 = (bf16[2,128,512]{2,1,0:T(8,128)(2,1)S(1)}, bf16[2,128,512]{2,1,0:T(8,128)(2,1)S(1)}, u32[]{:S(2)}, u32[]{:S(2)}) collective-permute-start(bf16[2,128,512]{2,1,0:T(8,128)(2,1)S(1)} %get-tuple-element.47), channel_id=1, source_target_pairs={{0,16},{2,18},{4,20},{6,22},{8,24},{10,26},{12,28},{14,30},{16,0},... | collective-permute-start | bytes 786440 | tf_op jit(solution)/shard_map/ppermute | solution.py:218
  262.8 34.8 %collective-permute-start.24 = (bf16[2,128,512]{2,1,0:T(8,128)(2,1)S(1)}, bf16[2,128,512]{2,1,0:T(8,128)(2,1)S(1)}, u32[]{:S(2)}, u32[]{:S(2)}) collective-permute-start(bf16[2,128,512]{2,1,0:T(8,128)(2,1)S(1)} %get-tuple-element.46), channel_id=1, source_target_pairs={{0,8},{2,10},{4,12},{6,14},{8,16},{10,18},{12,20},{14,22},{16,24},... | collective-permute-start | bytes 786440 | tf_op jit(solution)/shard_map/ppermute | solution.py:218
  269.5 29.0 %collective-permute-start.42 = (bf16[2,128,512]{2,1,0:T(8,128)(2,1)S(1)}, bf16[2,128,512]{2,1,0:T(8,128)(2,1)S(1)}, u32[]{:S(2)}, u32[]{:S(2)}) collective-permute-start(bf16[2,128,512]{2,1,0:T(8,128)(2,1)S(1)} %get-tuple-element.42), channel_id=1, source_target_pairs={{0,24},{2,26},{4,28},{6,30},{8,0},{10,2},{12,4},{14,6},{16,8},{18,... | collective-permute-start | bytes 786440 | tf_op jit(solution)/shard_map/ppermute | solution.py:218
  272.9 33.3 %collective-permute-start.43 = (bf16[2,128,512]{2,1,0:T(8,128)(2,1)S(1)}, bf16[2,128,512]{2,1,0:T(8,128)(2,1)S(1)}, u32[]{:S(2)}, u32[]{:S(2)}) collective-permute-start(bf16[2,128,512]{2,1,0:T(8,128)(2,1)S(1)} %get-tuple-element.44), channel_id=1, source_target_pairs={{0,16},{2,18},{4,20},{6,22},{8,24},{10,26},{12,28},{14,30},{16,0},... | collective-permute-start | bytes 786440 | tf_op jit(solution)/shard_map/ppermute | solution.py:218
  272.9 33.3 %collective-permute-start.44 = (bf16[2,128,512]{2,1,0:T(8,128)(2,1)S(1)}, bf16[2,128,512]{2,1,0:T(8,128)(2,1)S(1)}, u32[]{:S(2)}, u32[]{:S(2)}) collective-permute-start(bf16[2,128,512]{2,1,0:T(8,128)(2,1)S(1)} %get-tuple-element.43), channel_id=1, source_target_pairs={{0,8},{2,10},{4,12},{6,14},{8,16},{10,18},{12,20},{14,22},{16,24},... | collective-permute-start | bytes 786440 | tf_op jit(solution)/shard_map/ppermute | solution.py:218
  (19 other events, 127.9 us)

commit v3 on v2

--- a/solution.py
+++ b/solution.py
@@ -9,6 +9,7 @@
 
 F32 = jnp.float32
 BF16 = jnp.bfloat16
+MEBIBYTE = 1024 * 1024
 
 
 def slots_body(tokens, grad_out, gates, expert_ids, w_gate, w_up, w_down):
@@ -97,8 +98,8 @@
     return lax.dot_general(left, right, dims, preferred_element_type=F32)
 
 
-def after(value, *others):
-    return lax.optimization_barrier((value, *others))[0]
+def together(*values):
+    return lax.optimization_barrier(values)
 
 
 def picks(pos, place, capacity):
@@ -107,19 +108,25 @@
     return row == slot
 
 
+def column_of(side, far, start, features, half):
+    return pl.multiple_of((side ^ far) * (features // 2) + start, half)
+
+
 def gather_rows(side, pos, pieces, rows, capacity):
     half = pieces[0].shape[-1]
+    features = rows.shape[1]
     for core in range(2):
         for pair in range(2):
             place = 2 * core + pair
             pick = picks(pos, place, capacity).astype(BF16)
             at = pl.ds(place * capacity, capacity)
             for far in range(2):
-                column = pl.multiple_of((side ^ far) * 2 * half, half)
-                a = pieces[2 * core + pair][far, 0]
-                b = pieces[4 + 2 * core + far][pair, 0]
-                rows[at, pl.ds(column, half)] = dot(pick, a).astype(BF16)
-                rows[at, pl.ds(column + half, half)] = dot(pick, b).astype(BF16)
+                for chunk in range(len(pieces) // 8):
+                    column = column_of(side, far, 2 * chunk * half, features, half)
+                    a = pieces[8 * chunk + 2 * core + pair][far, 0]
+                    b = pieces[8 * chunk + 4 + 2 * core + far][pair, 0]
+                    rows[at, pl.ds(column, half)] = dot(pick, a).astype(BF16)
+                    rows[at, pl.ds(column + half, half)] = dot(pick, b).astype(BF16)
 
 
 def gate_rows(pos, gate, capacity):
@@ -132,39 +139,40 @@
 
 def scatter_rows(side, pos, values, outs, capacity):
     half = outs[0].shape[-1]
+    features = values.shape[1]
     for core in range(2):
         for pair in range(2):
             place = 2 * core + pair
             pick = picks(pos, place, capacity).astype(BF16)
             at = pl.ds(place * capacity, capacity)
             for far in range(2):
-                column = pl.multiple_of((side ^ far) * 2 * half, half)
+                column = column_of(side, far, 0, features, half)
                 a = dot(pick, values[at, pl.ds(column, half)], FIRST)
-                outs[core][pair, far, 0] = a.astype(BF16)
+                outs[core][0, pair, far, 0] = a.astype(BF16)
                 b = dot(pick, values[at, pl.ds(column + half, half)], FIRST)
-                outs[2 + core][far, pair, 0] = b.astype(BF16)
+                outs[core][1, far, pair, 0] = b.astype(BF16)
 
 
 def up_kernel(capacity, side, pos, gate, *refs):
-    pieces, (weight_gate, weight_up, rows, gate_pre, up_pre, scaled) = refs[:8], refs[8:]
+    pieces, (weight_gate, weight_up, rows, gate_pre, up_pre, scaled) = refs[:-6], refs[-6:]
     gather_rows(side[0], pos, pieces, rows, capacity)
     gates = gate_rows(pos, gate, capacity)
     got = rows[...]
-    pre = dot(got, weight_gate[...])
-    up = dot(got, weight_up[...])
+    pre = dot(got, weight_gate[...], LAST)
+    up = dot(got, weight_up[...], LAST)
     gate_pre[...] = pre
     up_pre[...] = up
     scaled[...] = (gates * (pre * jax.nn.sigmoid(pre) * up)).astype(BF16)
 
 
 def mix_kernel(capacity, side, pos, scaled, weight_down, *refs):
-    outs, values = refs[:4], refs[4]
+    outs, values = refs[:-1], refs[-1]
     values[...] = dot(scaled[...], weight_down[...]).astype(BF16)
     scatter_rows(side[0], pos, values, outs, capacity)
 
 
 def back_kernel(capacity, side, pos, gate, *refs):
-    pieces, (weight_down, gate_pre, up_pre, rows, grad_gate_pre, grad_up_pre, sums) = refs[:8], refs[8:]
+    pieces, (weight_down, gate_pre, up_pre, rows, grad_gate_pre, grad_up_pre, sums) = refs[:-7], refs[-7:]
     gather_rows(side[0], pos, pieces, rows, capacity)
     gates = gate_rows(pos, gate, capacity)
     plain = dot(rows[...], weight_down[...], LAST)
@@ -181,11 +189,26 @@
         sums[0, place : place + 1, :] = jnp.sum(jnp.where(pick, own, 0.0), axis=0, keepdims=True)
 
 
-def input_kernel(capacity, side, pos, grad_gate_pre, grad_up_pre, weight_gate, weight_up, *refs):
-    outs, values = refs[:4], refs[4]
-    terms = dot(grad_gate_pre[...], weight_gate[...], LAST)
-    values[...] = (terms + dot(grad_up_pre[...], weight_up[...], LAST)).astype(BF16)
+def input_kernel(capacity, side, pos, grad_gate_pre, grad_up_pre, *refs):
+    weights, outs, values = refs[:4], refs[4:-1], refs[-1]
+    span = weights[0].shape[1]
+    for at in range(2):
+        terms = dot(grad_gate_pre[...], weights[at][...])
+        terms = terms + dot(grad_up_pre[...], weights[2 + at][...])
+        values[:, at * span : (at + 1) * span] = terms.astype(BF16)
     scatter_rows(side[0], pos, values, outs, capacity)
+
+
+def weight_kernel(pairs, *refs):
+    lefts, rows, outs, turned = refs[:pairs], refs[pairs], refs[pairs + 1 : 2 * pairs + 1], refs[2 * pairs + 1 :]
+
+    @pl.when(pl.program_id(0) == 0)
+    def _():
+        for left, flat in zip(lefts, turned):
+            flat[...] = left[...].T
+
+    for flat, out in zip(turned, outs):
+        out[...] = dot(flat[...], rows[...]).astype(BF16)
 
 
 def gather_body(tokens, grad_out, gates, expert_ids, w_gate, w_up, w_down):
@@ -219,51 +242,89 @@
             value, "expert", [(e, (e + 4 * step) % expert_count) for e in range(expert_count)]
         )
 
-    def spread(rows, start):
-        own = after(jnp.stack([rows[:, :half], rows[:, half:]]), *start)
-        parts = [own] + [shift(own, step) for step in range(1, column)]
-        a = jnp.stack([part[0] for part in parts])
-        b = jnp.stack([part[1] for part in parts])
-        a = jnp.stack([a, swap_side(a)])
-        b = jnp.stack([b, swap_pair(b)])
-        far_a = swap_pair(a)
-        far_b = swap_side(b)
-        pieces = (a, far_a, swap_core(a), swap_core(far_a), b, far_b, swap_core(b), swap_core(far_b))
-        return pieces, parts
-
-    def spread_routing():
-        own = jnp.concatenate([expert_ids.astype(F32), gates], axis=1).T
-        all_parts = jnp.stack([own] + [shift(own, step) for step in range(1, column)])
-        all_parts = jnp.stack([all_parts, swap_pair(all_parts)], axis=1)
-        all_parts = jnp.concatenate([all_parts, swap_core(all_parts)], axis=1)
-        named = all_parts[:, :, :top_count] == me.astype(F32)
-        gate = jnp.sum(jnp.where(named, all_parts[:, :, top_count:], 0.0), axis=2)
+    def routing_rows(width):
+        high = lax.reduce_precision(gates, 8, 7)
+        middle = lax.reduce_precision(gates - high, 8, 7)
+        low = gates - high - middle
+        values = jnp.concatenate([expert_ids.astype(F32), high, middle, low], axis=1).T.astype(BF16)
+        rows = -(-values.size // (8 * width)) * 8
+        return jnp.pad(values.reshape(-1), (0, rows * width - values.size)).reshape(rows, width)
+
+    def column_parts(own):
+        return [own] + [shift(own, step) for step in range(1, column)]
+
+    def halves(rows):
+        size = rows.shape[1] // 2
+        return jnp.stack([rows[:, :size], rows[:, size:]])
+
+    def halves_of(parts):
+        return [jnp.stack([part[at] for part in parts]) for at in range(2)]
+
+    def across(a, b):
+        return swap_side(a), swap_pair(b)
+
+    def over(a, b):
+        return swap_pair(a), swap_side(b)
+
+    def cores(values):
+        return tuple(swap_core(value) for value in values)
+
+    def stacks(near, far):
+        return tuple(jnp.stack(both) for both in zip(near, far))
+
+    def routing_tables(parts):
+        size = 4 * top_count * tok_count
+        parts = parts.reshape(4, column, -1)[:, :, :size].reshape(4, column, 4, top_count, tok_count)
+        parts = parts.swapaxes(0, 1).astype(F32)
+        named = parts[:, :, 0] == me.astype(F32)
+        of_all = parts[:, :, 1] + parts[:, :, 2] + parts[:, :, 3]
+        gate = jnp.sum(jnp.where(named, of_all, 0.0), axis=2)
         member = jnp.any(named, axis=2)
         upto = jnp.triu(jnp.ones((tok_count, tok_count), BF16))
         count = jnp.dot(member.astype(BF16), upto, preferred_element_type=F32)
         return jnp.where(member, count - 1.0, -1.0), gate
 
+    def sums_of_experts(token_sums):
+        block = jnp.arange(expert_count)
+        place = (me // 4 - block // 4) % column * 4 + ((me ^ block) % 2) * 2 + ((me ^ block) // 2) % 2
+        token_sums = token_sums.reshape(expert_count, tok_count)[place]
+        return lax.all_to_all(token_sums, "expert", split_axis=0, concat_axis=0, tiled=True)
+
     def add(*terms):
         return sum(term.astype(F32) for term in terms)
 
-    def collect(outs):
-        own_a, other_a, own_b, other_b = outs
-        core_a, core_b = swap_core(other_a), swap_core(other_b)
-        first_a = swap_pair(add(own_a[1], core_a[1]).astype(BF16))
-        first_b = swap_side(add(own_b[1], core_b[1]).astype(BF16))
-        second_a = swap_side(add(own_a[0, 1], core_a[0, 1], first_a[1]).astype(BF16))
-        second_b = swap_pair(add(own_b[0, 1], core_b[0, 1], first_b[1]).astype(BF16))
-        a = add(own_a[0, 0], core_a[0, 0], first_a[0], second_a)
-        b = add(own_b[0, 0], core_b[0, 0], first_b[0], second_b)
-        both = jnp.stack([a, b], axis=1)
-        total = both[0]
-        for step in range(1, column):
-            total = total + shift(both[step].astype(BF16), column - step).astype(F32)
+    def sent_first(own, core):
+        return add(own[0, 1], core[0, 1]).astype(BF16), add(own[1, 1], core[1, 1]).astype(BF16)
+
+    def sent_second(own, core, first):
+        a = add(own[0, 0, 1], core[0, 0, 1], first[0][1]).astype(BF16)
+        return a, add(own[1, 0, 1], core[1, 0, 1], first[1][1]).astype(BF16)
+
+    def sent_column(own, core, first, second):
+        a = add(own[0, 0, 0], core[0, 0, 0], first[0][0], second[0])
+        b = add(own[1, 0, 0], core[1, 0, 0], first[1][0], second[1])
+        return jnp.stack([a, b], axis=1)
+
+    def from_column(both):
+        return [shift(both[step].astype(BF16), column - step) for step in range(1, column)]
+
+    def column_sum(own, received):
+        total = add(own, *received)
         return jnp.concatenate([total[0], total[1]], axis=1).astype(BF16)
 
+    small = pl.CostEstimate(flops=1 << 20, bytes_accessed=1 << 16, transcendentals=0)
     table = pl.BlockSpec((1, 4, tok_count), lambda i, s: (i, 0, 0))
-    piece = pl.BlockSpec((2, 1, tok_count, half), lambda i, s: (0, i, 0, 0))
-    out_piece = pl.BlockSpec((2, 2, 1, tok_count, half), lambda i, s: (0, 0, i, 0, 0))
+
+    def piece_of(piece, chunk=None):
+        block = (2, 1, *piece.shape[-2:])
+        if chunk is None:
+            return pl.BlockSpec(block, lambda i, s: (0, i, 0, 0))
+        return pl.BlockSpec((None, *block), lambda i, s: (chunk, 0, i, 0, 0))
+
+    def sums_out(columns):
+        block = (2, 2, 2, 1, tok_count, columns)
+        spec = pl.BlockSpec(block, lambda i, s: (0, 0, 0, i, 0, 0))
+        return [(shaped((2, 2, 2, column, tok_count, columns), BF16), spec)] * 2
 
     def rows_of(size):
         return pl.BlockSpec((step_rows, size), lambda i, s: (i, 0))
@@ -271,7 +332,7 @@
     def whole(*shape):
         return pl.BlockSpec(shape, lambda i, s: (0, 0), pipeline_mode=pl.Buffered(1))
 
-    def kernel(run, macs, in_specs, outs, scratch=()):
+    def kernel(run, in_specs, outs, scratch=(), mebibytes=26):
         return pl.pallas_call(
             functools.partial(run, capacity),
             out_shape=[shape for shape, _ in outs],
@@ -282,11 +343,25 @@
                 out_specs=[spec for _, spec in outs],
                 scratch_shapes=scratch,
             ),
-            compiler_params=pltpu.CompilerParams(vmem_limit_bytes=40 * 1024 * 1024),
-            cost_estimate=pl.CostEstimate(
-                flops=2 * macs, bytes_accessed=16 * 1024 * 1024, transcendentals=0
-            ),
+            compiler_params=pltpu.CompilerParams(vmem_limit_bytes=mebibytes * MEBIBYTE),
+            cost_estimate=small,
         )
+
+    def weight_grads(rows, *lefts):
+        span = features // 4
+        held = pl.BlockSpec((slots, hidden), lambda i: (0, 0), pipeline_mode=pl.Buffered(1))
+        columns = pl.BlockSpec((slots, span), lambda i: (0, i))
+        result = pl.BlockSpec((hidden, span), lambda i: (0, i))
+        return pl.pallas_call(
+            functools.partial(weight_kernel, len(lefts)),
+            out_shape=[shaped((hidden, features), BF16)] * len(lefts),
+            grid=(features // span,),
+            in_specs=[held] * len(lefts) + [columns],
+            out_specs=[result] * len(lefts),
+            scratch_shapes=[pltpu.VMEM((hidden, slots), BF16)] * len(lefts),
+            compiler_params=pltpu.CompilerParams(vmem_limit_bytes=26 * MEBIBYTE),
+            cost_estimate=small,
+        )(*lefts, rows)
 
     def shaped(shape, dtype):
         return jax.ShapeDtypeStruct(shape, dtype)
@@ -294,54 +369,150 @@
     row_out = (shaped((slots, features), BF16), rows_of(features))
     hidden_f32 = (shaped((slots, hidden), F32), rows_of(hidden))
     hidden_bf = (shaped((slots, hidden), BF16), rows_of(hidden))
-    piece_outs = [(shaped((2, 2, column, tok_count, half), BF16), out_piece)] * 4
-    macs = slots * features * hidden
     values = [pltpu.VMEM((step_rows, features), BF16)]
 
-    weight_gate, weight_up, weight_down = w_gate[0], w_up[0], w_down[0]
-    wide = whole(features, hidden)
-    tall = whole(hidden, features)
-
-    token_pieces, token_parts = spread(tokens, ())
-    pos, gate = spread_routing()
-    grad_pieces, _ = spread(grad_out, token_parts)
-
+    weight_gate, weight_up, weight_down = w_gate[0].T, w_up[0].T, w_down[0]
+    weight = whole(hidden, features)
+
+    token_rows = jnp.concatenate([tokens[:, :half], tokens[:, half:], routing_rows(half)])
+    own_1, own_2 = halves(grad_out[:, :half]), halves(grad_out[:, half:])
+    with jax.named_scope("column_tokens"):
+        token_parts = column_parts(token_rows)
+        token_parts, own_1, own_2 = together(token_parts, own_1, own_2)
+        near_a = jnp.stack([part[:tok_count] for part in token_parts])
+        near_b = jnp.stack([part[tok_count:] for part in token_parts])
+    with jax.named_scope("across_tokens"):
+        far_a, far_b = across(near_a, near_b)
+        parts_1 = column_parts(own_1)
+        far_a, far_b, parts_1, own_2 = together(far_a, far_b, parts_1, own_2)
+        near_a = jnp.stack([near_a, far_a])
+        routing = jnp.stack([near_b[:, tok_count:], far_b[:, tok_count:]])
+        near_b = jnp.stack([near_b[:, :tok_count], far_b[:, :tok_count]])
+    with jax.named_scope("over_tokens"):
+        far_a, far_b = over(near_a, near_b)
+        core_a, core_b = cores((near_a, near_b))
+        parts_2 = column_parts(own_2)
+        far_a, far_b, core_a, core_b, parts_2, core_routing = together(
+            far_a, far_b, core_a, core_b, parts_2, swap_core(routing)
+        )
+        pos, gate = routing_tables(jnp.stack([routing, core_routing]))
+    with jax.named_scope("across_grads"):
+        far_core_a, far_core_b = cores((far_a, far_b))
+        grads_1, grads_2 = halves_of(parts_1), halves_of(parts_2)
+        grads_a, grads_b = jnp.stack([grads_1[0], grads_2[0]]), jnp.stack([grads_1[1], grads_2[1]])
+        far_grads = across(grads_a, grads_b)
+        far_core_a, far_core_b, pos, gate = together(far_core_a, far_core_b, pos, gate)
+    pieces = (near_a, far_a, core_a, far_core_a, near_b, far_b, core_b, far_core_b)
     rows, gate_pre, up_pre, scaled = kernel(
         up_kernel,
-        2 * macs,
-        [table, table] + [piece] * 8 + [wide, wide],
+        [table, table] + [piece_of(piece) for piece in pieces] + [weight, weight],
         [row_out, hidden_f32, hidden_f32, hidden_bf],
-    )(side, pos, gate, *token_pieces, weight_gate, weight_up)
-    mix_out = kernel(
-        mix_kernel, macs, [table, rows_of(hidden), tall], piece_outs, values
-    )(side, pos, scaled, weight_down)
-    mixed = collect(mix_out)
+        mebibytes=58,
+    )(side, pos, gate, *pieces, weight_gate, weight_up)
+    far_grads, scaled = together(far_grads, scaled)
+    near_a = jnp.stack([grads_a, far_grads[0]], axis=1)
+    near_b = jnp.stack([grads_b, far_grads[1]], axis=1)
+    with jax.named_scope("over_grads_1"):
+        far_1 = over(near_a[0], near_b[0])
+        core_a, core_b = cores((near_a, near_b))
+    mix_own, mix_other = kernel(mix_kernel, [table, rows_of(hidden), weight], sums_out(half), values)(
+        side, pos, scaled, weight_down
+    )
+    far_1, core_a, core_b, near_a, near_b, mix_other = together(
+        far_1, core_a, core_b, near_a, near_b, mix_other
+    )
+    with jax.named_scope("over_grads_2"):
+        far_2 = over(near_a[1], near_b[1])
+    with jax.named_scope("cores_mixed"):
+        mix_core = swap_core(mix_other)
+        mix_send = sent_first(mix_own, mix_core)
+        far_core_1 = cores(far_1)
+    far_core_1, mix_send = together(far_core_1, mix_send)
+    with jax.named_scope("over_mixed"):
+        mix_first = over(*mix_send)
+    far_2, mix_send = together(far_2, mix_send)
+    with jax.named_scope("cores_grads"):
+        far_core_2 = cores(far_2)
+    pieces = [
+        piece
+        for chunk, far, far_core in ((0, far_1, far_core_1), (1, far_2, far_core_2))
+        for at, near, core in ((0, near_a, core_a), (1, near_b, core_b))
+        for piece in ((near, chunk), (far[at], None), (core, chunk), (far_core[at], None))
+    ]
     grad_rows, grad_gate_pre, grad_up_pre, token_sums = kernel(
         back_kernel,
-        macs,
-        [table, table] + [piece] * 8 + [tall, rows_of(hidden), rows_of(hidden)],
+        [table, table] + [piece_of(*piece) for piece in pieces] + [weight, rows_of(hidden), rows_of(hidden)],
         [row_out, hidden_bf, hidden_bf, (shaped((column, 4, tok_count), F32), table)],
-    )(side, pos, gate, *grad_pieces, weight_down, gate_pre, up_pre)
-    input_out = kernel(
-        input_kernel,
-        2 * macs,
-        [table, rows_of(hidden), rows_of(hidden), wide, wide],
-        piece_outs,
-        values,
-    )(side, pos, grad_gate_pre, grad_up_pre, weight_gate, weight_up)
-    grad_tokens = collect(input_out)
-
-    token_sums = token_sums + swap_side(token_sums)
-    block = jnp.arange(expert_count)
-    place = (me // 4 - block // 4) % column * 4 + ((me ^ block) % 2) * 2 + ((me ^ block) // 2) % 2
-    token_sums = token_sums.reshape(expert_count, tok_count)[place]
-    expert_sums = lax.all_to_all(token_sums, "expert", split_axis=0, concat_axis=0, tiled=True)
+    )(side, pos, gate, *(piece for piece, _ in pieces), weight_down, gate_pre, up_pre)
+
+    def input_terms(chunk, *hidden_grads):
+        columns = [
+            pl.BlockSpec((hidden, half), lambda i, s, at=at: (0, 2 * at + chunk), pipeline_mode=pl.Buffered(1))
+            for at in range(2)
+        ]
+        return kernel(
+            input_kernel,
+            [table, rows_of(hidden), rows_of(hidden)] + columns * 2,
+            sums_out(half // 2),
+            [pltpu.VMEM((step_rows, width), BF16)],
+        )(side, pos, *hidden_grads, weight_gate, weight_gate, weight_up, weight_up)
+
+    own_1, other_1 = input_terms(0, grad_gate_pre, grad_up_pre)
+    own_2, other_2 = input_terms(1, grad_gate_pre, grad_up_pre)
+    mix_first, other_1, other_2, token_sums = together(mix_first, other_1, other_2, token_sums)
+    with jax.named_scope("across_mixed"):
+        mix_send = sent_second(mix_own, mix_core, mix_first)
+        mix_second = across(*mix_send)
+    with jax.named_scope("cores_inputs"):
+        core_1, core_2 = cores((other_1, other_2))
+    with jax.named_scope("gates"):
+        token_sums = token_sums + swap_side(token_sums)
+    send_1, send_2 = sent_first(own_1, core_1), sent_first(own_2, core_2)
+    scaled, mix_send = together(scaled, mix_send)
+    (grad_down,) = weight_grads(grad_rows, scaled)
+    mix_second, send_1, send_2, token_sums, grad_down = together(
+        mix_second, send_1, send_2, token_sums, grad_down
+    )
+    with jax.named_scope("over_inputs_1"):
+        first_1 = over(*send_1)
+    with jax.named_scope("column_mixed"):
+        mix_both = sent_column(mix_own, mix_core, mix_first, mix_second)
+        mix_received = from_column(mix_both)
+    first_1, mix_both = together(first_1, mix_both)
+    with jax.named_scope("inputs_1_and_2"):
+        send_1 = sent_second(own_1, core_1, first_1)
+        to_side = jnp.concatenate([send_1[0][None], send_2[1]])
+        to_pair = jnp.concatenate([send_1[1][None], send_2[0]])
+        from_side, from_pair = swap_side(to_side), swap_pair(to_pair)
+    token_sums, grad_gate_pre, to_side, to_pair = together(token_sums, grad_gate_pre, to_side, to_pair)
+    grad_gate, grad_up = weight_grads(rows, grad_gate_pre, grad_up_pre)
+    with jax.named_scope("gates"):
+        expert_sums = sums_of_experts(token_sums)
+    from_side, from_pair, mix_received, grad_gate, grad_up = together(
+        from_side, from_pair, mix_received, grad_gate, grad_up
+    )
+    second_1, first_2 = (from_side[0], from_pair[0]), (from_pair[1:], from_side[1:])
+    with jax.named_scope("across_inputs_2"):
+        send_2 = sent_second(own_2, core_2, first_2)
+        second_2 = across(*send_2)
+    second_1, send_2 = together(second_1, send_2)
+    with jax.named_scope("column_inputs_1"):
+        both_1 = sent_column(own_1, core_1, first_1, second_1)
+        received_1 = from_column(both_1)
+    mix_received, both_1 = together(mix_received, both_1)
+    mixed = column_sum(mix_both[0], mix_received)
+    second_2, mixed, expert_sums = together(second_2, mixed, expert_sums)
+    with jax.named_scope("column_inputs_2"):
+        both_2 = sent_column(own_2, core_2, first_2, second_2)
+        received_2 = from_column(both_2)
+    both_1, both_2 = together(both_1, both_2)
+    grad_tokens_1 = column_sum(both_1[0], received_1)
+    grad_tokens = jnp.concatenate([grad_tokens_1, column_sum(both_2[0], received_2)], axis=1)
+
     chosen = expert_ids[None] == jnp.arange(expert_count, dtype=jnp.int32)[:, None, None]
     grad_gates = jnp.sum(jnp.where(chosen, expert_sums[:, :, None], 0.0), axis=0)
 
-    grad_down = dot(scaled, grad_rows, FIRST).astype(BF16)[None]
-    grad_gate = dot(rows, grad_gate_pre, FIRST).astype(BF16)[None]
-    grad_up = dot(rows, grad_up_pre, FIRST).astype(BF16)[None]
+    grad_gate, grad_up, grad_down = grad_gate.T[None], grad_up.T[None], grad_down[None]
     return (mixed, grad_tokens, grad_gates, grad_gate, grad_up, grad_down)
 
 
@@ -350,7 +521,7 @@
     tok_count, top_count = expert_ids.shape
     slot_total = tok_count * top_count * 4 // (3 * expert_count) * expert_count
     gathers = expert_count * tok_count <= 2 * slot_total
-    shaped = lax.axis_size("tensor") == 2 and expert_count % 4 == 0
+    shaped = lax.axis_size("tensor") == 2 and expert_count % 4 == 0 and expert_count <= 256
     plan = gather_body if gathers and shaped else slots_body
     return plan(tokens, grad_out, gates, expert_ids, w_gate, w_up, w_down)
 

time: 308 us -> 241 us (0.78)
  waiting for transfers between devices: 131 us -> 88.6 us
  matrix products: 16.2 us -> 0.81 us
  Pallas kernels: 44.4 us -> 55.2 us
  local copies, waits for them, and re-layouts: 21.9 us -> 12 us
  other arithmetic: 27.1 us -> 19.5 us
    ppermute x9 -> x10, waiting for transfers between devices: 49.7 us -> 13.9 us  [swap_pair(): return lax.ppermute(value, 'expert', chip_pairs)]
    dot_general x4 -> x1, matrix products: 16.2 us -> 0.81 us  [routing_tables(): count = jnp.dot(member.astype(BF16), upto, preferred_element_type=F32)]
    ppermute x9 -> x11, waiting for transfers between devices: 26.8 us -> 11.4 us  [swap_side(): return lax.ppermute(value, 'tensor', [(0, 1), (1, 0)])]
    unnamed x42 -> x58, local copies, waits for them, and re-layouts: 18.4 us -> 5.54 us
    convert_element_type x9, other arithmetic: 15.9 us -> 4.54 us  [the longest x3 2.19 us: sent_second(): return (a, add(own[1, 0, 1], core[1, 0, 1], first[1][1]).astype(BF16))]
    pallas_call x4 -> x7, Pallas kernels: 44.4 us -> 55.2 us  [the longest x2 14.1 us: weight_grads(): pl.pallas_call(functools.partial(weight_kernel, len(lefts)), out_shape=[s...]
    ppermute x13 -> x14, waiting for transfers between devices: 0.03 us -> 8.94 us  [swap_core(): return lax.ppermute(value, 'expert', core_pairs)]
    ppermute x9 -> x10, starting transfers between devices: 13 us -> 10.8 us  [swap_pair(): return lax.ppermute(value, 'expert', chip_pairs)]
  transfers between devices with their start and end apart: 47 -> 54, of which waited for: 16 -> 23; matrix products, arithmetic and copies ran while one was open for 18% -> 9% of each run, Pallas kernels for 14% -> 23%
where the time goes in v3:
time: 241 us; the launch traced here: 240 us
  waiting for transfers between devices  88.6 us (37%)
  starting transfers between devices  62.5 us (26%)
  Pallas kernels  55.2 us (23%)
  other arithmetic  19.5 us (8%)
  local copies, waits for them, and re-layouts  12 us (5%)
    ppermute x18, waiting for transfers between devices, shift(): lax.ppermute(value, 'expert', [(e, (e + 4 * step) % expert_count) for e i...  54.4 us
    ppermute x18, starting transfers between devices, shift(): lax.ppermute(value, 'expert', [(e, (e + 4 * step) % expert_count) for e i...  32.7 us
    pallas_call x2, Pallas kernels, weight_grads(): pl.pallas_call(functools.partial(weight_kernel, len(lefts)), out_shape=[s...  14.1 us
    ppermute x10, waiting for transfers between devices, swap_pair(): return lax.ppermute(value, 'expert', chip_pairs)  13.9 us
    pallas_call x1, Pallas kernels, gather_body(): kernel(up_kernel, [table, table] + [piece_of(piece) for piece in pieces]...  13.7 us
    pallas_call x2, Pallas kernels, input_terms(): kernel(input_kernel, [table, rows_of(hidden), rows_of(hidden)] + columns...  12.2 us
    ppermute x11, waiting for transfers between devices, swap_side(): return lax.ppermute(value, 'tensor', [(0, 1), (1, 0)])  11.4 us
    ppermute x10, starting transfers between devices, swap_pair(): return lax.ppermute(value, 'expert', chip_pairs)  10.8 us
  transfers between devices with their start and end apart: 54, of which 23 were waited for; matrix products, arithmetic and copies ran while one was open for 9% of the time, Pallas kernels for 23%

profile of v3, /device:TPU:0, one launch (start us, length us, event | category | flops | bytes accessed | tf_op | source)
XLA Modules:
  0.0 240.1 jit_solution(1220098181665769427)
XLA Ops:
  3.1 3.1 %collective-permute-start = (bf16[264,512]{1,0:T(8,128)(2,1)S(1)}, bf16[264,512]{1,0:T(8,128)(2,1)S(1)}, u32[]{:S(2)}, u32[]{:S(2)}) collective-permute-start(bf16[264,512]{1,0:T(8,128)(2,1)S(1)} %pad_maximum_fusion.13), channel_id=1, source_target_pairs={{0,8},{2,10},{4,12},{6,14},{8,16},{10,18},{12,20},{14,22},{16,24},... | collective-permute-start | bytes 811016 | tf_op jit(solution)/shard_map/column_tokens/ppermute | solution.py:241
  6.2 2.6 %collective-permute-start.1 = (bf16[264,512]{1,0:T(8,128)(2,1)S(1)}, bf16[264,512]{1,0:T(8,128)(2,1)S(1)}, u32[]{:S(2)}, u32[]{:S(2)}) collective-permute-start(bf16[264,512]{1,0:T(8,128)(2,1)S(1)} %pad_maximum_fusion.13), channel_id=1, source_target_pairs={{0,16},{2,18},{4,20},{6,22},{8,24},{10,26},{12,28},{14,30},{16,0},... | collective-permute-start | bytes 811016 | tf_op jit(solution)/shard_map/column_tokens/ppermute | solution.py:241
  8.8 1.3 collective-permute-start.2
  11.1 4.5 %collective-permute-done = bf16[264,512]{1,0:T(8,128)(2,1)S(1)} collective-permute-done((bf16[264,512]{1,0:T(8,128)(2,1)S(1)}, bf16[264,512]{1,0:T(8,128)(2,1)S(1)}, u32[]{:S(2)}, u32[]{:S(2)}) %collective-permute-start) | collective-permute-done | bytes 270368 | tf_op jit(solution)/shard_map/column_tokens/ppermute | solution.py:241
  15.6 10.8 %collective-permute-done.1 = bf16[264,512]{1,0:T(8,128)(2,1)S(1)} collective-permute-done((bf16[264,512]{1,0:T(8,128)(2,1)S(1)}, bf16[264,512]{1,0:T(8,128)(2,1)S(1)}, u32[]{:S(2)}, u32[]{:S(2)}) %collective-permute-start.1) | collective-permute-done | bytes 270368 | tf_op jit(solution)/shard_map/column_tokens/ppermute | solution.py:241
  26.6 1.6 collective-permute-start.4
  29.1 1.5 collective-permute-start.3
  30.6 6.3 %collective-permute-start.5 = (bf16[2,128,256]{2,1,0:T(8,128)(2,1)S(1)}, bf16[2,128,256]{2,1,0:T(8,128)(2,1)S(1)}, u32[]{:S(2)}, u32[]{:S(2)}) collective-permute-start(bf16[2,128,256]{2,1,0:T(8,128)(2,1)S(1)} %get-tuple-element.116), channel_id=1, source_target_pairs={{0,8},{2,10},{4,12},{6,14},{8,16},{10,18},{12,20},{14,22},{16,24},... | collective-permute-start | bytes 393224 | tf_op jit(solution)/shard_map/across_tokens/ppermute | solution.py:241
  36.8 1.6 collective-permute-start.6
  39.3 2.9 %collective-permute-done.5 = bf16[2,128,256]{2,1,0:T(8,128)(2,1)S(1)} collective-permute-done((bf16[2,128,256]{2,1,0:T(8,128)(2,1)S(1)}, bf16[2,128,256]{2,1,0:T(8,128)(2,1)S(1)}, u32[]{:S(2)}, u32[]{:S(2)}) %collective-permute-start.5) | collective-permute-done | bytes 131104 | tf_op jit(solution)/shard_map/across_tokens/ppermute | solution.py:241
  42.3 4.1 %collective-permute-done.6 = bf16[2,128,256]{2,1,0:T(8,128)(2,1)S(1)} collective-permute-done((bf16[2,128,256]{2,1,0:T(8,128)(2,1)S(1)}, bf16[2,128,256]{2,1,0:T(8,128)(2,1)S(1)}, u32[]{:S(2)}, u32[]{:S(2)}) %collective-permute-start.6) | collective-permute-done | bytes 131104 | tf_op jit(solution)/shard_map/across_tokens/ppermute | solution.py:241
  48.3 2.6 %collective-permute-done.15 = bf16[2,4,8,512]{3,2,1,0:T(8,128)(2,1)S(1)} collective-permute-done((bf16[2,4,8,512]{3,2,1,0:T(8,128)(2,1)S(1)}, bf16[2,4,8,512]{3,2,1,0:T(8,128)(2,1)S(1)}, u32[]{:S(2)}, u32[]{:S(2)}) %collective-permute-start.15) | collective-permute-done | bytes 65568 | tf_op jit(solution)/shard_map/over_tokens/ppermute | solution.py:232
  50.9 3.3 %collective-permute-start.12 = (bf16[2,128,256]{2,1,0:T(8,128)(2,1)S(1)}, bf16[2,128,256]{2,1,0:T(8,128)(2,1)S(1)}, u32[]{:S(2)}, u32[]{:S(2)}) collective-permute-start(bf16[2,128,256]{2,1,0:T(8,128)(2,1)S(1)} %get-tuple-element.120), channel_id=1, source_target_pairs={{0,8},{2,10},{4,12},{6,14},{8,16},{10,18},{12,20},{14,22},{16,24},... | collective-permute-start | bytes 393224 | tf_op jit(solution)/shard_map/over_tokens/ppermute | solution.py:241
  54.2 4.9 %collective-permute-done.12 = bf16[2,128,256]{2,1,0:T(8,128)(2,1)S(1)} collective-permute-done((bf16[2,128,256]{2,1,0:T(8,128)(2,1)S(1)}, bf16[2,128,256]{2,1,0:T(8,128)(2,1)S(1)}, u32[]{:S(2)}, u32[]{:S(2)}) %collective-permute-start.12) | collective-permute-done | bytes 131104 | tf_op jit(solution)/shard_map/over_tokens/ppermute | solution.py:241
  59.5 8.2 %collective-permute-done.13 = bf16[2,128,256]{2,1,0:T(8,128)(2,1)S(1)} collective-permute-done((bf16[2,128,256]{2,1,0:T(8,128)(2,1)S(1)}, bf16[2,128,256]{2,1,0:T(8,128)(2,1)S(1)}, u32[]{:S(2)}, u32[]{:S(2)}) %collective-permute-start.13) | collective-permute-done | bytes 131104 | tf_op jit(solution)/shard_map/over_tokens/ppermute | solution.py:241
  67.7 1.5 collective-permute-start.14
  69.3 3.8 %collective-permute-done.14 = bf16[2,128,256]{2,1,0:T(8,128)(2,1)S(1)} collective-permute-done((bf16[2,128,256]{2,1,0:T(8,128)(2,1)S(1)}, bf16[2,128,256]{2,1,0:T(8,128)(2,1)S(1)}, u32[]{:S(2)}, u32[]{:S(2)}) %collective-permute-start.14) | collective-permute-done | bytes 131104 | tf_op jit(solution)/shard_map/over_tokens/ppermute | solution.py:241
  79.7 13.7 %shard_map.118 = (bf16[1024,2048]{1,0:T(8,128)(2,1)}, f32[1024,704]{1,0:T(8,128)}, f32[1024,704]{1,0:T(8,128)}, bf16[1024,704]{1,0:T(8,128)(2,1)}) custom-call(s32[1]{0:T(128)} %bitcast.side, f32[4,4,128]{2,1,0:T(4,128)} %fusion.pos, f32[4,4,128]{2,1,0:T(4,128)} %copy.49.gate, bf16[2,4,128,512]{3,2,1,0:T(8,128)(2,1)} %copy-done.14, ...), custom_call_target="tpu_custom_call" | custom-call | flops 1048576 | bytes 65536 | tf_op jit(solution)/shard_map/pallas_call | solution.py:406
  95.3 1.5 collective-permute-start.20
  96.7 7.3 %shard_map.119 = (bf16[2,2,2,4,128,512]{5,4,3,2,1,0:T(8,128)(2,1)S(1)}, bf16[2,2,2,4,128,512]{5,4,3,2,1,0:T(8,128)(2,1)S(1)}) custom-call(s32[1]{0:T(128)} %bitcast.side, f32[4,4,128]{2,1,0:T(4,128)S(1)} %copy-done.11, bf16[1024,704]{1,0:T(8,128)(2,1)S(1)} %copy-done.3, bf16[704,2048]{1,0:T(8,128)(2,1)S(1)} %bitcast.246), custom_call_target="tpu_custom_call" | custom-call | flops 1048576 | bytes 65536 | tf_op jit(solution)/shard_map/pallas_call | solution.py:418
  104.0 4.3 %collective-permute-done.21.refs_5_ = bf16[2,4,128,256]{3,2,1,0:T(8,128)(2,1)S(1)} collective-permute-done((bf16[2,4,128,256]{3,2,1,0:T(8,128)(2,1)S(1)}, bf16[2,4,128,256]{3,2,1,0:T(8,128)(2,1)S(1)}, u32[]{:S(2)}, u32[]{:S(2)}) %collective-permute-start.21) | collective-permute-done | bytes 524320 | tf_op jit(solution)/shard_map/over_grads_1/ppermute | solution.py:238
  109.6 1.4 collective-permute-start.27
  111.9 4.2 %collective-permute-done.26 = bf16[2,2,2,4,128,512]{5,4,3,2,1,0:T(8,128)(2,1)S(1)} collective-permute-done((bf16[2,2,2,4,128,512]{5,4,3,2,1,0:T(8,128)(2,1)S(1)}, bf16[2,2,2,4,128,512]{5,4,3,2,1,0:T(8,128)(2,1)S(1)}, u32[]{:S(2)}, u32[]{:S(2)}) %collective-permute-start.26) | collective-permute-done | bytes 4194336 | tf_op jit(solution)/shard_map/cores_mixed/ppermute | solution.py:232
  116.9 1.4 copy-done.15
  118.3 1.4 collective-permute-start.31
  120.5 3.9 %collective-permute-done.27.refs_9_ = bf16[2,4,128,256]{3,2,1,0:T(8,128)(2,1)S(1)} collective-permute-done((bf16[2,4,128,256]{3,2,1,0:T(8,128)(2,1)S(1)}, bf16[2,4,128,256]{3,2,1,0:T(8,128)(2,1)S(1)}, u32[]{:S(2)}, u32[]{:S(2)}) %collective-permute-start.27) | collective-permute-done | bytes 524320 | tf_op jit(solution)/shard_map/over_grads_2/ppermute | solution.py:235
  124.4 1.5 collective-permute-done.28.refs_13_
  128.6 7.9 %shard_map.120 = (bf16[1024,2048]{1,0:T(8,128)(2,1)S(1)}, bf16[1024,704]{1,0:T(8,128)(2,1)S(1)}, bf16[1024,704]{1,0:T(8,128)(2,1)S(1)}, f32[4,4,128]{2,1,0:T(4,128)S(1)}) custom-call(s32[1]{0:T(128)} %bitcast.side, f32[4,4,128]{2,1,0:T(4,128)S(1)} %copy-done.11, f32[4,4,128]{2,1,0:T(4,128)S(1)} %copy-done.12, ...), custom_call_target="tpu_custom_call" | custom-call | flops 1048576 | bytes 65536 | tf_op jit(solution)/shard_map/pallas_call | solution.py:442
  136.5 6.1 %shard_map.121 = (bf16[2,2,2,4,128,256]{5,4,3,2,1,0:T(8,128)(2,1)S(1)}, bf16[2,2,2,4,128,256]{5,4,3,2,1,0:T(8,128)(2,1)S(1)}) custom-call(s32[1]{0:T(128)} %bitcast.side, f32[4,4,128]{2,1,0:T(4,128)S(1)} %copy-done.11, bf16[1024,704]{1,0:T(8,128)(2,1)S(1)} %get-tuple-element.172.grad_gate_pre.refs_0_, ...), custom_call_target="tpu_custom_call" | custom-call | flops 1048576 | bytes 65536 | tf_op jit(solution)/shard_map/pallas_call | solution.py:453
  142.6 6.1 %shard_map.122 = (bf16[2,2,2,4,128,256]{5,4,3,2,1,0:T(8,128)(2,1)S(1)}, bf16[2,2,2,4,128,256]{5,4,3,2,1,0:T(8,128)(2,1)S(1)}) custom-call(s32[1]{0:T(128)} %bitcast.side, f32[4,4,128]{2,1,0:T(4,128)S(1)} %copy-done.11, bf16[1024,704]{1,0:T(8,128)(2,1)S(1)} %get-tuple-element.172.grad_gate_pre.refs_0_, ...), custom_call_target="tpu_custom_call" | custom-call | flops 1048576 | bytes 65536 | tf_op jit(solution)/shard_map/pallas_call | solution.py:453
  152.6 5.4 %shard_map.123 = bf16[704,2048]{1,0:T(8,128)(2,1)} custom-call(bf16[1024,704]{1,0:T(8,128)(2,1)S(1)} %copy-done.3, bf16[1024,2048]{1,0:T(8,128)(2,1)S(1)} %get-tuple-element.162.refs_1_), custom_call_target="tpu_custom_call" | custom-call | flops 1048576 | bytes 65536 | tf_op jit(solution)/shard_map/pallas_call | solution.py:355
  159.3 5.1 %collective-permute-done.35 = bf16[4,128,512]{2,1,0:T(8,128)(2,1)S(1)} collective-permute-done((bf16[4,128,512]{2,1,0:T(8,128)(2,1)S(1)}, bf16[4,128,512]{2,1,0:T(8,128)(2,1)S(1)}, u32[]{:S(2)}, u32[]{:S(2)}) %collective-permute-start.35) | collective-permute-done | bytes 524320 | tf_op jit(solution)/shard_map/across_mixed/ppermute | solution.py:238
  167.8 1.6 pad_maximum_fusion
  169.3 8.5 %collective-permute-done.38 = bf16[2,4,128,256]{3,2,1,0:T(8,128)(2,1)S(1)} collective-permute-done((bf16[2,4,128,256]{3,2,1,0:T(8,128)(2,1)S(1)}, bf16[2,4,128,256]{3,2,1,0:T(8,128)(2,1)S(1)}, u32[]{:S(2)}, u32[]{:S(2)}) %collective-permute-start.38) | collective-permute-done | bytes 524320 | tf_op jit(solution)/shard_map/over_inputs_1/ppermute | solution.py:235
  183.5 3.7 %collective-permute-start.42 = (bf16[2,128,512]{2,1,0:T(8,128)(2,1)}, bf16[2,128,512]{2,1,0:T(8,128)(2,1)S(1)}, u32[]{:S(2)}, u32[]{:S(2)}) collective-permute-start(bf16[2,128,512]{2,1,0:T(8,128)(2,1)} %get-tuple-element.220), channel_id=1, source_target_pairs={{0,24},{2,26},{4,28},{6,30},{8,0},{10,2},{12,4},{14,6},{16,8},{18,... | collective-permute-start | bytes 786440 | tf_op jit(solution)/shard_map/column_mixed/ppermute | solution.py:241
  188.9 5.0 %all-to-all-start = ((f32[16,1,128]{2,1,0:T(1,128)}), f32[16,1,128]{2,1,0:T(1,128)S(1)}, u32[]{:S(2)}, u32[]{:S(2)}) async-start(f32[16,1,128]{2,1,0:T(1,128)} %bitcast.84), calls=%async_computation | async-start | bytes 16384 | tf_op jit(solution)/shard_map/gates/all_to_all | solution.py:291
  194.0 2.2 copy-done.4
  196.1 8.8 %shard_map.124 = (bf16[704,2048]{1,0:T(8,128)(2,1)}, bf16[704,2048]{1,0:T(8,128)(2,1)}) custom-call(bf16[1024,704]{1,0:T(8,128)(2,1)S(1)} %get-tuple-element.172.grad_gate_pre.refs_0_, bf16[1024,704]{1,0:T(8,128)(2,1)S(1)} %get-tuple-element.150.grad_up_pre.refs_1_, bf16[1024,2048]{1,0:T(8,128)(2,1)S(1)} %copy-done.4), custom_call_target="tpu_custom_call" | custom-call | flops 1048576 | bytes 65536 | tf_op jit(solution)/shard_map/pallas_call | solution.py:355
  204.9 3.0 %collective-permute-done.43 = bf16[2,128,512]{2,1,0:T(8,128)(2,1)} collective-permute-done((bf16[2,128,512]{2,1,0:T(8,128)(2,1)}, bf16[2,128,512]{2,1,0:T(8,128)(2,1)}, u32[]{:S(2)}, u32[]{:S(2)}) %collective-permute-start.43) | collective-permute-done | bytes 262176 | tf_op jit(solution)/shard_map/column_mixed/ppermute | solution.py:241
  209.9 1.5 fusion.25
  211.5 1.4 fusion.24
  215.0 1.7 collective-permute-start.47
  216.7 2.0 collective-permute-start.49
  218.7 1.3 fusion.29
  220.8 1.6 fusion.20
  222.6 2.5 %collective-permute-start.50 = (bf16[2,128,256]{2,1,0:T(8,128)(2,1)S(1)}, bf16[2,128,256]{2,1,0:T(8,128)(2,1)S(1)}, u32[]{:S(2)}, u32[]{:S(2)}) collective-permute-start(bf16[2,128,256]{2,1,0:T(8,128)(2,1)S(1)} %get-tuple-element.224), channel_id=1, source_target_pairs={{0,24},{2,26},{4,28},{6,30},{8,0},{10,2},{12,4},{14,6},{16,8},{18,... | collective-permute-start | bytes 393224 | tf_op jit(solution)/shard_map/column_inputs_2/ppermute | solution.py:241
  226.5 7.9 %collective-permute-done.48 = bf16[2,128,256]{2,1,0:T(8,128)(2,1)S(1)} collective-permute-done((bf16[2,128,256]{2,1,0:T(8,128)(2,1)S(1)}, bf16[2,128,256]{2,1,0:T(8,128)(2,1)S(1)}, u32[]{:S(2)}, u32[]{:S(2)}) %collective-permute-start.48) | collective-permute-done | bytes 131104 | tf_op jit(solution)/shard_map/column_inputs_1/ppermute | solution.py:241
  235.1 4.2 %collective-permute-done.51 = bf16[2,128,256]{2,1,0:T(8,128)(2,1)S(1)} collective-permute-done((bf16[2,128,256]{2,1,0:T(8,128)(2,1)S(1)}, bf16[2,128,256]{2,1,0:T(8,128)(2,1)S(1)}, u32[]{:S(2)}, u32[]{:S(2)}) %collective-permute-start.51) | collective-permute-done | bytes 131104 | tf_op jit(solution)/shard_map/column_inputs_2/ppermute | solution.py:241
  (215 shorter events, 45.9 us)
Async XLA Ops:
  3.1 12.6 %collective-permute-start = (bf16[264,512]{1,0:T(8,128)(2,1)S(1)}, bf16[264,512]{1,0:T(8,128)(2,1)S(1)}, u32[]{:S(2)}, u32[]{:S(2)}) collective-permute-start(bf16[264,512]{1,0:T(8,128)(2,1)S(1)} %pad_maximum_fusion.13), channel_id=1, source_target_pairs={{0,8},{2,10},{4,12},{6,14},{8,16},{10,18},{12,20},{14,22},{16,24},... | collective-permute-start | bytes 811016 | tf_op jit(solution)/shard_map/column_tokens/ppermute | solution.py:241
  6.2 20.2 %collective-permute-start.1 = (bf16[264,512]{1,0:T(8,128)(2,1)S(1)}, bf16[264,512]{1,0:T(8,128)(2,1)S(1)}, u32[]{:S(2)}, u32[]{:S(2)}) collective-permute-start(bf16[264,512]{1,0:T(8,128)(2,1)S(1)} %pad_maximum_fusion.13), channel_id=1, source_target_pairs={{0,16},{2,18},{4,20},{6,22},{8,24},{10,26},{12,28},{14,30},{16,0},... | collective-permute-start | bytes 811016 | tf_op jit(solution)/shard_map/column_tokens/ppermute | solution.py:241
  8.8 17.6 %collective-permute-start.2 = (bf16[264,512]{1,0:T(8,128)(2,1)S(1)}, bf16[264,512]{1,0:T(8,128)(2,1)S(1)}, u32[]{:S(2)}, u32[]{:S(2)}) collective-permute-start(bf16[264,512]{1,0:T(8,128)(2,1)S(1)} %pad_maximum_fusion.13), channel_id=1, source_target_pairs={{0,24},{2,26},{4,28},{6,30},{8,0},{10,2},{12,4},{14,6},{16,8},{18,... | collective-permute-start | bytes 811016 | tf_op jit(solution)/shard_map/column_tokens/ppermute | solution.py:241
  26.6 19.8 %collective-permute-start.4 = (bf16[4,136,512]{2,1,0:T(8,128)(2,1)S(1)}, bf16[4,136,512]{2,1,0:T(8,128)(2,1)S(1)}, u32[]{:S(2)}, u32[]{:S(2)}) collective-permute-start(bf16[4,136,512]{2,1,0:T(8,128)(2,1)S(1)} %pad_maximum_fusion.9), channel_id=1, source_target_pairs={{0,4},{2,6},{4,0},{6,2},{8,12},{10,14},{12,8},{14,10},{16,20},{18,... | collective-permute-start | bytes 1671176 | tf_op jit(solution)/shard_map/across_tokens/ppermute | solution.py:235
  29.1 17.3 %collective-permute-start.3 = (bf16[4,128,512]{2,1,0:T(8,128)(2,1)S(1)}, bf16[4,128,512]{2,1,0:T(8,128)(2,1)S(1)}, u32[]{:S(2)}, u32[]{:S(2)}) collective-permute-start(bf16[4,128,512]{2,1,0:T(8,128)(2,1)S(1)} %get-tuple-element.232), channel_id=1, source_target_pairs={{0,1},{1,0},{2,3},{3,2},{4,5},{5,4},{6,7},{7,6},{8,9},{9,8},{10,11... | collective-permute-start | bytes 1572872 | tf_op jit(solution)/shard_map/across_tokens/ppermute | solution.py:238
  30.6 11.7 %collective-permute-start.5 = (bf16[2,128,256]{2,1,0:T(8,128)(2,1)S(1)}, bf16[2,128,256]{2,1,0:T(8,128)(2,1)S(1)}, u32[]{:S(2)}, u32[]{:S(2)}) collective-permute-start(bf16[2,128,256]{2,1,0:T(8,128)(2,1)S(1)} %get-tuple-element.116), channel_id=1, source_target_pairs={{0,8},{2,10},{4,12},{6,14},{8,16},{10,18},{12,20},{14,22},{16,24},... | collective-permute-start | bytes 393224 | tf_op jit(solution)/shard_map/across_tokens/ppermute | solution.py:241
  36.8 9.6 %collective-permute-start.6 = (bf16[2,128,256]{2,1,0:T(8,128)(2,1)S(1)}, bf16[2,128,256]{2,1,0:T(8,128)(2,1)S(1)}, u32[]{:S(2)}, u32[]{:S(2)}) collective-permute-start(bf16[2,128,256]{2,1,0:T(8,128)(2,1)S(1)} %get-tuple-element.116), channel_id=1, source_target_pairs={{0,16},{2,18},{4,20},{6,22},{8,24},{10,26},{12,28},{14,30},{16,0},... | collective-permute-start | bytes 393224 | tf_op jit(solution)/shard_map/across_tokens/ppermute | solution.py:241
  38.4 8.0 %collective-permute-start.7 = (bf16[2,128,256]{2,1,0:T(8,128)(2,1)S(1)}, bf16[2,128,256]{2,1,0:T(8,128)(2,1)S(1)}, u32[]{:S(2)}, u32[]{:S(2)}) collective-permute-start(bf16[2,128,256]{2,1,0:T(8,128)(2,1)S(1)} %get-tuple-element.116), channel_id=1, source_target_pairs={{0,24},{2,26},{4,28},{6,30},{8,0},{10,2},{12,4},{14,6},{16,8},{18,... | collective-permute-start | bytes 393224 | tf_op jit(solution)/shard_map/across_tokens/ppermute | solution.py:241
  46.6 26.5 %collective-permute-start.11 = (bf16[2,4,128,512]{3,2,1,0:T(8,128)(2,1)S(1)}, bf16[2,4,128,512]{3,2,1,0:T(8,128)(2,1)S(1)}, u32[]{:S(2)}, u32[]{:S(2)}) collective-permute-start(bf16[2,4,128,512]{3,2,1,0:T(8,128)(2,1)S(1)} %pad_maximum_fusion.4.refs_4_), channel_id=1, source_target_pairs={{0,2},{2,0},{4,6},{6,4},{8,10},{10,8},{12,14},{14,12},{16,18},{18,... | collective-permute-start | bytes 3145736 | tf_op jit(solution)/shard_map/over_tokens/ppermute | solution.py:232
  46.7 26.4 %collective-permute-start.9 = (bf16[2,4,128,512]{3,2,1,0:T(8,128)(2,1)S(1)}, bf16[2,4,128,512]{3,2,1,0:T(8,128)(2,1)}, u32[]{:S(2)}, u32[]{:S(2)}) collective-permute-start(bf16[2,4,128,512]{3,2,1,0:T(8,128)(2,1)S(1)} %pad_maximum_fusion.4.refs_4_), channel_id=1, source_target_pairs={{0,1},{1,0},{2,3},{3,2},{4,5},{5,4},{6,7},{7,6},{8,9},{9,8},{10,11... | collective-permute-start | bytes 3145736 | tf_op jit(solution)/shard_map/over_tokens/ppermute | solution.py:238
  47.4 25.7 %collective-permute-start.10 = (bf16[2,4,128,512]{3,2,1,0:T(8,128)(2,1)S(1)}, bf16[2,4,128,512]{3,2,1,0:T(8,128)(2,1)S(1)}, u32[]{:S(2)}, u32[]{:S(2)}) collective-permute-start(bf16[2,4,128,512]{3,2,1,0:T(8,128)(2,1)S(1)} %pad_maximum_fusion.3.refs_0_), channel_id=1, source_target_pairs={{0,2},{2,0},{4,6},{6,4},{8,10},{10,8},{12,14},{14,12},{16,18},{18,... | collective-permute-start | bytes 3145736 | tf_op jit(solution)/shard_map/over_tokens/ppermute | solution.py:232
  47.6 25.5 %collective-permute-start.8 = (bf16[2,4,128,512]{3,2,1,0:T(8,128)(2,1)S(1)}, bf16[2,4,128,512]{3,2,1,0:T(8,128)(2,1)}, u32[]{:S(2)}, u32[]{:S(2)}) collective-permute-start(bf16[2,4,128,512]{3,2,1,0:T(8,128)(2,1)S(1)} %pad_maximum_fusion.3.refs_0_), channel_id=1, source_target_pairs={{0,4},{2,6},{4,0},{6,2},{8,12},{10,14},{12,8},{14,10},{16,20},{18,... | collective-permute-start | bytes 3145736 | tf_op jit(solution)/shard_map/over_tokens/ppermute | solution.py:235
  50.9 8.1 %collective-permute-start.12 = (bf16[2,128,256]{2,1,0:T(8,128)(2,1)S(1)}, bf16[2,128,256]{2,1,0:T(8,128)(2,1)S(1)}, u32[]{:S(2)}, u32[]{:S(2)}) collective-permute-start(bf16[2,128,256]{2,1,0:T(8,128)(2,1)S(1)} %get-tuple-element.120), channel_id=1, source_target_pairs={{0,8},{2,10},{4,12},{6,14},{8,16},{10,18},{12,20},{14,22},{16,24},... | collective-permute-start | bytes 393224 | tf_op jit(solution)/shard_map/over_tokens/ppermute | solution.py:241
  59.1 8.6 %collective-permute-start.13 = (bf16[2,128,256]{2,1,0:T(8,128)(2,1)S(1)}, bf16[2,128,256]{2,1,0:T(8,128)(2,1)S(1)}, u32[]{:S(2)}, u32[]{:S(2)}) collective-permute-start(bf16[2,128,256]{2,1,0:T(8,128)(2,1)S(1)} %get-tuple-element.120), channel_id=1, source_target_pairs={{0,16},{2,18},{4,20},{6,22},{8,24},{10,26},{12,28},{14,30},{16,0},... | collective-permute-start | bytes 393224 | tf_op jit(solution)/shard_map/over_tokens/ppermute | solution.py:241
  75.3 18.1 %collective-permute-start.19 = (bf16[2,4,128,256]{3,2,1,0:T(8,128)(2,1)S(1)}, bf16[2,4,128,256]{3,2,1,0:T(8,128)(2,1)S(1)}, u32[]{:S(2)}, u32[]{:S(2)}) collective-permute-start(bf16[2,4,128,256]{3,2,1,0:T(8,128)(2,1)S(1)} %get-tuple-element.228), channel_id=1, source_target_pairs={{0,4},{2,6},{4,0},{6,2},{8,12},{10,14},{12,8},{14,10},{16,20},{18,... | collective-permute-start | bytes 1572872 | tf_op jit(solution)/shard_map/across_grads/ppermute | solution.py:235
  76.8 16.6 %collective-permute-start.18 = (bf16[2,4,128,256]{3,2,1,0:T(8,128)(2,1)}, bf16[2,4,128,256]{3,2,1,0:T(8,128)(2,1)S(1)}, u32[]{:S(2)}, u32[]{:S(2)}) collective-permute-start(bf16[2,4,128,256]{3,2,1,0:T(8,128)(2,1)} %get-tuple-element.229), channel_id=1, source_target_pairs={{0,1},{1,0},{2,3},{3,2},{4,5},{5,4},{6,7},{7,6},{8,9},{9,8},{10,11... | collective-permute-start | bytes 1572872 | tf_op jit(solution)/shard_map/across_grads/ppermute | solution.py:238
  93.5 15.5 %collective-permute-start.23 = (bf16[2,2,4,128,256]{4,3,2,1,0:T(8,128)(2,1)S(1)}, bf16[2,2,4,128,256]{4,3,2,1,0:T(8,128)(2,1)S(1)}, u32[]{:S(2)}, u32[]{:S(2)}) collective-permute-start(bf16[2,2,4,128,256]{4,3,2,1,0:T(8,128)(2,1)S(1)} %pad_maximum_fusion.2.refs_4_.refs_12_), channel_id=1, source_target_pairs={{0,2},{2,0},{4,6},{6,4},{8,10},{10,8},{12,14},{14,12},{16,18},{18,... | collective-permute-start | bytes 3145736 | tf_op jit(solution)/shard_map/over_grads_1/ppermute | solution.py:232
  93.8 15.2 %collective-permute-start.22 = (bf16[2,2,4,128,256]{4,3,2,0,1:T(8,128)(2,1)S(1)}, bf16[2,2,4,128,256]{4,3,2,0,1:T(8,128)(2,1)S(1)}, u32[]{:S(2)}, u32[]{:S(2)}) collective-permute-start(bf16[2,2,4,128,256]{4,3,2,0,1:T(8,128)(2,1)S(1)} %pad_maximum_fusion.1), channel_id=1, source_target_pairs={{0,2},{2,0},{4,6},{6,4},{8,10},{10,8},{12,14},{14,12},{16,18},{18,... | collective-permute-start | bytes 3145736 | tf_op jit(solution)/shard_map/over_grads_1/ppermute | solution.py:232
  94.4 14.0 %collective-permute-start.21 = (bf16[2,4,128,256]{3,2,1,0:T(8,128)(2,1)S(1)}, bf16[2,4,128,256]{3,2,1,0:T(8,128)(2,1)S(1)}, u32[]{:S(2)}, u32[]{:S(2)}) collective-permute-start(bf16[2,4,128,256]{3,2,1,0:T(8,128)(2,1)S(1)} %fusion.14), channel_id=1, source_target_pairs={{0,1},{1,0},{2,3},{3,2},{4,5},{5,4},{6,7},{7,6},{8,9},{9,8},{10,11... | collective-permute-start | bytes 1572872 | tf_op jit(solution)/shard_map/over_grads_1/ppermute | solution.py:238
  95.3 13.7 %collective-permute-start.20 = (bf16[2,4,128,256]{3,2,1,0:T(8,128)(2,1)S(1)}, bf16[2,4,128,256]{3,2,1,0:T(8,128)(2,1)S(1)}, u32[]{:S(2)}, u32[]{:S(2)}) collective-permute-start(bf16[2,4,128,256]{3,2,1,0:T(8,128)(2,1)S(1)} %fusion.16), channel_id=1, source_target_pairs={{0,4},{2,6},{4,0},{6,2},{8,12},{10,14},{12,8},{14,10},{16,20},{18,... | collective-permute-start | bytes 1572872 | tf_op jit(solution)/shard_map/over_grads_1/ppermute | solution.py:235
  109.0 7.2 %collective-permute-start.26 = (bf16[2,2,2,4,128,512]{5,4,3,2,1,0:T(8,128)(2,1)S(1)}, bf16[2,2,2,4,128,512]{5,4,3,2,1,0:T(8,128)(2,1)S(1)}, u32[]{:S(2)}, u32[]{:S(2)}) collective-permute-start(bf16[2,2,2,4,128,512]{5,4,3,2,1,0:T(8,128)(2,1)S(1)} %get-tuple-element.138), channel_id=1, source_target_pairs={{0,2},{2,0},{4,6},{6,4},{8,10},{10,8},{12,14},{14,12},{16,18},{18,... | collective-permute-start | bytes 12582920 | tf_op jit(solution)/shard_map/cores_mixed/ppermute | solution.py:232
  109.0 9.3 %collective-permute-start.24 = (bf16[2,4,128,256]{3,2,1,0:T(8,128)(2,1)S(1)}, bf16[2,4,128,256]{3,2,1,0:T(8,128)(2,1)S(1)}, u32[]{:S(2)}, u32[]{:S(2)}) collective-permute-start(bf16[2,4,128,256]{3,2,1,0:T(8,128)(2,1)S(1)} %collective-permute-done.20.refs_1_), channel_id=1, source_target_pairs={{0,2},{2,0},{4,6},{6,4},{8,10},{10,8},{12,14},{14,12},{16,18},{18,... | collective-permute-start | bytes 1572872 | tf_op jit(solution)/shard_map/cores_mixed/ppermute | solution.py:232
  109.5 8.8 %collective-permute-start.25 = (bf16[2,4,128,256]{3,2,1,0:T(8,128)(2,1)S(1)}, bf16[2,4,128,256]{3,2,1,0:T(8,128)(2,1)S(1)}, u32[]{:S(2)}, u32[]{:S(2)}) collective-permute-start(bf16[2,4,128,256]{3,2,1,0:T(8,128)(2,1)S(1)} %collective-permute-done.21.refs_5_), channel_id=1, source_target_pairs={{0,2},{2,0},{4,6},{6,4},{8,10},{10,8},{12,14},{14,12},{16,18},{18,... | collective-permute-start | bytes 1572872 | tf_op jit(solution)/shard_map/cores_mixed/ppermute | solution.py:232
  109.6 14.8 %collective-permute-start.27 = (bf16[2,4,128,256]{3,2,1,0:T(8,128)(2,1)S(1)}, bf16[2,4,128,256]{3,2,1,0:T(8,128)(2,1)S(1)}, u32[]{:S(2)}, u32[]{:S(2)}) collective-permute-start(bf16[2,4,128,256]{3,2,1,0:T(8,128)(2,1)S(1)} %slice_bitcast_fusion.2), channel_id=1, source_target_pairs={{0,4},{2,6},{4,0},{6,2},{8,12},{10,14},{12,8},{14,10},{16,20},{18,... | collective-permute-start | bytes 1572872 | tf_op jit(solution)/shard_map/over_grads_2/ppermute | solution.py:235
  111.0 14.8 %collective-permute-start.28 = (bf16[2,4,128,256]{3,2,1,0:T(8,128)(2,1)S(1)}, bf16[2,4,128,256]{3,2,1,0:T(8,128)(2,1)S(1)}, u32[]{:S(2)}, u32[]{:S(2)}) collective-permute-start(bf16[2,4,128,256]{3,2,1,0:T(8,128)(2,1)S(1)} %slice_bitcast_fusion.1), channel_id=1, source_target_pairs={{0,1},{1,0},{2,3},{3,2},{4,5},{5,4},{6,7},{7,6},{8,9},{9,8},{10,11... | collective-permute-start | bytes 1572872 | tf_op jit(solution)/shard_map/over_grads_2/ppermute | solution.py:238
  118.3 30.5 %collective-permute-start.31 = (bf16[2,4,128,512]{3,2,1,0:T(8,128)(2,1)S(1)}, bf16[2,4,128,512]{3,2,1,0:T(8,128)(2,1)S(1)}, u32[]{:S(2)}, u32[]{:S(2)}) collective-permute-start(bf16[2,4,128,512]{3,2,1,0:T(8,128)(2,1)S(1)} %get-tuple-element.143), channel_id=1, source_target_pairs={{0,4},{2,6},{4,0},{6,2},{8,12},{10,14},{12,8},{14,10},{16,20},{18,... | collective-permute-start | bytes 3145736 | tf_op jit(solution)/shard_map/over_mixed/ppermute | solution.py:235
  119.7 29.1 %collective-permute-start.32 = (bf16[2,4,128,512]{3,2,1,0:T(8,128)(2,1)S(1)}, bf16[2,4,128,512]{3,2,1,0:T(8,128)(2,1)S(1)}, u32[]{:S(2)}, u32[]{:S(2)}) collective-permute-start(bf16[2,4,128,512]{3,2,1,0:T(8,128)(2,1)S(1)} %get-tuple-element.144), channel_id=1, source_target_pairs={{0,1},{1,0},{2,3},{3,2},{4,5},{5,4},{6,7},{7,6},{8,9},{9,8},{10,11... | collective-permute-start | bytes 3145736 | tf_op jit(solution)/shard_map/over_mixed/ppermute | solution.py:238
  148.8 9.2 %collective-permute-start.33 = (bf16[2,2,2,4,128,256]{5,4,3,2,1,0:T(8,128)(2,1)S(1)}, bf16[2,2,2,4,128,256]{5,4,3,2,1,0:T(8,128)(2,1)S(1)}, u32[]{:S(2)}, u32[]{:S(2)}) collective-permute-start(bf16[2,2,2,4,128,256]{5,4,3,2,1,0:T(8,128)(2,1)S(1)} %get-tuple-element.155), channel_id=1, source_target_pairs={{0,2},{2,0},{4,6},{6,4},{8,10},{10,8},{12,14},{14,12},{16,18},{18,... | collective-permute-start | bytes 6291464 | tf_op jit(solution)/shard_map/cores_inputs/ppermute | solution.py:232
  149.0 9.4 %collective-permute-start.34 = (bf16[2,2,2,4,128,256]{5,4,3,2,1,0:T(8,128)(2,1)S(1)}, bf16[2,2,2,4,128,256]{5,4,3,2,1,0:T(8,128)(2,1)S(1)}, u32[]{:S(2)}, u32[]{:S(2)}) collective-permute-start(bf16[2,2,2,4,128,256]{5,4,3,2,1,0:T(8,128)(2,1)S(1)} %get-tuple-element.157), channel_id=1, source_target_pairs={{0,2},{2,0},{4,6},{6,4},{8,10},{10,8},{12,14},{14,12},{16,18},{18,... | collective-permute-start | bytes 6291464 | tf_op jit(solution)/shard_map/cores_inputs/ppermute | solution.py:232
  149.4 8.6 %collective-permute-start.37 = (f32[4,4,128]{2,1,0:T(4,128)S(1)}, f32[4,4,128]{2,1,0:T(4,128)S(1)}, u32[]{:S(2)}, u32[]{:S(2)}) collective-permute-start(f32[4,4,128]{2,1,0:T(4,128)S(1)} %get-tuple-element.160), channel_id=1, source_target_pairs={{0,1},{1,0},{2,3},{3,2},{4,5},{5,4},{6,7},{7,6},{8,9},{9,8},{10,11... | collective-permute-start | bytes 24584 | tf_op jit(solution)/shard_map/gates/ppermute | solution.py:238
  150.7 13.7 %collective-permute-start.35 = (bf16[4,128,512]{2,1,0:T(8,128)(2,1)S(1)}, bf16[4,128,512]{2,1,0:T(8,128)(2,1)S(1)}, u32[]{:S(2)}, u32[]{:S(2)}) collective-permute-start(bf16[4,128,512]{2,1,0:T(8,128)(2,1)S(1)} %get-tuple-element.203), channel_id=1, source_target_pairs={{0,1},{1,0},{2,3},{3,2},{4,5},{5,4},{6,7},{7,6},{8,9},{9,8},{10,11... | collective-permute-start | bytes 1572872 | tf_op jit(solution)/shard_map/across_mixed/ppermute | solution.py:238
  151.9 13.4 %collective-permute-start.36 = (bf16[4,128,512]{2,1,0:T(8,128)(2,1)S(1)}, bf16[4,128,512]{2,1,0:T(8,128)(2,1)S(1)}, u32[]{:S(2)}, u32[]{:S(2)}) collective-permute-start(bf16[4,128,512]{2,1,0:T(8,128)(2,1)S(1)} %get-tuple-element.202), channel_id=1, source_target_pairs={{0,4},{2,6},{4,0},{6,2},{8,12},{10,14},{12,8},{14,10},{16,20},{18,... | collective-permute-start | bytes 1572872 | tf_op jit(solution)/shard_map/across_mixed/ppermute | solution.py:235
  165.3 12.5 %collective-permute-start.38 = (bf16[2,4,128,256]{3,2,1,0:T(8,128)(2,1)S(1)}, bf16[2,4,128,256]{3,2,1,0:T(8,128)(2,1)S(1)}, u32[]{:S(2)}, u32[]{:S(2)}) collective-permute-start(bf16[2,4,128,256]{3,2,1,0:T(8,128)(2,1)S(1)} %get-tuple-element.163), channel_id=1, source_target_pairs={{0,4},{2,6},{4,0},{6,2},{8,12},{10,14},{12,8},{14,10},{16,20},{18,... | collective-permute-start | bytes 1572872 | tf_op jit(solution)/shard_map/over_inputs_1/ppermute | solution.py:235
  166.0 12.2 %collective-permute-start.39 = (bf16[2,4,128,256]{3,2,1,0:T(8,128)(2,1)S(1)}, bf16[2,4,128,256]{3,2,1,0:T(8,128)(2,1)S(1)}, u32[]{:S(2)}, u32[]{:S(2)}) collective-permute-start(bf16[2,4,128,256]{3,2,1,0:T(8,128)(2,1)S(1)} %get-tuple-element.164), channel_id=1, source_target_pairs={{0,1},{1,0},{2,3},{3,2},{4,5},{5,4},{6,7},{7,6},{8,9},{9,8},{10,11... | collective-permute-start | bytes 1572872 | tf_op jit(solution)/shard_map/over_inputs_1/ppermute | solution.py:238
  179.4 28.5 %collective-permute-start.41 = (bf16[3,4,128,256]{3,2,1,0:T(8,128)(2,1)}, bf16[3,4,128,256]{3,2,1,0:T(8,128)(2,1)}, u32[]{:S(2)}, u32[]{:S(2)}) collective-permute-start(bf16[3,4,128,256]{3,2,1,0:T(8,128)(2,1)} %pad_maximum_fusion.8), channel_id=1, source_target_pairs={{0,4},{2,6},{4,0},{6,2},{8,12},{10,14},{12,8},{14,10},{16,20},{18,... | collective-permute-start | bytes 2359304 | tf_op jit(solution)/shard_map/inputs_1_and_2/ppermute | solution.py:235
  181.7 26.2 %collective-permute-start.40 = (bf16[3,4,128,256]{3,2,1,0:T(8,128)(2,1)}, bf16[3,4,128,256]{3,2,1,0:T(8,128)(2,1)}, u32[]{:S(2)}, u32[]{:S(2)}) collective-permute-start(bf16[3,4,128,256]{3,2,1,0:T(8,128)(2,1)} %pad_maximum_fusion.7), channel_id=1, source_target_pairs={{0,1},{1,0},{2,3},{3,2},{4,5},{5,4},{6,7},{7,6},{8,9},{9,8},{10,11... | collective-permute-start | bytes 2359304 | tf_op jit(solution)/shard_map/inputs_1_and_2/ppermute | solution.py:238
  183.5 21.5 %collective-permute-start.42 = (bf16[2,128,512]{2,1,0:T(8,128)(2,1)}, bf16[2,128,512]{2,1,0:T(8,128)(2,1)S(1)}, u32[]{:S(2)}, u32[]{:S(2)}) collective-permute-start(bf16[2,128,512]{2,1,0:T(8,128)(2,1)} %get-tuple-element.220), channel_id=1, source_target_pairs={{0,24},{2,26},{4,28},{6,30},{8,0},{10,2},{12,4},{14,6},{16,8},{18,... | collective-permute-start | bytes 786440 | tf_op jit(solution)/shard_map/column_mixed/ppermute | solution.py:241
  187.1 20.8 %collective-permute-start.43 = (bf16[2,128,512]{2,1,0:T(8,128)(2,1)}, bf16[2,128,512]{2,1,0:T(8,128)(2,1)}, u32[]{:S(2)}, u32[]{:S(2)}) collective-permute-start(bf16[2,128,512]{2,1,0:T(8,128)(2,1)} %get-tuple-element.219), channel_id=1, source_target_pairs={{0,16},{2,18},{4,20},{6,22},{8,24},{10,26},{12,28},{14,30},{16,0},... | collective-permute-start | bytes 786440 | tf_op jit(solution)/shard_map/column_mixed/ppermute | solution.py:241
  187.5 20.4 %collective-permute-start.44 = (bf16[2,128,512]{2,1,0:T(8,128)(2,1)}, bf16[2,128,512]{2,1,0:T(8,128)(2,1)}, u32[]{:S(2)}, u32[]{:S(2)}) collective-permute-start(bf16[2,128,512]{2,1,0:T(8,128)(2,1)} %get-tuple-element.218), channel_id=1, source_target_pairs={{0,8},{2,10},{4,12},{6,14},{8,16},{10,18},{12,20},{14,22},{16,24},... | collective-permute-start | bytes 786440 | tf_op jit(solution)/shard_map/column_mixed/ppermute | solution.py:241
  188.9 31.9 %all-to-all-start = ((f32[16,1,128]{2,1,0:T(1,128)}), f32[16,1,128]{2,1,0:T(1,128)S(1)}, u32[]{:S(2)}, u32[]{:S(2)}) async-start(f32[16,1,128]{2,1,0:T(1,128)} %bitcast.84), calls=%async_computation | async-start | bytes 16384 | tf_op jit(solution)/shard_map/gates/all_to_all | solution.py:291
  213.0 7.8 %collective-permute-start.45 = (bf16[4,128,256]{2,1,0:T(8,128)(2,1)S(1)}, bf16[4,128,256]{2,1,0:T(8,128)(2,1)S(1)}, u32[]{:S(2)}, u32[]{:S(2)}) collective-permute-start(bf16[4,128,256]{2,1,0:T(8,128)(2,1)S(1)} %get-tuple-element.211), channel_id=1, source_target_pairs={{0,1},{1,0},{2,3},{3,2},{4,5},{5,4},{6,7},{7,6},{8,9},{9,8},{10,11... | collective-permute-start | bytes 786440 | tf_op jit(solution)/shard_map/across_inputs_2/ppermute | solution.py:238
  213.8 7.0 %collective-permute-start.46 = (bf16[4,128,256]{2,1,0:T(8,128)(2,1)S(1)}, bf16[4,128,256]{2,1,0:T(8,128)(2,1)S(1)}, u32[]{:S(2)}, u32[]{:S(2)}) collective-permute-start(bf16[4,128,256]{2,1,0:T(8,128)(2,1)S(1)} %get-tuple-element.210), channel_id=1, source_target_pairs={{0,4},{2,6},{4,0},{6,2},{8,12},{10,14},{12,8},{14,10},{16,20},{18,... | collective-permute-start | bytes 786440 | tf_op jit(solution)/shard_map/across_inputs_2/ppermute | solution.py:235
  215.0 10.7 %collective-permute-start.47 = (bf16[2,128,256]{2,1,0:T(8,128)(2,1)S(1)}, bf16[2,128,256]{2,1,0:T(8,128)(2,1)S(1)}, u32[]{:S(2)}, u32[]{:S(2)}) collective-permute-start(bf16[2,128,256]{2,1,0:T(8,128)(2,1)S(1)} %get-tuple-element.221), channel_id=1, source_target_pairs={{0,24},{2,26},{4,28},{6,30},{8,0},{10,2},{12,4},{14,6},{16,8},{18,... | collective-permute-start | bytes 393224 | tf_op jit(solution)/shard_map/column_inputs_1/ppermute | solution.py:241
  216.7 17.7 %collective-permute-start.48 = (bf16[2,128,256]{2,1,0:T(8,128)(2,1)S(1)}, bf16[2,128,256]{2,1,0:T(8,128)(2,1)S(1)}, u32[]{:S(2)}, u32[]{:S(2)}) collective-permute-start(bf16[2,128,256]{2,1,0:T(8,128)(2,1)S(1)} %get-tuple-element.223), channel_id=1, source_target_pairs={{0,16},{2,18},{4,20},{6,22},{8,24},{10,26},{12,28},{14,30},{16,0},... | collective-permute-start | bytes 393224 | tf_op jit(solution)/shard_map/column_inputs_1/ppermute | solution.py:241
  216.7 17.7 %collective-permute-start.49 = (bf16[2,128,256]{2,1,0:T(8,128)(2,1)S(1)}, bf16[2,128,256]{2,1,0:T(8,128)(2,1)S(1)}, u32[]{:S(2)}, u32[]{:S(2)}) collective-permute-start(bf16[2,128,256]{2,1,0:T(8,128)(2,1)S(1)} %get-tuple-element.222), channel_id=1, source_target_pairs={{0,8},{2,10},{4,12},{6,14},{8,16},{10,18},{12,20},{14,22},{16,24},... | collective-permute-start | bytes 393224 | tf_op jit(solution)/shard_map/column_inputs_1/ppermute | solution.py:241
  222.6 12.4 %collective-permute-start.50 = (bf16[2,128,256]{2,1,0:T(8,128)(2,1)S(1)}, bf16[2,128,256]{2,1,0:T(8,128)(2,1)S(1)}, u32[]{:S(2)}, u32[]{:S(2)}) collective-permute-start(bf16[2,128,256]{2,1,0:T(8,128)(2,1)S(1)} %get-tuple-element.224), channel_id=1, source_target_pairs={{0,24},{2,26},{4,28},{6,30},{8,0},{10,2},{12,4},{14,6},{16,8},{18,... | collective-permute-start | bytes 393224 | tf_op jit(solution)/shard_map/column_inputs_2/ppermute | solution.py:241
  225.2 14.1 %collective-permute-start.51 = (bf16[2,128,256]{2,1,0:T(8,128)(2,1)S(1)}, bf16[2,128,256]{2,1,0:T(8,128)(2,1)S(1)}, u32[]{:S(2)}, u32[]{:S(2)}) collective-permute-start(bf16[2,128,256]{2,1,0:T(8,128)(2,1)S(1)} %get-tuple-element.226), channel_id=1, source_target_pairs={{0,16},{2,18},{4,20},{6,22},{8,24},{10,26},{12,28},{14,30},{16,0},... | collective-permute-start | bytes 393224 | tf_op jit(solution)/shard_map/column_inputs_2/ppermute | solution.py:241
  225.6 13.7 %collective-permute-start.52 = (bf16[2,128,256]{2,1,0:T(8,128)(2,1)S(1)}, bf16[2,128,256]{2,1,0:T(8,128)(2,1)S(1)}, u32[]{:S(2)}, u32[]{:S(2)}) collective-permute-start(bf16[2,128,256]{2,1,0:T(8,128)(2,1)S(1)} %get-tuple-element.225), channel_id=1, source_target_pairs={{0,8},{2,10},{4,12},{6,14},{8,16},{10,18},{12,20},{14,22},{16,24},... | collective-permute-start | bytes 393224 | tf_op jit(solution)/shard_map/column_inputs_2/ppermute | solution.py:241
  (35 other events, 290.3 us)

commit v4 on v3

--- a/solution.py
+++ b/solution.py
@@ -253,6 +253,16 @@
     def column_parts(own):
         return [own] + [shift(own, step) for step in range(1, column)]
 
+    def relayed_parts(own):
+        if column != 4:
+            return column_parts(own)
+        one, three = shift(own, 1), shift(own, 3)
+        inner = [(e, (e + 8) % expert_count) for e in range(expert_count) if e // 4 in (0, 3)]
+        two = lax.ppermute(own, "expert", inner)
+        outer = [(e, e - 4) for e in range(4, 8)] + [(e, e + 4) for e in range(8, 12)]
+        passed = lax.ppermute(jnp.where(me // 4 == 1, three, one), "expert", outer)
+        return [own, one, jnp.where((me // 4 == 1) | (me // 4 == 2), two, passed), three]
+
     def halves(rows):
         size = rows.shape[1] // 2
         return jnp.stack([rows[:, :size], rows[:, size:]])
@@ -377,7 +387,7 @@
     token_rows = jnp.concatenate([tokens[:, :half], tokens[:, half:], routing_rows(half)])
     own_1, own_2 = halves(grad_out[:, :half]), halves(grad_out[:, half:])
     with jax.named_scope("column_tokens"):
-        token_parts = column_parts(token_rows)
+        token_parts = relayed_parts(token_rows)
         token_parts, own_1, own_2 = together(token_parts, own_1, own_2)
         near_a = jnp.stack([part[:tok_count] for part in token_parts])
         near_b = jnp.stack([part[tok_count:] for part in token_parts])
@@ -392,16 +402,16 @@
         far_a, far_b = over(near_a, near_b)
         core_a, core_b = cores((near_a, near_b))
         parts_2 = column_parts(own_2)
-        far_a, far_b, core_a, core_b, parts_2, core_routing = together(
-            far_a, far_b, core_a, core_b, parts_2, swap_core(routing)
+        pos, gate = routing_tables(jnp.stack([routing, swap_core(routing)]))
+        far_a, far_b, core_a, core_b, parts_2, pos, gate = together(
+            far_a, far_b, core_a, core_b, parts_2, pos, gate
         )
-        pos, gate = routing_tables(jnp.stack([routing, core_routing]))
     with jax.named_scope("across_grads"):
         far_core_a, far_core_b = cores((far_a, far_b))
         grads_1, grads_2 = halves_of(parts_1), halves_of(parts_2)
         grads_a, grads_b = jnp.stack([grads_1[0], grads_2[0]]), jnp.stack([grads_1[1], grads_2[1]])
         far_grads = across(grads_a, grads_b)
-        far_core_a, far_core_b, pos, gate = together(far_core_a, far_core_b, pos, gate)
+        far_core_a, far_core_b, pos = together(far_core_a, far_core_b, pos)
     pieces = (near_a, far_a, core_a, far_core_a, near_b, far_b, core_b, far_core_b)
     rows, gate_pre, up_pre, scaled = kernel(
         up_kernel,
@@ -459,54 +469,51 @@
 
     own_1, other_1 = input_terms(0, grad_gate_pre, grad_up_pre)
     own_2, other_2 = input_terms(1, grad_gate_pre, grad_up_pre)
+    with jax.named_scope("gates"):
+        token_sums = token_sums + swap_side(token_sums)
     mix_first, other_1, other_2, token_sums = together(mix_first, other_1, other_2, token_sums)
     with jax.named_scope("across_mixed"):
         mix_send = sent_second(mix_own, mix_core, mix_first)
         mix_second = across(*mix_send)
     with jax.named_scope("cores_inputs"):
         core_1, core_2 = cores((other_1, other_2))
-    with jax.named_scope("gates"):
-        token_sums = token_sums + swap_side(token_sums)
     send_1, send_2 = sent_first(own_1, core_1), sent_first(own_2, core_2)
     scaled, mix_send = together(scaled, mix_send)
     (grad_down,) = weight_grads(grad_rows, scaled)
-    mix_second, send_1, send_2, token_sums, grad_down = together(
-        mix_second, send_1, send_2, token_sums, grad_down
-    )
+    send_1, send_2, grad_down = together(send_1, send_2, grad_down)
     with jax.named_scope("over_inputs_1"):
         first_1 = over(*send_1)
     with jax.named_scope("column_mixed"):
         mix_both = sent_column(mix_own, mix_core, mix_first, mix_second)
         mix_received = from_column(mix_both)
-    first_1, mix_both = together(first_1, mix_both)
-    with jax.named_scope("inputs_1_and_2"):
+    first_1, send_2, mix_received[::2] = together(first_1, send_2, mix_received[::2])
+    with jax.named_scope("across_inputs_1"):
         send_1 = sent_second(own_1, core_1, first_1)
-        to_side = jnp.concatenate([send_1[0][None], send_2[1]])
-        to_pair = jnp.concatenate([send_1[1][None], send_2[0]])
-        from_side, from_pair = swap_side(to_side), swap_pair(to_pair)
-    token_sums, grad_gate_pre, to_side, to_pair = together(token_sums, grad_gate_pre, to_side, to_pair)
+        second_1 = across(*send_1)
+    with jax.named_scope("over_inputs_2"):
+        send_1, send_2 = together(send_1, send_2)
+        first_2 = over(*send_2)
+    grad_gate_pre, send_2 = together(grad_gate_pre, send_2)
     grad_gate, grad_up = weight_grads(rows, grad_gate_pre, grad_up_pre)
-    with jax.named_scope("gates"):
-        expert_sums = sums_of_experts(token_sums)
-    from_side, from_pair, mix_received, grad_gate, grad_up = together(
-        from_side, from_pair, mix_received, grad_gate, grad_up
-    )
-    second_1, first_2 = (from_side[0], from_pair[0]), (from_pair[1:], from_side[1:])
+    second_1, mix_received, grad_gate, grad_up = together(second_1, mix_received, grad_gate, grad_up)
+    with jax.named_scope("column_inputs_1"):
+        both_1 = sent_column(own_1, core_1, first_1, second_1)
+        received_1 = from_column(both_1)
+    first_2, both_1 = together(first_2, both_1)
     with jax.named_scope("across_inputs_2"):
         send_2 = sent_second(own_2, core_2, first_2)
         second_2 = across(*send_2)
-    second_1, send_2 = together(second_1, send_2)
-    with jax.named_scope("column_inputs_1"):
-        both_1 = sent_column(own_1, core_1, first_1, second_1)
-        received_1 = from_column(both_1)
-    mix_received, both_1 = together(mix_received, both_1)
+    mix_received, send_2 = together(mix_received, send_2)
     mixed = column_sum(mix_both[0], mix_received)
-    second_2, mixed, expert_sums = together(second_2, mixed, expert_sums)
+    second_2, mixed = together(second_2, mixed)
     with jax.named_scope("column_inputs_2"):
         both_2 = sent_column(own_2, core_2, first_2, second_2)
         received_2 = from_column(both_2)
-    both_1, both_2 = together(both_1, both_2)
+    token_sums, both_1, both_2 = together(token_sums, both_1, both_2)
+    with jax.named_scope("gates"):
+        expert_sums = sums_of_experts(token_sums)
     grad_tokens_1 = column_sum(both_1[0], received_1)
+    received_2, expert_sums, grad_tokens_1 = together(received_2, expert_sums, grad_tokens_1)
     grad_tokens = jnp.concatenate([grad_tokens_1, column_sum(both_2[0], received_2)], axis=1)
 
     chosen = expert_ids[None] == jnp.arange(expert_count, dtype=jnp.int32)[:, None, None]

time: 241 us -> 232 us (0.963)
  waiting for transfers between devices: 88.6 us -> 82.4 us
  other arithmetic: 19.5 us -> 15.4 us
  starting transfers between devices: 62.5 us -> 66.5 us
  local copies, waits for them, and re-layouts: 12 us -> 9.05 us
    ppermute x18 -> x17, waiting for transfers between devices: 54.4 us -> 39.8 us  [shift(): lax.ppermute(value, 'expert', [(e, (e + 4 * step) % expert_count) for e i...]
    ppermute x0 -> x2, waiting for transfers between devices: none -> 8.38 us  [the longest x1 6.15 us: relayed_parts(): passed = lax.ppermute(jnp.where(me // 4 == 1, three, one), 'expert', outer)]
    ppermute x10 -> x11, waiting for transfers between devices: 13.9 us -> 7.31 us  [swap_pair(): return lax.ppermute(value, 'expert', chip_pairs)]
    all_to_all x1, waiting for transfers between devices: 0.01 us -> 6.31 us  [sums_of_experts(): lax.all_to_all(token_sums, 'expert', split_axis=0, concat_axis=0, tiled=T...]
    ppermute x0 -> x2, starting transfers between devices: none -> 4.15 us  [the longest x1 2.86 us: relayed_parts(): two = lax.ppermute(own, 'expert', inner)]
    another operation x6 -> x5, other arithmetic: 5.34 us -> 1.25 us  [sent_column(): return jnp.stack([a, b], axis=1)]
    ppermute x18 -> x17, starting transfers between devices: 32.7 us -> 29.3 us  [shift(): lax.ppermute(value, 'expert', [(e, (e + 4 * step) % expert_count) for e i...]
    ppermute x11 -> x12, waiting for transfers between devices: 11.4 us -> 14.5 us  [swap_side(): return lax.ppermute(value, 'tensor', [(0, 1), (1, 0)])]
  transfers between devices with their start and end apart: 54 -> 57, of which waited for: 23 -> 26; matrix products, arithmetic and copies ran while one was open for 9% -> 8% of each run, Pallas kernels for 23% -> 24%
where the time goes in v4:
time: 232 us; the launch traced here: 231 us
  waiting for transfers between devices  82.4 us (36%)
  starting transfers between devices  66.5 us (29%)
  Pallas kernels  54.9 us (24%)
  other arithmetic  15.4 us (7%)
  local copies, waits for them, and re-layouts  9.05 us (4%)
    ppermute x17, waiting for transfers between devices, shift(): lax.ppermute(value, 'expert', [(e, (e + 4 * step) % expert_count) for e i...  39.8 us
    ppermute x17, starting transfers between devices, shift(): lax.ppermute(value, 'expert', [(e, (e + 4 * step) % expert_count) for e i...  29.3 us
    ppermute x12, waiting for transfers between devices, swap_side(): return lax.ppermute(value, 'tensor', [(0, 1), (1, 0)])  14.5 us
    pallas_call x2, Pallas kernels, weight_grads(): pl.pallas_call(functools.partial(weight_kernel, len(lefts)), out_shape=[s...  14.1 us
    pallas_call x1, Pallas kernels, gather_body(): kernel(up_kernel, [table, table] + [piece_of(piece) for piece in pieces]...  13.7 us
    ppermute x12, starting transfers between devices, swap_side(): return lax.ppermute(value, 'tensor', [(0, 1), (1, 0)])  12.8 us
    ppermute x11, starting transfers between devices, swap_pair(): return lax.ppermute(value, 'expert', chip_pairs)  12.3 us
    pallas_call x2, Pallas kernels, input_terms(): kernel(input_kernel, [table, rows_of(hidden), rows_of(hidden)] + columns...  12.2 us
  transfers between devices with their start and end apart: 57, of which 26 were waited for; matrix products, arithmetic and copies ran while one was open for 8% of the time, Pallas kernels for 24%

profile of v4, /device:TPU:0, one launch (start us, length us, event | category | flops | bytes accessed | tf_op | source)
XLA Modules:
  0.0 231.4 jit_solution(17941721006743519888)
XLA Ops:
  3.1 3.1 %collective-permute-start = (bf16[264,512]{1,0:T(8,128)(2,1)S(1)}, bf16[264,512]{1,0:T(8,128)(2,1)S(1)}, u32[]{:S(2)}, u32[]{:S(2)}) collective-permute-start(bf16[264,512]{1,0:T(8,128)(2,1)S(1)} %pad_maximum_fusion.11), channel_id=1, source_target_pairs={{0,8},{2,10},{4,12},{6,14},{8,16},{10,18},{12,20},{14,22},{16,24},... | collective-permute-start | bytes 811016 | tf_op jit(solution)/shard_map/column_tokens/ppermute | solution.py:241
  6.2 2.1 collective-permute-start.2
  8.3 2.9 %collective-permute-start.1 = (bf16[264,512]{1,0:T(8,128)(2,1)S(1)}, bf16[264,512]{1,0:T(8,128)(2,1)S(1)}, u32[]{:S(2)}, u32[]{:S(2)}) collective-permute-start(bf16[264,512]{1,0:T(8,128)(2,1)S(1)} %pad_maximum_fusion.11), channel_id=1, source_target_pairs={{0,16},{2,18},{4,20},{6,22},{24,8},{26,10},{28,12},{30,14},{1,17},... | collective-permute-start | bytes 811016 | tf_op jit(solution)/shard_map/column_tokens/ppermute | solution.py:261
  11.2 4.4 %collective-permute-done = bf16[264,512]{1,0:T(8,128)(2,1)S(1)} collective-permute-done((bf16[264,512]{1,0:T(8,128)(2,1)S(1)}, bf16[264,512]{1,0:T(8,128)(2,1)S(1)}, u32[]{:S(2)}, u32[]{:S(2)}) %collective-permute-start) | collective-permute-done | bytes 270368 | tf_op jit(solution)/shard_map/column_tokens/ppermute | solution.py:241
  15.6 4.4 %collective-permute-done.2 = bf16[264,512]{1,0:T(8,128)(2,1)S(1)} collective-permute-done((bf16[264,512]{1,0:T(8,128)(2,1)S(1)}, bf16[264,512]{1,0:T(8,128)(2,1)S(1)}, u32[]{:S(2)}, u32[]{:S(2)}) %collective-permute-start.2) | collective-permute-done | bytes 270368 | tf_op jit(solution)/shard_map/column_tokens/ppermute | solution.py:241
  20.0 1.3 collective-permute-start.3
  21.4 2.2 collective-permute-done.1
  23.6 6.1 %collective-permute-done.3 = bf16[264,512]{1,0:T(8,128)(2,1)S(1)} collective-permute-done((bf16[264,512]{1,0:T(8,128)(2,1)S(1)}, bf16[264,512]{1,0:T(8,128)(2,1)S(1)}, u32[]{:S(2)}, u32[]{:S(2)}) %collective-permute-start.3) | collective-permute-done | bytes 270368 | tf_op jit(solution)/shard_map/column_tokens/ppermute | solution.py:263
  30.0 1.8 collective-permute-start.5
  32.7 1.5 collective-permute-start.4
  34.7 5.9 %collective-permute-start.7 = (bf16[2,128,256]{2,1,0:T(8,128)(2,1)S(1)}, bf16[2,128,256]{2,1,0:T(8,128)(2,1)S(1)}, u32[]{:S(2)}, u32[]{:S(2)}) collective-permute-start(bf16[2,128,256]{2,1,0:T(8,128)(2,1)S(1)} %get-tuple-element.122), channel_id=1, source_target_pairs={{0,16},{2,18},{4,20},{6,22},{8,24},{10,26},{12,28},{14,30},{16,0},... | collective-permute-start | bytes 393224 | tf_op jit(solution)/shard_map/across_tokens/ppermute | solution.py:241
  41.2 2.0 collective-permute-done.6
  43.2 3.3 %collective-permute-done.7 = bf16[2,128,256]{2,1,0:T(8,128)(2,1)S(1)} collective-permute-done((bf16[2,128,256]{2,1,0:T(8,128)(2,1)S(1)}, bf16[2,128,256]{2,1,0:T(8,128)(2,1)S(1)}, u32[]{:S(2)}, u32[]{:S(2)}) %collective-permute-start.7) | collective-permute-done | bytes 131104 | tf_op jit(solution)/shard_map/across_tokens/ppermute | solution.py:241
  54.7 5.1 %collective-permute-done.13 = bf16[2,128,256]{2,1,0:T(8,128)(2,1)} collective-permute-done((bf16[2,128,256]{2,1,0:T(8,128)(2,1)S(1)}, bf16[2,128,256]{2,1,0:T(8,128)(2,1)}, u32[]{:S(2)}, u32[]{:S(2)}) %collective-permute-start.13) | collective-permute-done | bytes 131104 | tf_op jit(solution)/shard_map/over_tokens/ppermute | solution.py:241
  61.0 5.9 %collective-permute-done.14 = bf16[2,128,256]{2,1,0:T(8,128)(2,1)} collective-permute-done((bf16[2,128,256]{2,1,0:T(8,128)(2,1)S(1)}, bf16[2,128,256]{2,1,0:T(8,128)(2,1)}, u32[]{:S(2)}, u32[]{:S(2)}) %collective-permute-start.14) | collective-permute-done | bytes 131104 | tf_op jit(solution)/shard_map/over_tokens/ppermute | solution.py:241
  66.9 1.3 collective-permute-start.15
  68.1 1.6 fusion.pos
  69.7 2.4 %collective-permute-done.15 = bf16[2,128,256]{2,1,0:T(8,128)(2,1)S(1)} collective-permute-done((bf16[2,128,256]{2,1,0:T(8,128)(2,1)S(1)}, bf16[2,128,256]{2,1,0:T(8,128)(2,1)S(1)}, u32[]{:S(2)}, u32[]{:S(2)}) %collective-permute-start.15) | collective-permute-done | bytes 131104 | tf_op jit(solution)/shard_map/over_tokens/ppermute | solution.py:241
  72.2 2.7 %collective-permute-done.9.refs_1_ = bf16[2,4,128,512]{3,2,1,0:T(8,128)(2,1)} collective-permute-done((bf16[2,4,128,512]{3,2,1,0:T(8,128)(2,1)S(1)}, bf16[2,4,128,512]{3,2,1,0:T(8,128)(2,1)}, u32[]{:S(2)}, u32[]{:S(2)}) %collective-permute-start.9) | collective-permute-done | bytes 1048608 | tf_op jit(solution)/shard_map/over_tokens/ppermute | solution.py:235
  78.7 1.3 collective-permute-start.19
  80.6 13.7 %shard_map.118 = (bf16[1024,2048]{1,0:T(8,128)(2,1)}, f32[1024,704]{1,0:T(8,128)}, f32[1024,704]{1,0:T(8,128)}, bf16[1024,704]{1,0:T(8,128)(2,1)}) custom-call(s32[1]{0:T(128)} %bitcast.side, f32[4,4,128]{2,1,0:T(4,128)} %fusion.pos, f32[4,4,128]{2,1,0:T(4,128)} %copy.49.gate, bf16[2,4,128,512]{3,2,1,0:T(8,128)(2,1)} %copy-done.12, ...), custom_call_target="tpu_custom_call" | custom-call | flops 1048576 | bytes 65536 | tf_op jit(solution)/shard_map/pallas_call | solution.py:416
  96.1 1.8 collective-permute-start.21
  97.9 7.2 %shard_map.119 = (bf16[2,2,2,4,128,512]{5,4,3,2,1,0:T(8,128)(2,1)S(1)}, bf16[2,2,2,4,128,512]{5,4,3,2,1,0:T(8,128)(2,1)S(1)}) custom-call(s32[1]{0:T(128)} %bitcast.side, f32[4,4,128]{2,1,0:T(4,128)S(1)} %copy-done.9, bf16[1024,704]{1,0:T(8,128)(2,1)S(1)} %copy-done.3, bf16[704,2048]{1,0:T(8,128)(2,1)S(1)} %bitcast.246), custom_call_target="tpu_custom_call" | custom-call | flops 1048576 | bytes 65536 | tf_op jit(solution)/shard_map/pallas_call | solution.py:428
  105.1 4.1 %collective-permute-done.22.refs_5_ = bf16[2,4,128,256]{3,2,1,0:T(8,128)(2,1)S(1)} collective-permute-done((bf16[2,4,128,256]{3,2,1,0:T(8,128)(2,1)S(1)}, bf16[2,4,128,256]{3,2,1,0:T(8,128)(2,1)S(1)}, u32[]{:S(2)}, u32[]{:S(2)}) %collective-permute-start.22) | collective-permute-done | bytes 524320 | tf_op jit(solution)/shard_map/over_grads_1/ppermute | solution.py:238
  110.4 1.8 collective-permute-start.28
  112.2 1.3 collective-permute-start.29
  113.5 3.4 %collective-permute-done.27 = bf16[2,2,2,4,128,512]{5,4,3,2,1,0:T(8,128)(2,1)S(1)} collective-permute-done((bf16[2,2,2,4,128,512]{5,4,3,2,1,0:T(8,128)(2,1)S(1)}, bf16[2,2,2,4,128,512]{5,4,3,2,1,0:T(8,128)(2,1)S(1)}, u32[]{:S(2)}, u32[]{:S(2)}) %collective-permute-start.27) | collective-permute-done | bytes 4194336 | tf_op jit(solution)/shard_map/cores_mixed/ppermute | solution.py:232
  116.9 2.0 fusion.2
  120.1 1.8 collective-permute-start.32
  123.1 2.1 collective-permute-done.28.refs_9_
  125.2 1.9 collective-permute-done.29.refs_13_
  129.7 7.7 %shard_map.120 = (bf16[1024,2048]{1,0:T(8,128)(2,1)S(1)}, bf16[1024,704]{1,0:T(8,128)(2,1)S(1)}, bf16[1024,704]{1,0:T(8,128)(2,1)S(1)}, f32[4,4,128]{2,1,0:T(4,128)S(1)}) custom-call(s32[1]{0:T(128)} %bitcast.side, f32[4,4,128]{2,1,0:T(4,128)S(1)} %copy-done.9, f32[4,4,128]{2,1,0:T(4,128)S(1)} %copy-done.10, ...), custom_call_target="tpu_custom_call" | custom-call | flops 1048576 | bytes 65536 | tf_op jit(solution)/shard_map/pallas_call | solution.py:452
  137.5 1.3 collective-permute-start.34
  138.7 6.1 %shard_map.121 = (bf16[2,2,2,4,128,256]{5,4,3,2,1,0:T(8,128)(2,1)S(1)}, bf16[2,2,2,4,128,256]{5,4,3,2,1,0:T(8,128)(2,1)S(1)}) custom-call(s32[1]{0:T(128)} %bitcast.side, f32[4,4,128]{2,1,0:T(4,128)S(1)} %copy-done.9, bf16[1024,704]{1,0:T(8,128)(2,1)S(1)} %get-tuple-element.180.grad_gate_pre.refs_0_, ...), custom_call_target="tpu_custom_call" | custom-call | flops 1048576 | bytes 65536 | tf_op jit(solution)/shard_map/pallas_call | solution.py:463
  144.9 6.1 %shard_map.122 = (bf16[2,2,2,4,128,256]{5,4,3,2,1,0:T(8,128)(2,1)S(1)}, bf16[2,2,2,4,128,256]{5,4,3,2,1,0:T(8,128)(2,1)S(1)}) custom-call(s32[1]{0:T(128)} %bitcast.side, f32[4,4,128]{2,1,0:T(4,128)S(1)} %copy-done.9, bf16[1024,704]{1,0:T(8,128)(2,1)S(1)} %get-tuple-element.180.grad_gate_pre.refs_0_, ...), custom_call_target="tpu_custom_call" | custom-call | flops 1048576 | bytes 65536 | tf_op jit(solution)/shard_map/pallas_call | solution.py:463
  153.2 5.4 %shard_map.123 = bf16[704,2048]{1,0:T(8,128)(2,1)} custom-call(bf16[1024,704]{1,0:T(8,128)(2,1)S(1)} %copy-done.3, bf16[1024,2048]{1,0:T(8,128)(2,1)S(1)} %get-tuple-element.167.refs_1_), custom_call_target="tpu_custom_call" | custom-call | flops 1048576 | bytes 65536 | tf_op jit(solution)/shard_map/pallas_call | solution.py:365
  159.3 1.8 collective-permute-start.37
  162.3 4.6 %collective-permute-done.39 = bf16[4,128,512]{2,1,0:T(8,128)(2,1)S(1)} collective-permute-done((bf16[4,128,512]{2,1,0:T(8,128)(2,1)S(1)}, bf16[4,128,512]{2,1,0:T(8,128)(2,1)S(1)}, u32[]{:S(2)}, u32[]{:S(2)}) %collective-permute-start.39) | collective-permute-done | bytes 524320 | tf_op jit(solution)/shard_map/across_mixed/ppermute | solution.py:238
  168.5 2.0 collective-permute-start.41
  171.3 9.3 %collective-permute-done.41 = bf16[2,128,512]{2,1,0:T(8,128)(2,1)S(1)} collective-permute-done((bf16[2,128,512]{2,1,0:T(8,128)(2,1)S(1)}, bf16[2,128,512]{2,1,0:T(8,128)(2,1)S(1)}, u32[]{:S(2)}, u32[]{:S(2)}) %collective-permute-start.41) | collective-permute-done | bytes 262176 | tf_op jit(solution)/shard_map/column_mixed/ppermute | solution.py:241
  180.7 2.4 %collective-permute-done.42 = bf16[2,128,512]{2,1,0:T(8,128)(2,1)S(1)} collective-permute-done((bf16[2,128,512]{2,1,0:T(8,128)(2,1)S(1)}, bf16[2,128,512]{2,1,0:T(8,128)(2,1)S(1)}, u32[]{:S(2)}, u32[]{:S(2)}) %collective-permute-start.42) | collective-permute-done | bytes 262176 | tf_op jit(solution)/shard_map/column_mixed/ppermute | solution.py:241
  185.0 1.7 collective-permute-start.43
  187.5 8.8 %shard_map.124 = (bf16[704,2048]{1,0:T(8,128)(2,1)}, bf16[704,2048]{1,0:T(8,128)(2,1)}) custom-call(bf16[1024,704]{1,0:T(8,128)(2,1)S(1)} %get-tuple-element.180.grad_gate_pre.refs_0_, bf16[1024,704]{1,0:T(8,128)(2,1)S(1)} %get-tuple-element.156.grad_up_pre.refs_1_, bf16[1024,2048]{1,0:T(8,128)(2,1)S(1)} %copy-done.4), custom_call_target="tpu_custom_call" | custom-call | flops 1048576 | bytes 65536 | tf_op jit(solution)/shard_map/pallas_call | solution.py:365
  196.7 8.2 %collective-permute-start.54 = (bf16[2,128,256]{2,1,0:T(8,128)(2,1)S(1)}, bf16[2,128,256]{2,1,0:T(8,128)(2,1)S(1)}, u32[]{:S(2)}, u32[]{:S(2)}) collective-permute-start(bf16[2,128,256]{2,1,0:T(8,128)(2,1)S(1)} %get-tuple-element.235), channel_id=1, source_target_pairs={{0,16},{2,18},{4,20},{6,22},{8,24},{10,26},{12,28},{14,30},{16,0},... | collective-permute-start | bytes 393224 | tf_op jit(solution)/shard_map/column_inputs_1/ppermute | solution.py:241
  207.8 3.8 %collective-permute-done.48 = bf16[4,128,256]{2,1,0:T(8,128)(2,1)S(1)} collective-permute-done((bf16[4,128,256]{2,1,0:T(8,128)(2,1)S(1)}, bf16[4,128,256]{2,1,0:T(8,128)(2,1)S(1)}, u32[]{:S(2)}, u32[]{:S(2)}) %collective-permute-start.48) | collective-permute-done | bytes 262176 | tf_op jit(solution)/shard_map/across_inputs_2/ppermute | solution.py:238
  213.3 3.9 %collective-permute-start.50 = (bf16[2,128,256]{2,1,0:T(8,128)(2,1)S(1)}, bf16[2,128,256]{2,1,0:T(8,128)(2,1)S(1)}, u32[]{:S(2)}, u32[]{:S(2)}) collective-permute-start(bf16[2,128,256]{2,1,0:T(8,128)(2,1)S(1)} %get-tuple-element.238), channel_id=1, source_target_pairs={{0,24},{2,26},{4,28},{6,30},{8,0},{10,2},{12,4},{14,6},{16,8},{18,... | collective-permute-start | bytes 393224 | tf_op jit(solution)/shard_map/column_inputs_2/ppermute | solution.py:241
  219.1 4.6 %all-to-all-start = ((f32[16,1,128]{2,1,0:T(1,128)}), f32[16,1,128]{2,1,0:T(1,128)S(1)}, u32[]{:S(2)}, u32[]{:S(2)}) async-start(f32[16,1,128]{2,1,0:T(1,128)} %bitcast.94), calls=%async_computation | async-start | bytes 16384 | tf_op jit(solution)/shard_map/gates/all_to_all | solution.py:301
  223.7 6.3 %all-to-all-done = f32[16,1,128]{2,1,0:T(1,128)S(1)} async-done(((f32[16,1,128]{2,1,0:T(1,128)}), f32[16,1,128]{2,1,0:T(1,128)S(1)}, u32[]{:S(2)}, u32[]{:S(2)}) %all-to-all-start) | async-done | bytes 8224 | tf_op jit(solution)/shard_map/gates/all_to_all | solution.py:301
  (207 shorter events, 43.7 us)
Async XLA Ops:
  3.1 12.5 %collective-permute-start = (bf16[264,512]{1,0:T(8,128)(2,1)S(1)}, bf16[264,512]{1,0:T(8,128)(2,1)S(1)}, u32[]{:S(2)}, u32[]{:S(2)}) collective-permute-start(bf16[264,512]{1,0:T(8,128)(2,1)S(1)} %pad_maximum_fusion.11), channel_id=1, source_target_pairs={{0,8},{2,10},{4,12},{6,14},{8,16},{10,18},{12,20},{14,22},{16,24},... | collective-permute-start | bytes 811016 | tf_op jit(solution)/shard_map/column_tokens/ppermute | solution.py:241
  6.2 13.7 %collective-permute-start.2 = (bf16[264,512]{1,0:T(8,128)(2,1)S(1)}, bf16[264,512]{1,0:T(8,128)(2,1)S(1)}, u32[]{:S(2)}, u32[]{:S(2)}) collective-permute-start(bf16[264,512]{1,0:T(8,128)(2,1)S(1)} %pad_maximum_fusion.11), channel_id=1, source_target_pairs={{0,24},{2,26},{4,28},{6,30},{8,0},{10,2},{12,4},{14,6},{16,8},{18,... | collective-permute-start | bytes 811016 | tf_op jit(solution)/shard_map/column_tokens/ppermute | solution.py:241
  8.3 15.3 %collective-permute-start.1 = (bf16[264,512]{1,0:T(8,128)(2,1)S(1)}, bf16[264,512]{1,0:T(8,128)(2,1)S(1)}, u32[]{:S(2)}, u32[]{:S(2)}) collective-permute-start(bf16[264,512]{1,0:T(8,128)(2,1)S(1)} %pad_maximum_fusion.11), channel_id=1, source_target_pairs={{0,16},{2,18},{4,20},{6,22},{24,8},{26,10},{28,12},{30,14},{1,17},... | collective-permute-start | bytes 811016 | tf_op jit(solution)/shard_map/column_tokens/ppermute | solution.py:261
  20.0 9.8 %collective-permute-start.3 = (bf16[264,512]{1,0:T(8,128)(2,1)S(1)}, bf16[264,512]{1,0:T(8,128)(2,1)S(1)}, u32[]{:S(2)}, u32[]{:S(2)}) collective-permute-start(bf16[264,512]{1,0:T(8,128)(2,1)S(1)} %broadcast_select_fusion), channel_id=1, source_target_pairs={{8,0},{10,2},{12,4},{14,6},{16,24},{18,26},{20,28},{22,30},{9,1},{... | collective-permute-start | bytes 811016 | tf_op jit(solution)/shard_map/column_tokens/ppermute | solution.py:263
  30.0 17.0 %collective-permute-start.5 = (bf16[4,136,512]{2,1,0:T(8,128)(2,1)S(1)}, bf16[4,136,512]{2,1,0:T(8,128)(2,1)S(1)}, u32[]{:S(2)}, u32[]{:S(2)}) collective-permute-start(bf16[4,136,512]{2,1,0:T(8,128)(2,1)S(1)} %pad_maximum_fusion.7), channel_id=1, source_target_pairs={{0,4},{2,6},{4,0},{6,2},{8,12},{10,14},{12,8},{14,10},{16,20},{18,... | collective-permute-start | bytes 1671176 | tf_op jit(solution)/shard_map/across_tokens/ppermute | solution.py:235
  32.7 14.3 %collective-permute-start.4 = (bf16[4,128,512]{2,1,0:T(8,128)(2,1)S(1)}, bf16[4,128,512]{2,1,0:T(8,128)(2,1)S(1)}, u32[]{:S(2)}, u32[]{:S(2)}) collective-permute-start(bf16[4,128,512]{2,1,0:T(8,128)(2,1)S(1)} %get-tuple-element.244), channel_id=1, source_target_pairs={{0,1},{1,0},{2,3},{3,2},{4,5},{5,4},{6,7},{7,6},{8,9},{9,8},{10,11... | collective-permute-start | bytes 1572872 | tf_op jit(solution)/shard_map/across_tokens/ppermute | solution.py:238
  34.7 8.4 %collective-permute-start.6 = (bf16[2,128,256]{2,1,0:T(8,128)(2,1)S(1)}, bf16[2,128,256]{2,1,0:T(8,128)(2,1)S(1)}, u32[]{:S(2)}, u32[]{:S(2)}) collective-permute-start(bf16[2,128,256]{2,1,0:T(8,128)(2,1)S(1)} %get-tuple-element.122), channel_id=1, source_target_pairs={{0,8},{2,10},{4,12},{6,14},{8,16},{10,18},{12,20},{14,22},{16,24},... | collective-permute-start | bytes 393224 | tf_op jit(solution)/shard_map/across_tokens/ppermute | solution.py:241
  34.7 11.7 %collective-permute-start.7 = (bf16[2,128,256]{2,1,0:T(8,128)(2,1)S(1)}, bf16[2,128,256]{2,1,0:T(8,128)(2,1)S(1)}, u32[]{:S(2)}, u32[]{:S(2)}) collective-permute-start(bf16[2,128,256]{2,1,0:T(8,128)(2,1)S(1)} %get-tuple-element.122), channel_id=1, source_target_pairs={{0,16},{2,18},{4,20},{6,22},{8,24},{10,26},{12,28},{14,30},{16,0},... | collective-permute-start | bytes 393224 | tf_op jit(solution)/shard_map/across_tokens/ppermute | solution.py:241
  48.0 24.2 %collective-permute-start.10 = (bf16[2,4,128,512]{3,2,1,0:T(8,128)(2,1)S(1)}, bf16[2,4,128,512]{3,2,1,0:T(8,128)(2,1)}, u32[]{:S(2)}, u32[]{:S(2)}) collective-permute-start(bf16[2,4,128,512]{3,2,1,0:T(8,128)(2,1)S(1)} %pad_maximum_fusion.4.refs_4_), channel_id=1, source_target_pairs={{0,1},{1,0},{2,3},{3,2},{4,5},{5,4},{6,7},{7,6},{8,9},{9,8},{10,11... | collective-permute-start | bytes 3145736 | tf_op jit(solution)/shard_map/over_tokens/ppermute | solution.py:238
  48.1 24.1 %collective-permute-start.12 = (bf16[2,4,128,512]{3,2,1,0:T(8,128)(2,1)S(1)}, bf16[2,4,128,512]{3,2,1,0:T(8,128)(2,1)S(1)}, u32[]{:S(2)}, u32[]{:S(2)}) collective-permute-start(bf16[2,4,128,512]{3,2,1,0:T(8,128)(2,1)S(1)} %pad_maximum_fusion.4.refs_4_), channel_id=1, source_target_pairs={{0,2},{2,0},{4,6},{6,4},{8,10},{10,8},{12,14},{14,12},{16,18},{18,... | collective-permute-start | bytes 3145736 | tf_op jit(solution)/shard_map/over_tokens/ppermute | solution.py:232
  49.1 23.1 %collective-permute-start.11 = (bf16[2,4,128,512]{3,2,1,0:T(8,128)(2,1)S(1)}, bf16[2,4,128,512]{3,2,1,0:T(8,128)(2,1)}, u32[]{:S(2)}, u32[]{:S(2)}) collective-permute-start(bf16[2,4,128,512]{3,2,1,0:T(8,128)(2,1)S(1)} %pad_maximum_fusion.3.refs_0_), channel_id=1, source_target_pairs={{0,2},{2,0},{4,6},{6,4},{8,10},{10,8},{12,14},{14,12},{16,18},{18,... | collective-permute-start | bytes 3145736 | tf_op jit(solution)/shard_map/over_tokens/ppermute | solution.py:232
  49.2 25.7 %collective-permute-start.9 = (bf16[2,4,128,512]{3,2,1,0:T(8,128)(2,1)S(1)}, bf16[2,4,128,512]{3,2,1,0:T(8,128)(2,1)}, u32[]{:S(2)}, u32[]{:S(2)}) collective-permute-start(bf16[2,4,128,512]{3,2,1,0:T(8,128)(2,1)S(1)} %pad_maximum_fusion.3.refs_0_), channel_id=1, source_target_pairs={{0,4},{2,6},{4,0},{6,2},{8,12},{10,14},{12,8},{14,10},{16,20},{18,... | collective-permute-start | bytes 3145736 | tf_op jit(solution)/shard_map/over_tokens/ppermute | solution.py:235
  52.0 7.7 %collective-permute-start.13 = (bf16[2,128,256]{2,1,0:T(8,128)(2,1)S(1)}, bf16[2,128,256]{2,1,0:T(8,128)(2,1)}, u32[]{:S(2)}, u32[]{:S(2)}) collective-permute-start(bf16[2,128,256]{2,1,0:T(8,128)(2,1)S(1)} %get-tuple-element.126), channel_id=1, source_target_pairs={{0,8},{2,10},{4,12},{6,14},{8,16},{10,18},{12,20},{14,22},{16,24},... | collective-permute-start | bytes 393224 | tf_op jit(solution)/shard_map/over_tokens/ppermute | solution.py:241
  59.7 7.1 %collective-permute-start.14 = (bf16[2,128,256]{2,1,0:T(8,128)(2,1)S(1)}, bf16[2,128,256]{2,1,0:T(8,128)(2,1)}, u32[]{:S(2)}, u32[]{:S(2)}) collective-permute-start(bf16[2,128,256]{2,1,0:T(8,128)(2,1)S(1)} %get-tuple-element.126), channel_id=1, source_target_pairs={{0,16},{2,18},{4,20},{6,22},{8,24},{10,26},{12,28},{14,30},{16,0},... | collective-permute-start | bytes 393224 | tf_op jit(solution)/shard_map/over_tokens/ppermute | solution.py:241
  78.3 16.0 %collective-permute-start.20 = (bf16[2,4,128,256]{3,2,1,0:T(8,128)(2,1)S(1)}, bf16[2,4,128,256]{3,2,1,0:T(8,128)(2,1)S(1)}, u32[]{:S(2)}, u32[]{:S(2)}) collective-permute-start(bf16[2,4,128,256]{3,2,1,0:T(8,128)(2,1)S(1)} %get-tuple-element.240), channel_id=1, source_target_pairs={{0,4},{2,6},{4,0},{6,2},{8,12},{10,14},{12,8},{14,10},{16,20},{18,... | collective-permute-start | bytes 1572872 | tf_op jit(solution)/shard_map/across_grads/ppermute | solution.py:235
  78.7 15.6 %collective-permute-start.19 = (bf16[2,4,128,256]{3,2,1,0:T(8,128)(2,1)S(1)}, bf16[2,4,128,256]{3,2,1,0:T(8,128)(2,1)S(1)}, u32[]{:S(2)}, u32[]{:S(2)}) collective-permute-start(bf16[2,4,128,256]{3,2,1,0:T(8,128)(2,1)S(1)} %get-tuple-element.241), channel_id=1, source_target_pairs={{0,1},{1,0},{2,3},{3,2},{4,5},{5,4},{6,7},{7,6},{8,9},{9,8},{10,11... | collective-permute-start | bytes 1572872 | tf_op jit(solution)/shard_map/across_grads/ppermute | solution.py:238
  94.4 15.3 %collective-permute-start.24 = (bf16[2,2,4,128,256]{4,3,2,1,0:T(8,128)(2,1)S(1)}, bf16[2,2,4,128,256]{4,3,2,1,0:T(8,128)(2,1)S(1)}, u32[]{:S(2)}, u32[]{:S(2)}) collective-permute-start(bf16[2,2,4,128,256]{4,3,2,1,0:T(8,128)(2,1)S(1)} %pad_maximum_fusion.2.refs_4_.refs_12_), channel_id=1, source_target_pairs={{0,2},{2,0},{4,6},{6,4},{8,10},{10,8},{12,14},{14,12},{16,18},{18,... | collective-permute-start | bytes 3145736 | tf_op jit(solution)/shard_map/over_grads_1/ppermute | solution.py:232
  94.6 15.1 %collective-permute-start.23 = (bf16[2,2,4,128,256]{4,3,2,0,1:T(8,128)(2,1)S(1)}, bf16[2,2,4,128,256]{4,3,2,0,1:T(8,128)(2,1)S(1)}, u32[]{:S(2)}, u32[]{:S(2)}) collective-permute-start(bf16[2,2,4,128,256]{4,3,2,0,1:T(8,128)(2,1)S(1)} %pad_maximum_fusion.1), channel_id=1, source_target_pairs={{0,2},{2,0},{4,6},{6,4},{8,10},{10,8},{12,14},{14,12},{16,18},{18,... | collective-permute-start | bytes 3145736 | tf_op jit(solution)/shard_map/over_grads_1/ppermute | solution.py:232
  95.3 13.9 %collective-permute-start.22 = (bf16[2,4,128,256]{3,2,1,0:T(8,128)(2,1)S(1)}, bf16[2,4,128,256]{3,2,1,0:T(8,128)(2,1)S(1)}, u32[]{:S(2)}, u32[]{:S(2)}) collective-permute-start(bf16[2,4,128,256]{3,2,1,0:T(8,128)(2,1)S(1)} %fusion.14), channel_id=1, source_target_pairs={{0,1},{1,0},{2,3},{3,2},{4,5},{5,4},{6,7},{7,6},{8,9},{9,8},{10,11... | collective-permute-start | bytes 1572872 | tf_op jit(solution)/shard_map/over_grads_1/ppermute | solution.py:238
  96.1 13.6 %collective-permute-start.21 = (bf16[2,4,128,256]{3,2,1,0:T(8,128)(2,1)S(1)}, bf16[2,4,128,256]{3,2,1,0:T(8,128)(2,1)S(1)}, u32[]{:S(2)}, u32[]{:S(2)}) collective-permute-start(bf16[2,4,128,256]{3,2,1,0:T(8,128)(2,1)S(1)} %fusion.16), channel_id=1, source_target_pairs={{0,4},{2,6},{4,0},{6,2},{8,12},{10,14},{12,8},{14,10},{16,20},{18,... | collective-permute-start | bytes 1572872 | tf_op jit(solution)/shard_map/over_grads_1/ppermute | solution.py:235
  109.7 7.2 %collective-permute-start.27 = (bf16[2,2,2,4,128,512]{5,4,3,2,1,0:T(8,128)(2,1)S(1)}, bf16[2,2,2,4,128,512]{5,4,3,2,1,0:T(8,128)(2,1)S(1)}, u32[]{:S(2)}, u32[]{:S(2)}) collective-permute-start(bf16[2,2,2,4,128,512]{5,4,3,2,1,0:T(8,128)(2,1)S(1)} %get-tuple-element.144), channel_id=1, source_target_pairs={{0,2},{2,0},{4,6},{6,4},{8,10},{10,8},{12,14},{14,12},{16,18},{18,... | collective-permute-start | bytes 12582920 | tf_op jit(solution)/shard_map/cores_mixed/ppermute | solution.py:232
  109.7 10.3 %collective-permute-start.25 = (bf16[2,4,128,256]{3,2,1,0:T(8,128)(2,1)S(1)}, bf16[2,4,128,256]{3,2,1,0:T(8,128)(2,1)S(1)}, u32[]{:S(2)}, u32[]{:S(2)}) collective-permute-start(bf16[2,4,128,256]{3,2,1,0:T(8,128)(2,1)S(1)} %collective-permute-done.21.refs_1_), channel_id=1, source_target_pairs={{0,2},{2,0},{4,6},{6,4},{8,10},{10,8},{12,14},{14,12},{16,18},{18,... | collective-permute-start | bytes 1572872 | tf_op jit(solution)/shard_map/cores_mixed/ppermute | solution.py:232
  110.2 9.8 %collective-permute-start.26 = (bf16[2,4,128,256]{3,2,1,0:T(8,128)(2,1)S(1)}, bf16[2,4,128,256]{3,2,1,0:T(8,128)(2,1)S(1)}, u32[]{:S(2)}, u32[]{:S(2)}) collective-permute-start(bf16[2,4,128,256]{3,2,1,0:T(8,128)(2,1)S(1)} %collective-permute-done.22.refs_5_), channel_id=1, source_target_pairs={{0,2},{2,0},{4,6},{6,4},{8,10},{10,8},{12,14},{14,12},{16,18},{18,... | collective-permute-start | bytes 1572872 | tf_op jit(solution)/shard_map/cores_mixed/ppermute | solution.py:232
  110.4 14.8 %collective-permute-start.28 = (bf16[2,4,128,256]{3,2,1,0:T(8,128)(2,1)S(1)}, bf16[2,4,128,256]{3,2,1,0:T(8,128)(2,1)S(1)}, u32[]{:S(2)}, u32[]{:S(2)}) collective-permute-start(bf16[2,4,128,256]{3,2,1,0:T(8,128)(2,1)S(1)} %slice_bitcast_fusion.2), channel_id=1, source_target_pairs={{0,4},{2,6},{4,0},{6,2},{8,12},{10,14},{12,8},{14,10},{16,20},{18,... | collective-permute-start | bytes 1572872 | tf_op jit(solution)/shard_map/over_grads_2/ppermute | solution.py:235
  112.2 14.8 %collective-permute-start.29 = (bf16[2,4,128,256]{3,2,1,0:T(8,128)(2,1)S(1)}, bf16[2,4,128,256]{3,2,1,0:T(8,128)(2,1)S(1)}, u32[]{:S(2)}, u32[]{:S(2)}) collective-permute-start(bf16[2,4,128,256]{3,2,1,0:T(8,128)(2,1)S(1)} %slice_bitcast_fusion.1), channel_id=1, source_target_pairs={{0,1},{1,0},{2,3},{3,2},{4,5},{5,4},{6,7},{7,6},{8,9},{9,8},{10,11... | collective-permute-start | bytes 1572872 | tf_op jit(solution)/shard_map/over_grads_2/ppermute | solution.py:238
  120.1 31.0 %collective-permute-start.32 = (bf16[2,4,128,512]{3,2,1,0:T(8,128)(2,1)}, bf16[2,4,128,512]{3,2,1,0:T(8,128)(2,1)S(1)}, u32[]{:S(2)}, u32[]{:S(2)}) collective-permute-start(bf16[2,4,128,512]{3,2,1,0:T(8,128)(2,1)} %get-tuple-element.149), channel_id=1, source_target_pairs={{0,4},{2,6},{4,0},{6,2},{8,12},{10,14},{12,8},{14,10},{16,20},{18,... | collective-permute-start | bytes 3145736 | tf_op jit(solution)/shard_map/over_mixed/ppermute | solution.py:235
  121.9 29.2 %collective-permute-start.33 = (bf16[2,4,128,512]{3,2,1,0:T(8,128)(2,1)}, bf16[2,4,128,512]{3,2,1,0:T(8,128)(2,1)S(1)}, u32[]{:S(2)}, u32[]{:S(2)}) collective-permute-start(bf16[2,4,128,512]{3,2,1,0:T(8,128)(2,1)} %get-tuple-element.150), channel_id=1, source_target_pairs={{0,1},{1,0},{2,3},{3,2},{4,5},{5,4},{6,7},{7,6},{8,9},{9,8},{10,11... | collective-permute-start | bytes 3145736 | tf_op jit(solution)/shard_map/over_mixed/ppermute | solution.py:238
  137.5 13.5 %collective-permute-start.34 = (f32[4,4,128]{2,1,0:T(4,128)S(1)}, f32[4,4,128]{2,1,0:T(4,128)S(1)}, u32[]{:S(2)}, u32[]{:S(2)}) collective-permute-start(f32[4,4,128]{2,1,0:T(4,128)S(1)} %get-tuple-element.160), channel_id=1, source_target_pairs={{0,1},{1,0},{2,3},{3,2},{4,5},{5,4},{6,7},{7,6},{8,9},{9,8},{10,11... | collective-permute-start | bytes 24584 | tf_op jit(solution)/shard_map/gates/ppermute | solution.py:238
  151.0 7.6 %collective-permute-start.35 = (bf16[2,2,2,4,128,256]{5,4,3,2,1,0:T(8,128)(2,1)S(1)}, bf16[2,2,2,4,128,256]{5,4,3,2,1,0:T(8,128)(2,1)S(1)}, u32[]{:S(2)}, u32[]{:S(2)}) collective-permute-start(bf16[2,2,2,4,128,256]{5,4,3,2,1,0:T(8,128)(2,1)S(1)} %get-tuple-element.161), channel_id=1, source_target_pairs={{0,2},{2,0},{4,6},{6,4},{8,10},{10,8},{12,14},{14,12},{16,18},{18,... | collective-permute-start | bytes 6291464 | tf_op jit(solution)/shard_map/cores_inputs/ppermute | solution.py:232
  151.1 7.8 %collective-permute-start.36 = (bf16[2,2,2,4,128,256]{5,4,3,2,1,0:T(8,128)(2,1)S(1)}, bf16[2,2,2,4,128,256]{5,4,3,2,1,0:T(8,128)(2,1)S(1)}, u32[]{:S(2)}, u32[]{:S(2)}) collective-permute-start(bf16[2,2,2,4,128,256]{5,4,3,2,1,0:T(8,128)(2,1)S(1)} %get-tuple-element.163), channel_id=1, source_target_pairs={{0,2},{2,0},{4,6},{6,4},{8,10},{10,8},{12,14},{14,12},{16,18},{18,... | collective-permute-start | bytes 6291464 | tf_op jit(solution)/shard_map/cores_inputs/ppermute | solution.py:232
  152.1 14.8 %collective-permute-start.39 = (bf16[4,128,512]{2,1,0:T(8,128)(2,1)S(1)}, bf16[4,128,512]{2,1,0:T(8,128)(2,1)S(1)}, u32[]{:S(2)}, u32[]{:S(2)}) collective-permute-start(bf16[4,128,512]{2,1,0:T(8,128)(2,1)S(1)} %get-tuple-element.215), channel_id=1, source_target_pairs={{0,1},{1,0},{2,3},{3,2},{4,5},{5,4},{6,7},{7,6},{8,9},{9,8},{10,11... | collective-permute-start | bytes 1572872 | tf_op jit(solution)/shard_map/across_mixed/ppermute | solution.py:238
  152.9 14.8 %collective-permute-start.40 = (bf16[4,128,512]{2,1,0:T(8,128)(2,1)S(1)}, bf16[4,128,512]{2,1,0:T(8,128)(2,1)S(1)}, u32[]{:S(2)}, u32[]{:S(2)}) collective-permute-start(bf16[4,128,512]{2,1,0:T(8,128)(2,1)S(1)} %get-tuple-element.214), channel_id=1, source_target_pairs={{0,4},{2,6},{4,0},{6,2},{8,12},{10,14},{12,8},{14,10},{16,20},{18,... | collective-permute-start | bytes 1572872 | tf_op jit(solution)/shard_map/across_mixed/ppermute | solution.py:235
  159.3 23.8 %collective-permute-start.37 = (bf16[2,4,128,256]{3,2,1,0:T(8,128)(2,1)S(1)}, bf16[2,4,128,256]{3,2,1,0:T(8,128)(2,1)S(1)}, u32[]{:S(2)}, u32[]{:S(2)}) collective-permute-start(bf16[2,4,128,256]{3,2,1,0:T(8,128)(2,1)S(1)} %get-tuple-element.168), channel_id=1, source_target_pairs={{0,4},{2,6},{4,0},{6,2},{8,12},{10,14},{12,8},{14,10},{16,20},{18,... | collective-permute-start | bytes 1572872 | tf_op jit(solution)/shard_map/over_inputs_1/ppermute | solution.py:235
  161.1 22.0 %collective-permute-start.38 = (bf16[2,4,128,256]{3,2,1,0:T(8,128)(2,1)S(1)}, bf16[2,4,128,256]{3,2,1,0:T(8,128)(2,1)S(1)}, u32[]{:S(2)}, u32[]{:S(2)}) collective-permute-start(bf16[2,4,128,256]{3,2,1,0:T(8,128)(2,1)S(1)} %get-tuple-element.169), channel_id=1, source_target_pairs={{0,1},{1,0},{2,3},{3,2},{4,5},{5,4},{6,7},{7,6},{8,9},{9,8},{10,11... | collective-permute-start | bytes 1572872 | tf_op jit(solution)/shard_map/over_inputs_1/ppermute | solution.py:238
  168.5 12.2 %collective-permute-start.41 = (bf16[2,128,512]{2,1,0:T(8,128)(2,1)S(1)}, bf16[2,128,512]{2,1,0:T(8,128)(2,1)S(1)}, u32[]{:S(2)}, u32[]{:S(2)}) collective-permute-start(bf16[2,128,512]{2,1,0:T(8,128)(2,1)S(1)} %get-tuple-element.232), channel_id=1, source_target_pairs={{0,24},{2,26},{4,28},{6,30},{8,0},{10,2},{12,4},{14,6},{16,8},{18,... | collective-permute-start | bytes 786440 | tf_op jit(solution)/shard_map/column_mixed/ppermute | solution.py:241
  170.5 12.6 %collective-permute-start.42 = (bf16[2,128,512]{2,1,0:T(8,128)(2,1)S(1)}, bf16[2,128,512]{2,1,0:T(8,128)(2,1)S(1)}, u32[]{:S(2)}, u32[]{:S(2)}) collective-permute-start(bf16[2,128,512]{2,1,0:T(8,128)(2,1)S(1)} %get-tuple-element.231), channel_id=1, source_target_pairs={{0,8},{2,10},{4,12},{6,14},{8,16},{10,18},{12,20},{14,22},{16,24},... | collective-permute-start | bytes 786440 | tf_op jit(solution)/shard_map/column_mixed/ppermute | solution.py:241
  170.5 25.8 %collective-permute-start.47 = (bf16[2,128,512]{2,1,0:T(8,128)(2,1)S(1)}, bf16[2,128,512]{2,1,0:T(8,128)(2,1)S(1)}, u32[]{:S(2)}, u32[]{:S(2)}) collective-permute-start(bf16[2,128,512]{2,1,0:T(8,128)(2,1)S(1)} %get-tuple-element.230), channel_id=1, source_target_pairs={{0,16},{2,18},{4,20},{6,22},{8,24},{10,26},{12,28},{14,30},{16,0},... | collective-permute-start | bytes 786440 | tf_op jit(solution)/shard_map/column_mixed/ppermute | solution.py:241
  183.3 13.0 %collective-permute-start.45 = (bf16[4,128,256]{2,1,0:T(8,128)(2,1)S(1)}, bf16[4,128,256]{2,1,0:T(8,128)(2,1)S(1)}, u32[]{:S(2)}, u32[]{:S(2)}) collective-permute-start(bf16[4,128,256]{2,1,0:T(8,128)(2,1)S(1)} %get-tuple-element.225), channel_id=1, source_target_pairs={{0,1},{1,0},{2,3},{3,2},{4,5},{5,4},{6,7},{7,6},{8,9},{9,8},{10,11... | collective-permute-start | bytes 786440 | tf_op jit(solution)/shard_map/across_inputs_1/ppermute | solution.py:238
  184.5 11.8 %collective-permute-start.46 = (bf16[4,128,256]{2,1,0:T(8,128)(2,1)S(1)}, bf16[4,128,256]{2,1,0:T(8,128)(2,1)S(1)}, u32[]{:S(2)}, u32[]{:S(2)}) collective-permute-start(bf16[4,128,256]{2,1,0:T(8,128)(2,1)S(1)} %get-tuple-element.224), channel_id=1, source_target_pairs={{0,4},{2,6},{4,0},{6,2},{8,12},{10,14},{12,8},{14,10},{16,20},{18,... | collective-permute-start | bytes 786440 | tf_op jit(solution)/shard_map/across_inputs_1/ppermute | solution.py:235
  185.0 20.0 %collective-permute-start.43 = (bf16[2,4,128,256]{3,2,1,0:T(8,128)(2,1)S(1)}, bf16[2,4,128,256]{3,2,1,0:T(8,128)(2,1)S(1)}, u32[]{:S(2)}, u32[]{:S(2)}) collective-permute-start(bf16[2,4,128,256]{3,2,1,0:T(8,128)(2,1)S(1)} %get-tuple-element.176), channel_id=1, source_target_pairs={{0,4},{2,6},{4,0},{6,2},{8,12},{10,14},{12,8},{14,10},{16,20},{18,... | collective-permute-start | bytes 1572872 | tf_op jit(solution)/shard_map/over_inputs_2/ppermute | solution.py:235
  186.7 18.4 %collective-permute-start.44 = (bf16[2,4,128,256]{3,2,1,0:T(8,128)(2,1)S(1)}, bf16[2,4,128,256]{3,2,1,0:T(8,128)(2,1)S(1)}, u32[]{:S(2)}, u32[]{:S(2)}) collective-permute-start(bf16[2,4,128,256]{3,2,1,0:T(8,128)(2,1)S(1)} %get-tuple-element.177), channel_id=1, source_target_pairs={{0,1},{1,0},{2,3},{3,2},{4,5},{5,4},{6,7},{7,6},{8,9},{9,8},{10,11... | collective-permute-start | bytes 1572872 | tf_op jit(solution)/shard_map/over_inputs_2/ppermute | solution.py:238
  196.6 20.6 %collective-permute-start.53 = (bf16[2,128,256]{2,1,0:T(8,128)(2,1)S(1)}, bf16[2,128,256]{2,1,0:T(8,128)(2,1)S(1)}, u32[]{:S(2)}, u32[]{:S(2)}) collective-permute-start(bf16[2,128,256]{2,1,0:T(8,128)(2,1)S(1)} %get-tuple-element.233), channel_id=1, source_target_pairs={{0,24},{2,26},{4,28},{6,30},{8,0},{10,2},{12,4},{14,6},{16,8},{18,... | collective-permute-start | bytes 393224 | tf_op jit(solution)/shard_map/column_inputs_1/ppermute | solution.py:241
  196.7 21.2 %collective-permute-start.54 = (bf16[2,128,256]{2,1,0:T(8,128)(2,1)S(1)}, bf16[2,128,256]{2,1,0:T(8,128)(2,1)S(1)}, u32[]{:S(2)}, u32[]{:S(2)}) collective-permute-start(bf16[2,128,256]{2,1,0:T(8,128)(2,1)S(1)} %get-tuple-element.235), channel_id=1, source_target_pairs={{0,16},{2,18},{4,20},{6,22},{8,24},{10,26},{12,28},{14,30},{16,0},... | collective-permute-start | bytes 393224 | tf_op jit(solution)/shard_map/column_inputs_1/ppermute | solution.py:241
  204.9 12.9 %collective-permute-start.55 = (bf16[2,128,256]{2,1,0:T(8,128)(2,1)S(1)}, bf16[2,128,256]{2,1,0:T(8,128)(2,1)S(1)}, u32[]{:S(2)}, u32[]{:S(2)}) collective-permute-start(bf16[2,128,256]{2,1,0:T(8,128)(2,1)S(1)} %get-tuple-element.234), channel_id=1, source_target_pairs={{0,8},{2,10},{4,12},{6,14},{8,16},{10,18},{12,20},{14,22},{16,24},... | collective-permute-start | bytes 393224 | tf_op jit(solution)/shard_map/column_inputs_1/ppermute | solution.py:241
  213.3 16.7 %collective-permute-start.50 = (bf16[2,128,256]{2,1,0:T(8,128)(2,1)S(1)}, bf16[2,128,256]{2,1,0:T(8,128)(2,1)S(1)}, u32[]{:S(2)}, u32[]{:S(2)}) collective-permute-start(bf16[2,128,256]{2,1,0:T(8,128)(2,1)S(1)} %get-tuple-element.238), channel_id=1, source_target_pairs={{0,24},{2,26},{4,28},{6,30},{8,0},{10,2},{12,4},{14,6},{16,8},{18,... | collective-permute-start | bytes 393224 | tf_op jit(solution)/shard_map/column_inputs_2/ppermute | solution.py:241
  217.2 12.8 %collective-permute-start.51 = (bf16[2,128,256]{2,1,0:T(8,128)(2,1)S(1)}, bf16[2,128,256]{2,1,0:T(8,128)(2,1)S(1)}, u32[]{:S(2)}, u32[]{:S(2)}) collective-permute-start(bf16[2,128,256]{2,1,0:T(8,128)(2,1)S(1)} %get-tuple-element.237), channel_id=1, source_target_pairs={{0,16},{2,18},{4,20},{6,22},{8,24},{10,26},{12,28},{14,30},{16,0},... | collective-permute-start | bytes 393224 | tf_op jit(solution)/shard_map/column_inputs_2/ppermute | solution.py:241
  217.2 12.8 %collective-permute-start.52 = (bf16[2,128,256]{2,1,0:T(8,128)(2,1)S(1)}, bf16[2,128,256]{2,1,0:T(8,128)(2,1)S(1)}, u32[]{:S(2)}, u32[]{:S(2)}) collective-permute-start(bf16[2,128,256]{2,1,0:T(8,128)(2,1)S(1)} %get-tuple-element.236), channel_id=1, source_target_pairs={{0,8},{2,10},{4,12},{6,14},{8,16},{10,18},{12,20},{14,22},{16,24},... | collective-permute-start | bytes 393224 | tf_op jit(solution)/shard_map/column_inputs_2/ppermute | solution.py:241
  219.1 10.9 %all-to-all-start = ((f32[16,1,128]{2,1,0:T(1,128)}), f32[16,1,128]{2,1,0:T(1,128)S(1)}, u32[]{:S(2)}, u32[]{:S(2)}) async-start(f32[16,1,128]{2,1,0:T(1,128)} %bitcast.94), calls=%async_computation | async-start | bytes 16384 | tf_op jit(solution)/shard_map/gates/all_to_all | solution.py:301
  (32 other events, 261.7 us)

commit v5 on v4

--- a/solution.py
+++ b/solution.py
@@ -190,11 +190,12 @@
 
 
 def input_kernel(capacity, side, pos, grad_gate_pre, grad_up_pre, *refs):
-    weights, outs, values = refs[:4], refs[4:-1], refs[-1]
-    span = weights[0].shape[1]
-    for at in range(2):
-        terms = dot(grad_gate_pre[...], weights[at][...])
-        terms = terms + dot(grad_up_pre[...], weights[2 + at][...])
+    blocks, outs, values = refs[:-3], refs[-3:-1], refs[-1]
+    count = len(blocks) // 2
+    span = blocks[0].shape[1]
+    for at in range(count):
+        terms = dot(grad_gate_pre[...], blocks[at][...])
+        terms = terms + dot(grad_up_pre[...], blocks[count + at][...])
         values[:, at * span : (at + 1) * span] = terms.astype(BF16)
     scatter_rows(side[0], pos, values, outs, capacity)
 
@@ -342,7 +343,7 @@
     def whole(*shape):
         return pl.BlockSpec(shape, lambda i, s: (0, 0), pipeline_mode=pl.Buffered(1))
 
-    def kernel(run, in_specs, outs, scratch=(), mebibytes=26):
+    def kernel(run, in_specs, outs, scratch=(), mebibytes=22):
         return pl.pallas_call(
             functools.partial(run, capacity),
             out_shape=[shape for shape, _ in outs],
@@ -369,7 +370,7 @@
             in_specs=[held] * len(lefts) + [columns],
             out_specs=[result] * len(lefts),
             scratch_shapes=[pltpu.VMEM((hidden, slots), BF16)] * len(lefts),
-            compiler_params=pltpu.CompilerParams(vmem_limit_bytes=26 * MEBIBYTE),
+            compiler_params=pltpu.CompilerParams(vmem_limit_bytes=14 * MEBIBYTE),
             cost_estimate=small,
         )(*lefts, rows)
 
@@ -455,20 +456,23 @@
         [row_out, hidden_bf, hidden_bf, (shaped((column, 4, tok_count), F32), table)],
     )(side, pos, gate, *(piece for piece, _ in pieces), weight_down, gate_pre, up_pre)
 
-    def input_terms(chunk, *hidden_grads):
-        columns = [
-            pl.BlockSpec((hidden, half), lambda i, s, at=at: (0, 2 * at + chunk), pipeline_mode=pl.Buffered(1))
-            for at in range(2)
+    def input_terms(quarters):
+        span = width // 4
+        blocks = [
+            pl.BlockSpec((hidden, span), lambda i, s, at=4 * far + quarter: (0, at), pipeline_mode=pl.Buffered(1))
+            for far in range(2)
+            for quarter in quarters
         ]
+        count = len(blocks)
         return kernel(
             input_kernel,
-            [table, rows_of(hidden), rows_of(hidden)] + columns * 2,
-            sums_out(half // 2),
-            [pltpu.VMEM((step_rows, width), BF16)],
-        )(side, pos, *hidden_grads, weight_gate, weight_gate, weight_up, weight_up)
-
-    own_1, other_1 = input_terms(0, grad_gate_pre, grad_up_pre)
-    own_2, other_2 = input_terms(1, grad_gate_pre, grad_up_pre)
+            [table, rows_of(hidden), rows_of(hidden)] + blocks * 2,
+            sums_out(len(quarters) * span // 2),
+            [pltpu.VMEM((step_rows, count * span), BF16)],
+        )(side, pos, grad_gate_pre, grad_up_pre, *[weight_gate] * count, *[weight_up] * count)
+
+    own_1, other_1 = input_terms((0, 1, 2))
+    own_2, other_2 = input_terms((3,))
     with jax.named_scope("gates"):
         token_sums = token_sums + swap_side(token_sums)
     mix_first, other_1, other_2, token_sums = together(mix_first, other_1, other_2, token_sums)
@@ -486,16 +490,18 @@
     with jax.named_scope("column_mixed"):
         mix_both = sent_column(mix_own, mix_core, mix_first, mix_second)
         mix_received = from_column(mix_both)
-    first_1, send_2, mix_received[::2] = together(first_1, send_2, mix_received[::2])
+    grad_gate_pre, mix_both = together(grad_gate_pre, mix_both)
+    grad_gate, grad_up = weight_grads(rows, grad_gate_pre, grad_up_pre)
+    first_1, send_2, mix_received[::2], grad_gate, grad_up = together(
+        first_1, send_2, mix_received[::2], grad_gate, grad_up
+    )
     with jax.named_scope("across_inputs_1"):
         send_1 = sent_second(own_1, core_1, first_1)
         second_1 = across(*send_1)
     with jax.named_scope("over_inputs_2"):
         send_1, send_2 = together(send_1, send_2)
         first_2 = over(*send_2)
-    grad_gate_pre, send_2 = together(grad_gate_pre, send_2)
-    grad_gate, grad_up = weight_grads(rows, grad_gate_pre, grad_up_pre)
-    second_1, mix_received, grad_gate, grad_up = together(second_1, mix_received, grad_gate, grad_up)
+    second_1, mix_received = together(second_1, mix_received)
     with jax.named_scope("column_inputs_1"):
         both_1 = sent_column(own_1, core_1, first_1, second_1)
         received_1 = from_column(both_1)

time: 232 us -> 228 us (0.983)
  starting transfers between devices: 66.5 us -> 62.2 us
  local copies, waits for them, and re-layouts: 9.05 us -> 11.9 us
    ppermute x17, starting transfers between devices: 29.3 us -> 23.2 us  [shift(): lax.ppermute(value, 'expert', [(e, (e + 4 * step) % expert_count) for e i...]
    all_to_all x1, waiting for transfers between devices: 6.31 us -> 0.79 us  [sums_of_experts(): lax.all_to_all(token_sums, 'expert', split_axis=0, concat_axis=0, tiled=T...]
    ppermute x17, waiting for transfers between devices: 39.8 us -> 43 us  [shift(): lax.ppermute(value, 'expert', [(e, (e + 4 * step) % expert_count) for e i...]
    ppermute x11, waiting for transfers between devices: 7.31 us -> 9.86 us  [swap_pair(): return lax.ppermute(value, 'expert', chip_pairs)]
    ppermute x12, waiting for transfers between devices: 14.5 us -> 12.1 us  [swap_side(): return lax.ppermute(value, 'tensor', [(0, 1), (1, 0)])]
    unnamed x46 -> x42, local copies, waits for them, and re-layouts: 2.82 us -> 5.05 us
  transfers between devices with their start and end apart: 57 -> 57, of which waited for: 26 -> 28; matrix products, arithmetic and copies ran while one was open for 8% -> 8% of each run, Pallas kernels for 24% -> 24%
where the time goes in v5:
time: 228 us
  waiting for transfers between devices  80.3 us (35%)
  starting transfers between devices  62.2 us (27%)
  Pallas kernels  55.7 us (24%)
  other arithmetic  14.4 us (6%)
  local copies, waits for them, and re-layouts  11.9 us (5%)
    ppermute x17, waiting for transfers between devices, shift(): lax.ppermute(value, 'expert', [(e, (e + 4 * step) % expert_count) for e i...  43 us
    ppermute x17, starting transfers between devices, shift(): lax.ppermute(value, 'expert', [(e, (e + 4 * step) % expert_count) for e i...  23.2 us
    pallas_call x2, Pallas kernels, weight_grads(): pl.pallas_call(functools.partial(weight_kernel, len(lefts)), out_shape=[s...  14.1 us
    pallas_call x1, Pallas kernels, gather_body(): kernel(up_kernel, [table, table] + [piece_of(piece) for piece in pieces]...  13.5 us
    ppermute x11, starting transfers between devices, swap_pair(): return lax.ppermute(value, 'expert', chip_pairs)  13.4 us
    pallas_call x2, Pallas kernels, input_terms(): kernel(input_kernel, [table, rows_of(hidden), rows_of(hidden)] + blocks *...  13 us
    ppermute x12, starting transfers between devices, swap_side(): return lax.ppermute(value, 'tensor', [(0, 1), (1, 0)])  12.5 us
    ppermute x12, waiting for transfers between devices, swap_side(): return lax.ppermute(value, 'tensor', [(0, 1), (1, 0)])  12.1 us
  transfers between devices with their start and end apart: 57, of which 28 were waited for; matrix products, arithmetic and copies ran while one was open for 8% of the time, Pallas kernels for 24%

profile of v5, /device:TPU:0, one launch (start us, length us, event | category | flops | bytes accessed | tf_op | source)
XLA Modules:
  0.0 227.6 jit_solution(250865251822605833)
XLA Ops:
  3.1 3.1 %collective-permute-start = (bf16[264,512]{1,0:T(8,128)(2,1)S(1)}, bf16[264,512]{1,0:T(8,128)(2,1)S(1)}, u32[]{:S(2)}, u32[]{:S(2)}) collective-permute-start(bf16[264,512]{1,0:T(8,128)(2,1)S(1)} %pad_maximum_fusion.11), channel_id=1, source_target_pairs={{0,8},{2,10},{4,12},{6,14},{8,16},{10,18},{12,20},{14,22},{16,24},... | collective-permute-start | bytes 811016 | tf_op jit(solution)/shard_map/column_tokens/ppermute | solution.py:242
  6.2 2.1 collective-permute-start.2
  8.3 2.9 %collective-permute-start.1 = (bf16[264,512]{1,0:T(8,128)(2,1)S(1)}, bf16[264,512]{1,0:T(8,128)(2,1)S(1)}, u32[]{:S(2)}, u32[]{:S(2)}) collective-permute-start(bf16[264,512]{1,0:T(8,128)(2,1)S(1)} %pad_maximum_fusion.11), channel_id=1, source_target_pairs={{0,16},{2,18},{4,20},{6,22},{24,8},{26,10},{28,12},{30,14},{1,17},... | collective-permute-start | bytes 811016 | tf_op jit(solution)/shard_map/column_tokens/ppermute | solution.py:262
  11.2 4.4 %collective-permute-done = bf16[264,512]{1,0:T(8,128)(2,1)S(1)} collective-permute-done((bf16[264,512]{1,0:T(8,128)(2,1)S(1)}, bf16[264,512]{1,0:T(8,128)(2,1)S(1)}, u32[]{:S(2)}, u32[]{:S(2)}) %collective-permute-start) | collective-permute-done | bytes 270368 | tf_op jit(solution)/shard_map/column_tokens/ppermute | solution.py:242
  15.6 4.4 %collective-permute-done.2 = bf16[264,512]{1,0:T(8,128)(2,1)S(1)} collective-permute-done((bf16[264,512]{1,0:T(8,128)(2,1)S(1)}, bf16[264,512]{1,0:T(8,128)(2,1)S(1)}, u32[]{:S(2)}, u32[]{:S(2)}) %collective-permute-start.2) | collective-permute-done | bytes 270368 | tf_op jit(solution)/shard_map/column_tokens/ppermute | solution.py:242
  20.0 1.3 collective-permute-start.3
  21.4 2.2 collective-permute-done.1
  23.6 6.1 %collective-permute-done.3 = bf16[264,512]{1,0:T(8,128)(2,1)S(1)} collective-permute-done((bf16[264,512]{1,0:T(8,128)(2,1)S(1)}, bf16[264,512]{1,0:T(8,128)(2,1)S(1)}, u32[]{:S(2)}, u32[]{:S(2)}) %collective-permute-start.3) | collective-permute-done | bytes 270368 | tf_op jit(solution)/shard_map/column_tokens/ppermute | solution.py:264
  30.0 1.8 collective-permute-start.5
  32.7 1.5 collective-permute-start.4
  34.7 6.0 %collective-permute-start.7 = (bf16[2,128,256]{2,1,0:T(8,128)(2,1)S(1)}, bf16[2,128,256]{2,1,0:T(8,128)(2,1)S(1)}, u32[]{:S(2)}, u32[]{:S(2)}) collective-permute-start(bf16[2,128,256]{2,1,0:T(8,128)(2,1)S(1)} %get-tuple-element.123), channel_id=1, source_target_pairs={{0,16},{2,18},{4,20},{6,22},{8,24},{10,26},{12,28},{14,30},{16,0},... | collective-permute-start | bytes 393224 | tf_op jit(solution)/shard_map/across_tokens/ppermute | solution.py:242
  41.2 2.0 collective-permute-done.6
  43.1 3.3 %collective-permute-done.7 = bf16[2,128,256]{2,1,0:T(8,128)(2,1)S(1)} collective-permute-done((bf16[2,128,256]{2,1,0:T(8,128)(2,1)S(1)}, bf16[2,128,256]{2,1,0:T(8,128)(2,1)S(1)}, u32[]{:S(2)}, u32[]{:S(2)}) %collective-permute-start.7) | collective-permute-done | bytes 131104 | tf_op jit(solution)/shard_map/across_tokens/ppermute | solution.py:242
  54.6 5.1 %collective-permute-done.13 = bf16[2,128,256]{2,1,0:T(8,128)(2,1)} collective-permute-done((bf16[2,128,256]{2,1,0:T(8,128)(2,1)S(1)}, bf16[2,128,256]{2,1,0:T(8,128)(2,1)}, u32[]{:S(2)}, u32[]{:S(2)}) %collective-permute-start.13) | collective-permute-done | bytes 131104 | tf_op jit(solution)/shard_map/over_tokens/ppermute | solution.py:242
  61.0 5.9 %collective-permute-done.14 = bf16[2,128,256]{2,1,0:T(8,128)(2,1)} collective-permute-done((bf16[2,128,256]{2,1,0:T(8,128)(2,1)S(1)}, bf16[2,128,256]{2,1,0:T(8,128)(2,1)}, u32[]{:S(2)}, u32[]{:S(2)}) %collective-permute-start.14) | collective-permute-done | bytes 131104 | tf_op jit(solution)/shard_map/over_tokens/ppermute | solution.py:242
  66.8 1.4 collective-permute-start.15
  68.3 1.6 fusion.pos
  69.8 2.3 collective-permute-done.15
  72.1 2.7 %collective-permute-done.9.refs_1_ = bf16[2,4,128,512]{3,2,1,0:T(8,128)(2,1)} collective-permute-done((bf16[2,4,128,512]{3,2,1,0:T(8,128)(2,1)S(1)}, bf16[2,4,128,512]{3,2,1,0:T(8,128)(2,1)}, u32[]{:S(2)}, u32[]{:S(2)}) %collective-permute-start.9) | collective-permute-done | bytes 1048608 | tf_op jit(solution)/shard_map/over_tokens/ppermute | solution.py:236
  78.7 1.3 collective-permute-start.19
  80.6 13.5 %shard_map.118 = (bf16[1024,2048]{1,0:T(8,128)(2,1)}, f32[1024,704]{1,0:T(8,128)}, f32[1024,704]{1,0:T(8,128)}, bf16[1024,704]{1,0:T(8,128)(2,1)}) custom-call(s32[1]{0:T(128)} %bitcast.side, f32[4,4,128]{2,1,0:T(4,128)} %fusion.pos, f32[4,4,128]{2,1,0:T(4,128)} %copy.49.gate, bf16[2,4,128,512]{3,2,1,0:T(8,128)(2,1)} %copy-done.10, ...), custom_call_target="tpu_custom_call" | custom-call | flops 1048576 | bytes 65536 | tf_op jit(solution)/shard_map/pallas_call | solution.py:417
  96.0 1.8 collective-permute-start.21
  97.7 7.2 %shard_map.119 = (bf16[2,2,2,4,128,512]{5,4,3,2,1,0:T(8,128)(2,1)S(1)}, bf16[2,2,2,4,128,512]{5,4,3,2,1,0:T(8,128)(2,1)S(1)}) custom-call(s32[1]{0:T(128)} %bitcast.side, f32[4,4,128]{2,1,0:T(4,128)S(1)} %copy-done.7, bf16[1024,704]{1,0:T(8,128)(2,1)S(1)} %copy-done.3, bf16[704,2048]{1,0:T(8,128)(2,1)S(1)} %bitcast.252), custom_call_target="tpu_custom_call" | custom-call | flops 1048576 | bytes 65536 | tf_op jit(solution)/shard_map/pallas_call | solution.py:429
  104.9 4.1 %collective-permute-done.22.refs_5_ = bf16[2,4,128,256]{3,2,1,0:T(8,128)(2,1)S(1)} collective-permute-done((bf16[2,4,128,256]{3,2,1,0:T(8,128)(2,1)S(1)}, bf16[2,4,128,256]{3,2,1,0:T(8,128)(2,1)S(1)}, u32[]{:S(2)}, u32[]{:S(2)}) %collective-permute-start.22) | collective-permute-done | bytes 524320 | tf_op jit(solution)/shard_map/over_grads_1/ppermute | solution.py:239
  110.2 1.8 collective-permute-start.28
  113.3 3.4 %collective-permute-done.27 = bf16[2,2,2,4,128,512]{5,4,3,2,1,0:T(8,128)(2,1)S(1)} collective-permute-done((bf16[2,2,2,4,128,512]{5,4,3,2,1,0:T(8,128)(2,1)S(1)}, bf16[2,2,2,4,128,512]{5,4,3,2,1,0:T(8,128)(2,1)S(1)}, u32[]{:S(2)}, u32[]{:S(2)}) %collective-permute-start.27) | collective-permute-done | bytes 4194336 | tf_op jit(solution)/shard_map/cores_mixed/ppermute | solution.py:233
  117.5 1.4 copy-done.11
  118.9 1.8 collective-permute-start.32
  121.9 3.1 %collective-permute-done.28.refs_9_ = bf16[2,4,128,256]{3,2,1,0:T(8,128)(2,1)S(1)} collective-permute-done((bf16[2,4,128,256]{3,2,1,0:T(8,128)(2,1)S(1)}, bf16[2,4,128,256]{3,2,1,0:T(8,128)(2,1)S(1)}, u32[]{:S(2)}, u32[]{:S(2)}) %collective-permute-start.28) | collective-permute-done | bytes 524320 | tf_op jit(solution)/shard_map/over_grads_2/ppermute | solution.py:236
  125.0 1.9 collective-permute-done.29.refs_13_
  129.6 7.9 %shard_map.120 = (bf16[1024,2048]{1,0:T(8,128)(2,1)S(1)}, bf16[1024,704]{1,0:T(8,128)(2,1)S(1)}, bf16[1024,704]{1,0:T(8,128)(2,1)S(1)}, f32[4,4,128]{2,1,0:T(4,128)S(1)}) custom-call(s32[1]{0:T(128)} %bitcast.side, f32[4,4,128]{2,1,0:T(4,128)S(1)} %copy-done.7, f32[4,4,128]{2,1,0:T(4,128)S(1)} %copy-done.8, ...), custom_call_target="tpu_custom_call" | custom-call | flops 1048576 | bytes 65536 | tf_op jit(solution)/shard_map/pallas_call | solution.py:453
  138.7 3.8 %shard_map.121 = (bf16[2,2,2,4,128,128]{5,4,3,2,1,0:T(8,128)(2,1)S(1)}, bf16[2,2,2,4,128,128]{5,4,3,2,1,0:T(8,128)(2,1)S(1)}) custom-call(s32[1]{0:T(128)} %bitcast.side, f32[4,4,128]{2,1,0:T(4,128)S(1)} %copy-done.7, bf16[1024,704]{1,0:T(8,128)(2,1)S(1)} %get-tuple-element.173.grad_gate_pre.refs_0_, ...), custom_call_target="tpu_custom_call" | custom-call | flops 1048576 | bytes 65536 | tf_op jit(solution)/shard_map/pallas_call | solution.py:467
  142.5 9.1 %shard_map.122 = (bf16[2,2,2,4,128,384]{5,4,3,2,1,0:T(8,128)(2,1)S(1)}, bf16[2,2,2,4,128,384]{5,4,3,2,1,0:T(8,128)(2,1)S(1)}) custom-call(s32[1]{0:T(128)} %bitcast.side, f32[4,4,128]{2,1,0:T(4,128)S(1)} %copy-done.7, bf16[1024,704]{1,0:T(8,128)(2,1)S(1)} %get-tuple-element.173.grad_gate_pre.refs_0_, ...), custom_call_target="tpu_custom_call" | custom-call | flops 1048576 | bytes 65536 | tf_op jit(solution)/shard_map/pallas_call | solution.py:467
  154.0 5.4 %shard_map.123 = bf16[704,2048]{1,0:T(8,128)(2,1)} custom-call(bf16[1024,704]{1,0:T(8,128)(2,1)S(1)} %copy-done.3, bf16[1024,2048]{1,0:T(8,128)(2,1)S(1)} %get-tuple-element.168.refs_1_), custom_call_target="tpu_custom_call" | custom-call | flops 1048576 | bytes 65536 | tf_op jit(solution)/shard_map/pallas_call | solution.py:366
  160.0 1.8 collective-permute-start.37
  163.0 4.6 %collective-permute-done.39 = bf16[4,128,512]{2,1,0:T(8,128)(2,1)S(1)} collective-permute-done((bf16[4,128,512]{2,1,0:T(8,128)(2,1)S(1)}, bf16[4,128,512]{2,1,0:T(8,128)(2,1)S(1)}, u32[]{:S(2)}, u32[]{:S(2)}) %collective-permute-start.39) | collective-permute-done | bytes 524320 | tf_op jit(solution)/shard_map/across_mixed/ppermute | solution.py:239
  169.2 2.2 collective-permute-start.41
  171.6 2.0 copy-done.4
  173.6 8.8 %shard_map.124 = (bf16[704,2048]{1,0:T(8,128)(2,1)}, bf16[704,2048]{1,0:T(8,128)(2,1)}) custom-call(bf16[1024,704]{1,0:T(8,128)(2,1)S(1)} %get-tuple-element.173.grad_gate_pre.refs_0_, bf16[1024,704]{1,0:T(8,128)(2,1)S(1)} %get-tuple-element.157.grad_up_pre.refs_1_, bf16[1024,2048]{1,0:T(8,128)(2,1)S(1)} %copy-done.4), custom_call_target="tpu_custom_call" | custom-call | flops 1048576 | bytes 65536 | tf_op jit(solution)/shard_map/pallas_call | solution.py:366
  182.4 1.8 collective-permute-done.37
  186.5 1.6 collective-permute-start.43
  189.0 10.2 %collective-permute-done.47 = bf16[2,128,512]{2,1,0:T(8,128)(2,1)S(1)} collective-permute-done((bf16[2,128,512]{2,1,0:T(8,128)(2,1)S(1)}, bf16[2,128,512]{2,1,0:T(8,128)(2,1)S(1)}, u32[]{:S(2)}, u32[]{:S(2)}) %collective-permute-start.47) | collective-permute-done | bytes 262176 | tf_op jit(solution)/shard_map/column_mixed/ppermute | solution.py:242
  199.6 1.4 collective-permute-start.53
  202.8 1.7 collective-permute-start.49
  205.5 1.5 collective-permute-done.48
  209.2 5.5 %all-to-all-start = ((f32[16,1,128]{2,1,0:T(1,128)}), f32[16,1,128]{2,1,0:T(1,128)S(1)}, u32[]{:S(2)}, u32[]{:S(2)}) async-start(f32[16,1,128]{2,1,0:T(1,128)} %bitcast.94), calls=%async_computation | async-start | bytes 16384 | tf_op jit(solution)/shard_map/gates/all_to_all | solution.py:302
  215.4 3.7 %collective-permute-start.50 = (bf16[2,128,128]{2,1,0:T(8,128)(2,1)}, bf16[2,128,128]{2,1,0:T(8,128)(2,1)S(1)}, u32[]{:S(2)}, u32[]{:S(2)}) collective-permute-start(bf16[2,128,128]{2,1,0:T(8,128)(2,1)} %get-tuple-element.246), channel_id=1, source_target_pairs={{0,24},{2,26},{4,28},{6,30},{8,0},{10,2},{12,4},{14,6},{16,8},{18,... | collective-permute-start | bytes 196616 | tf_op jit(solution)/shard_map/column_inputs_2/ppermute | solution.py:242
  221.9 4.3 %collective-permute-done.51 = bf16[2,128,128]{2,1,0:T(8,128)(2,1)S(1)} collective-permute-done((bf16[2,128,128]{2,1,0:T(8,128)(2,1)}, bf16[2,128,128]{2,1,0:T(8,128)(2,1)S(1)}, u32[]{:S(2)}, u32[]{:S(2)}) %collective-permute-start.51) | collective-permute-done | bytes 65568 | tf_op jit(solution)/shard_map/column_inputs_2/ppermute | solution.py:242
  (204 shorter events, 47.7 us)
Async XLA Ops:
  3.1 12.5 %collective-permute-start = (bf16[264,512]{1,0:T(8,128)(2,1)S(1)}, bf16[264,512]{1,0:T(8,128)(2,1)S(1)}, u32[]{:S(2)}, u32[]{:S(2)}) collective-permute-start(bf16[264,512]{1,0:T(8,128)(2,1)S(1)} %pad_maximum_fusion.11), channel_id=1, source_target_pairs={{0,8},{2,10},{4,12},{6,14},{8,16},{10,18},{12,20},{14,22},{16,24},... | collective-permute-start | bytes 811016 | tf_op jit(solution)/shard_map/column_tokens/ppermute | solution.py:242
  6.2 13.7 %collective-permute-start.2 = (bf16[264,512]{1,0:T(8,128)(2,1)S(1)}, bf16[264,512]{1,0:T(8,128)(2,1)S(1)}, u32[]{:S(2)}, u32[]{:S(2)}) collective-permute-start(bf16[264,512]{1,0:T(8,128)(2,1)S(1)} %pad_maximum_fusion.11), channel_id=1, source_target_pairs={{0,24},{2,26},{4,28},{6,30},{8,0},{10,2},{12,4},{14,6},{16,8},{18,... | collective-permute-start | bytes 811016 | tf_op jit(solution)/shard_map/column_tokens/ppermute | solution.py:242
  8.3 15.3 %collective-permute-start.1 = (bf16[264,512]{1,0:T(8,128)(2,1)S(1)}, bf16[264,512]{1,0:T(8,128)(2,1)S(1)}, u32[]{:S(2)}, u32[]{:S(2)}) collective-permute-start(bf16[264,512]{1,0:T(8,128)(2,1)S(1)} %pad_maximum_fusion.11), channel_id=1, source_target_pairs={{0,16},{2,18},{4,20},{6,22},{24,8},{26,10},{28,12},{30,14},{1,17},... | collective-permute-start | bytes 811016 | tf_op jit(solution)/shard_map/column_tokens/ppermute | solution.py:262
  20.0 9.8 %collective-permute-start.3 = (bf16[264,512]{1,0:T(8,128)(2,1)S(1)}, bf16[264,512]{1,0:T(8,128)(2,1)S(1)}, u32[]{:S(2)}, u32[]{:S(2)}) collective-permute-start(bf16[264,512]{1,0:T(8,128)(2,1)S(1)} %broadcast_select_fusion), channel_id=1, source_target_pairs={{8,0},{10,2},{12,4},{14,6},{16,24},{18,26},{20,28},{22,30},{9,1},{... | collective-permute-start | bytes 811016 | tf_op jit(solution)/shard_map/column_tokens/ppermute | solution.py:264
  30.0 17.0 %collective-permute-start.5 = (bf16[4,136,512]{2,1,0:T(8,128)(2,1)S(1)}, bf16[4,136,512]{2,1,0:T(8,128)(2,1)S(1)}, u32[]{:S(2)}, u32[]{:S(2)}) collective-permute-start(bf16[4,136,512]{2,1,0:T(8,128)(2,1)S(1)} %pad_maximum_fusion.6), channel_id=1, source_target_pairs={{0,4},{2,6},{4,0},{6,2},{8,12},{10,14},{12,8},{14,10},{16,20},{18,... | collective-permute-start | bytes 1671176 | tf_op jit(solution)/shard_map/across_tokens/ppermute | solution.py:236
  32.7 14.3 %collective-permute-start.4 = (bf16[4,128,512]{2,1,0:T(8,128)(2,1)S(1)}, bf16[4,128,512]{2,1,0:T(8,128)(2,1)S(1)}, u32[]{:S(2)}, u32[]{:S(2)}) collective-permute-start(bf16[4,128,512]{2,1,0:T(8,128)(2,1)S(1)} %get-tuple-element.243), channel_id=1, source_target_pairs={{0,1},{1,0},{2,3},{3,2},{4,5},{5,4},{6,7},{7,6},{8,9},{9,8},{10,11... | collective-permute-start | bytes 1572872 | tf_op jit(solution)/shard_map/across_tokens/ppermute | solution.py:239
  34.7 8.4 %collective-permute-start.6 = (bf16[2,128,256]{2,1,0:T(8,128)(2,1)S(1)}, bf16[2,128,256]{2,1,0:T(8,128)(2,1)S(1)}, u32[]{:S(2)}, u32[]{:S(2)}) collective-permute-start(bf16[2,128,256]{2,1,0:T(8,128)(2,1)S(1)} %get-tuple-element.123), channel_id=1, source_target_pairs={{0,8},{2,10},{4,12},{6,14},{8,16},{10,18},{12,20},{14,22},{16,24},... | collective-permute-start | bytes 393224 | tf_op jit(solution)/shard_map/across_tokens/ppermute | solution.py:242
  34.7 11.7 %collective-permute-start.7 = (bf16[2,128,256]{2,1,0:T(8,128)(2,1)S(1)}, bf16[2,128,256]{2,1,0:T(8,128)(2,1)S(1)}, u32[]{:S(2)}, u32[]{:S(2)}) collective-permute-start(bf16[2,128,256]{2,1,0:T(8,128)(2,1)S(1)} %get-tuple-element.123), channel_id=1, source_target_pairs={{0,16},{2,18},{4,20},{6,22},{8,24},{10,26},{12,28},{14,30},{16,0},... | collective-permute-start | bytes 393224 | tf_op jit(solution)/shard_map/across_tokens/ppermute | solution.py:242
  48.0 24.1 %collective-permute-start.10 = (bf16[2,4,128,512]{3,2,1,0:T(8,128)(2,1)S(1)}, bf16[2,4,128,512]{3,2,1,0:T(8,128)(2,1)}, u32[]{:S(2)}, u32[]{:S(2)}) collective-permute-start(bf16[2,4,128,512]{3,2,1,0:T(8,128)(2,1)S(1)} %pad_maximum_fusion.5.refs_4_), channel_id=1, source_target_pairs={{0,1},{1,0},{2,3},{3,2},{4,5},{5,4},{6,7},{7,6},{8,9},{9,8},{10,11... | collective-permute-start | bytes 3145736 | tf_op jit(solution)/shard_map/over_tokens/ppermute | solution.py:239
  48.1 24.0 %collective-permute-start.12 = (bf16[2,4,128,512]{3,2,1,0:T(8,128)(2,1)S(1)}, bf16[2,4,128,512]{3,2,1,0:T(8,128)(2,1)S(1)}, u32[]{:S(2)}, u32[]{:S(2)}) collective-permute-start(bf16[2,4,128,512]{3,2,1,0:T(8,128)(2,1)S(1)} %pad_maximum_fusion.5.refs_4_), channel_id=1, source_target_pairs={{0,2},{2,0},{4,6},{6,4},{8,10},{10,8},{12,14},{14,12},{16,18},{18,... | collective-permute-start | bytes 3145736 | tf_op jit(solution)/shard_map/over_tokens/ppermute | solution.py:233
  49.1 23.0 %collective-permute-start.11 = (bf16[2,4,128,512]{3,2,1,0:T(8,128)(2,1)S(1)}, bf16[2,4,128,512]{3,2,1,0:T(8,128)(2,1)}, u32[]{:S(2)}, u32[]{:S(2)}) collective-permute-start(bf16[2,4,128,512]{3,2,1,0:T(8,128)(2,1)S(1)} %pad_maximum_fusion.4.refs_0_), channel_id=1, source_target_pairs={{0,2},{2,0},{4,6},{6,4},{8,10},{10,8},{12,14},{14,12},{16,18},{18,... | collective-permute-start | bytes 3145736 | tf_op jit(solution)/shard_map/over_tokens/ppermute | solution.py:233
  49.2 25.7 %collective-permute-start.9 = (bf16[2,4,128,512]{3,2,1,0:T(8,128)(2,1)S(1)}, bf16[2,4,128,512]{3,2,1,0:T(8,128)(2,1)}, u32[]{:S(2)}, u32[]{:S(2)}) collective-permute-start(bf16[2,4,128,512]{3,2,1,0:T(8,128)(2,1)S(1)} %pad_maximum_fusion.4.refs_0_), channel_id=1, source_target_pairs={{0,4},{2,6},{4,0},{6,2},{8,12},{10,14},{12,8},{14,10},{16,20},{18,... | collective-permute-start | bytes 3145736 | tf_op jit(solution)/shard_map/over_tokens/ppermute | solution.py:236
  52.0 7.7 %collective-permute-start.13 = (bf16[2,128,256]{2,1,0:T(8,128)(2,1)S(1)}, bf16[2,128,256]{2,1,0:T(8,128)(2,1)}, u32[]{:S(2)}, u32[]{:S(2)}) collective-permute-start(bf16[2,128,256]{2,1,0:T(8,128)(2,1)S(1)} %get-tuple-element.127), channel_id=1, source_target_pairs={{0,8},{2,10},{4,12},{6,14},{8,16},{10,18},{12,20},{14,22},{16,24},... | collective-permute-start | bytes 393224 | tf_op jit(solution)/shard_map/over_tokens/ppermute | solution.py:242
  59.7 7.1 %collective-permute-start.14 = (bf16[2,128,256]{2,1,0:T(8,128)(2,1)S(1)}, bf16[2,128,256]{2,1,0:T(8,128)(2,1)}, u32[]{:S(2)}, u32[]{:S(2)}) collective-permute-start(bf16[2,128,256]{2,1,0:T(8,128)(2,1)S(1)} %get-tuple-element.127), channel_id=1, source_target_pairs={{0,16},{2,18},{4,20},{6,22},{8,24},{10,26},{12,28},{14,30},{16,0},... | collective-permute-start | bytes 393224 | tf_op jit(solution)/shard_map/over_tokens/ppermute | solution.py:242
  78.3 15.8 %collective-permute-start.20 = (bf16[2,4,128,256]{3,2,1,0:T(8,128)(2,1)S(1)}, bf16[2,4,128,256]{3,2,1,0:T(8,128)(2,1)S(1)}, u32[]{:S(2)}, u32[]{:S(2)}) collective-permute-start(bf16[2,4,128,256]{3,2,1,0:T(8,128)(2,1)S(1)} %get-tuple-element.239), channel_id=1, source_target_pairs={{0,4},{2,6},{4,0},{6,2},{8,12},{10,14},{12,8},{14,10},{16,20},{18,... | collective-permute-start | bytes 1572872 | tf_op jit(solution)/shard_map/across_grads/ppermute | solution.py:236
  78.7 15.4 %collective-permute-start.19 = (bf16[2,4,128,256]{3,2,1,0:T(8,128)(2,1)S(1)}, bf16[2,4,128,256]{3,2,1,0:T(8,128)(2,1)S(1)}, u32[]{:S(2)}, u32[]{:S(2)}) collective-permute-start(bf16[2,4,128,256]{3,2,1,0:T(8,128)(2,1)S(1)} %get-tuple-element.240), channel_id=1, source_target_pairs={{0,1},{1,0},{2,3},{3,2},{4,5},{5,4},{6,7},{7,6},{8,9},{9,8},{10,11... | collective-permute-start | bytes 1572872 | tf_op jit(solution)/shard_map/across_grads/ppermute | solution.py:239
  94.2 15.3 %collective-permute-start.24 = (bf16[2,2,4,128,256]{4,3,2,1,0:T(8,128)(2,1)S(1)}, bf16[2,2,4,128,256]{4,3,2,1,0:T(8,128)(2,1)S(1)}, u32[]{:S(2)}, u32[]{:S(2)}) collective-permute-start(bf16[2,2,4,128,256]{4,3,2,1,0:T(8,128)(2,1)S(1)} %pad_maximum_fusion.3.refs_4_.refs_12_), channel_id=1, source_target_pairs={{0,2},{2,0},{4,6},{6,4},{8,10},{10,8},{12,14},{14,12},{16,18},{18,... | collective-permute-start | bytes 3145736 | tf_op jit(solution)/shard_map/over_grads_1/ppermute | solution.py:233
  94.4 15.1 %collective-permute-start.23 = (bf16[2,2,4,128,256]{4,3,2,0,1:T(8,128)(2,1)S(1)}, bf16[2,2,4,128,256]{4,3,2,0,1:T(8,128)(2,1)S(1)}, u32[]{:S(2)}, u32[]{:S(2)}) collective-permute-start(bf16[2,2,4,128,256]{4,3,2,0,1:T(8,128)(2,1)S(1)} %pad_maximum_fusion.2), channel_id=1, source_target_pairs={{0,2},{2,0},{4,6},{6,4},{8,10},{10,8},{12,14},{14,12},{16,18},{18,... | collective-permute-start | bytes 3145736 | tf_op jit(solution)/shard_map/over_grads_1/ppermute | solution.py:233
  95.1 13.9 %collective-permute-start.22 = (bf16[2,4,128,256]{3,2,1,0:T(8,128)(2,1)S(1)}, bf16[2,4,128,256]{3,2,1,0:T(8,128)(2,1)S(1)}, u32[]{:S(2)}, u32[]{:S(2)}) collective-permute-start(bf16[2,4,128,256]{3,2,1,0:T(8,128)(2,1)S(1)} %fusion.18), channel_id=1, source_target_pairs={{0,1},{1,0},{2,3},{3,2},{4,5},{5,4},{6,7},{7,6},{8,9},{9,8},{10,11... | collective-permute-start | bytes 1572872 | tf_op jit(solution)/shard_map/over_grads_1/ppermute | solution.py:239
  96.0 13.6 %collective-permute-start.21 = (bf16[2,4,128,256]{3,2,1,0:T(8,128)(2,1)S(1)}, bf16[2,4,128,256]{3,2,1,0:T(8,128)(2,1)S(1)}, u32[]{:S(2)}, u32[]{:S(2)}) collective-permute-start(bf16[2,4,128,256]{3,2,1,0:T(8,128)(2,1)S(1)} %fusion.20), channel_id=1, source_target_pairs={{0,4},{2,6},{4,0},{6,2},{8,12},{10,14},{12,8},{14,10},{16,20},{18,... | collective-permute-start | bytes 1572872 | tf_op jit(solution)/shard_map/over_grads_1/ppermute | solution.py:236
  109.6 7.2 %collective-permute-start.27 = (bf16[2,2,2,4,128,512]{5,4,3,2,1,0:T(8,128)(2,1)S(1)}, bf16[2,2,2,4,128,512]{5,4,3,2,1,0:T(8,128)(2,1)S(1)}, u32[]{:S(2)}, u32[]{:S(2)}) collective-permute-start(bf16[2,2,2,4,128,512]{5,4,3,2,1,0:T(8,128)(2,1)S(1)} %get-tuple-element.145), channel_id=1, source_target_pairs={{0,2},{2,0},{4,6},{6,4},{8,10},{10,8},{12,14},{14,12},{16,18},{18,... | collective-permute-start | bytes 12582920 | tf_op jit(solution)/shard_map/cores_mixed/ppermute | solution.py:233
  109.6 9.3 %collective-permute-start.25 = (bf16[2,4,128,256]{3,2,1,0:T(8,128)(2,1)S(1)}, bf16[2,4,128,256]{3,2,1,0:T(8,128)(2,1)S(1)}, u32[]{:S(2)}, u32[]{:S(2)}) collective-permute-start(bf16[2,4,128,256]{3,2,1,0:T(8,128)(2,1)S(1)} %collective-permute-done.21.refs_1_), channel_id=1, source_target_pairs={{0,2},{2,0},{4,6},{6,4},{8,10},{10,8},{12,14},{14,12},{16,18},{18,... | collective-permute-start | bytes 1572872 | tf_op jit(solution)/shard_map/cores_mixed/ppermute | solution.py:233
  110.1 8.8 %collective-permute-start.26 = (bf16[2,4,128,256]{3,2,1,0:T(8,128)(2,1)S(1)}, bf16[2,4,128,256]{3,2,1,0:T(8,128)(2,1)S(1)}, u32[]{:S(2)}, u32[]{:S(2)}) collective-permute-start(bf16[2,4,128,256]{3,2,1,0:T(8,128)(2,1)S(1)} %collective-permute-done.22.refs_5_), channel_id=1, source_target_pairs={{0,2},{2,0},{4,6},{6,4},{8,10},{10,8},{12,14},{14,12},{16,18},{18,... | collective-permute-start | bytes 1572872 | tf_op jit(solution)/shard_map/cores_mixed/ppermute | solution.py:233
  110.2 14.8 %collective-permute-start.28 = (bf16[2,4,128,256]{3,2,1,0:T(8,128)(2,1)S(1)}, bf16[2,4,128,256]{3,2,1,0:T(8,128)(2,1)S(1)}, u32[]{:S(2)}, u32[]{:S(2)}) collective-permute-start(bf16[2,4,128,256]{3,2,1,0:T(8,128)(2,1)S(1)} %slice_bitcast_fusion.2), channel_id=1, source_target_pairs={{0,4},{2,6},{4,0},{6,2},{8,12},{10,14},{12,8},{14,10},{16,20},{18,... | collective-permute-start | bytes 1572872 | tf_op jit(solution)/shard_map/over_grads_2/ppermute | solution.py:236
  112.0 14.8 %collective-permute-start.29 = (bf16[2,4,128,256]{3,2,1,0:T(8,128)(2,1)S(1)}, bf16[2,4,128,256]{3,2,1,0:T(8,128)(2,1)S(1)}, u32[]{:S(2)}, u32[]{:S(2)}) collective-permute-start(bf16[2,4,128,256]{3,2,1,0:T(8,128)(2,1)S(1)} %slice_bitcast_fusion.1), channel_id=1, source_target_pairs={{0,1},{1,0},{2,3},{3,2},{4,5},{5,4},{6,7},{7,6},{8,9},{9,8},{10,11... | collective-permute-start | bytes 1572872 | tf_op jit(solution)/shard_map/over_grads_2/ppermute | solution.py:239
  118.9 32.9 %collective-permute-start.32 = (bf16[2,4,128,512]{3,2,1,0:T(8,128)(2,1)S(1)}, bf16[2,4,128,512]{3,2,1,0:T(8,128)(2,1)S(1)}, u32[]{:S(2)}, u32[]{:S(2)}) collective-permute-start(bf16[2,4,128,512]{3,2,1,0:T(8,128)(2,1)S(1)} %get-tuple-element.150), channel_id=1, source_target_pairs={{0,4},{2,6},{4,0},{6,2},{8,12},{10,14},{12,8},{14,10},{16,20},{18,... | collective-permute-start | bytes 3145736 | tf_op jit(solution)/shard_map/over_mixed/ppermute | solution.py:236
  120.7 31.1 %collective-permute-start.33 = (bf16[2,4,128,512]{3,2,1,0:T(8,128)(2,1)S(1)}, bf16[2,4,128,512]{3,2,1,0:T(8,128)(2,1)S(1)}, u32[]{:S(2)}, u32[]{:S(2)}) collective-permute-start(bf16[2,4,128,512]{3,2,1,0:T(8,128)(2,1)S(1)} %get-tuple-element.151), channel_id=1, source_target_pairs={{0,1},{1,0},{2,3},{3,2},{4,5},{5,4},{6,7},{7,6},{8,9},{9,8},{10,11... | collective-permute-start | bytes 3145736 | tf_op jit(solution)/shard_map/over_mixed/ppermute | solution.py:239
  137.4 14.3 %collective-permute-start.34 = (f32[4,4,128]{2,1,0:T(4,128)S(1)}, f32[4,4,128]{2,1,0:T(4,128)S(1)}, u32[]{:S(2)}, u32[]{:S(2)}) collective-permute-start(f32[4,4,128]{2,1,0:T(4,128)S(1)} %get-tuple-element.161), channel_id=1, source_target_pairs={{0,1},{1,0},{2,3},{3,2},{4,5},{5,4},{6,7},{7,6},{8,9},{9,8},{10,11... | collective-permute-start | bytes 24584 | tf_op jit(solution)/shard_map/gates/ppermute | solution.py:239
  151.7 7.7 %collective-permute-start.36 = (bf16[2,2,2,4,128,384]{5,4,3,2,1,0:T(8,128)(2,1)S(1)}, bf16[2,2,2,4,128,384]{5,4,3,2,1,0:T(8,128)(2,1)S(1)}, u32[]{:S(2)}, u32[]{:S(2)}) collective-permute-start(bf16[2,2,2,4,128,384]{5,4,3,2,1,0:T(8,128)(2,1)S(1)} %get-tuple-element.164), channel_id=1, source_target_pairs={{0,2},{2,0},{4,6},{6,4},{8,10},{10,8},{12,14},{14,12},{16,18},{18,... | collective-permute-start | bytes 9437192 | tf_op jit(solution)/shard_map/cores_inputs/ppermute | solution.py:233
  151.8 7.5 %collective-permute-start.35 = (bf16[2,2,2,4,128,128]{5,4,3,2,1,0:T(8,128)(2,1)S(1)}, bf16[2,2,2,4,128,128]{5,4,3,2,1,0:T(8,128)(2,1)S(1)}, u32[]{:S(2)}, u32[]{:S(2)}) collective-permute-start(bf16[2,2,2,4,128,128]{5,4,3,2,1,0:T(8,128)(2,1)S(1)} %get-tuple-element.162), channel_id=1, source_target_pairs={{0,2},{2,0},{4,6},{6,4},{8,10},{10,8},{12,14},{14,12},{16,18},{18,... | collective-permute-start | bytes 3145736 | tf_op jit(solution)/shard_map/cores_inputs/ppermute | solution.py:233
  152.8 14.8 %collective-permute-start.39 = (bf16[4,128,512]{2,1,0:T(8,128)(2,1)S(1)}, bf16[4,128,512]{2,1,0:T(8,128)(2,1)S(1)}, u32[]{:S(2)}, u32[]{:S(2)}) collective-permute-start(bf16[4,128,512]{2,1,0:T(8,128)(2,1)S(1)} %get-tuple-element.217), channel_id=1, source_target_pairs={{0,1},{1,0},{2,3},{3,2},{4,5},{5,4},{6,7},{7,6},{8,9},{9,8},{10,11... | collective-permute-start | bytes 1572872 | tf_op jit(solution)/shard_map/across_mixed/ppermute | solution.py:239
  153.7 14.8 %collective-permute-start.40 = (bf16[4,128,512]{2,1,0:T(8,128)(2,1)S(1)}, bf16[4,128,512]{2,1,0:T(8,128)(2,1)S(1)}, u32[]{:S(2)}, u32[]{:S(2)}) collective-permute-start(bf16[4,128,512]{2,1,0:T(8,128)(2,1)S(1)} %get-tuple-element.216), channel_id=1, source_target_pairs={{0,4},{2,6},{4,0},{6,2},{8,12},{10,14},{12,8},{14,10},{16,20},{18,... | collective-permute-start | bytes 1572872 | tf_op jit(solution)/shard_map/across_mixed/ppermute | solution.py:236
  160.0 24.2 %collective-permute-start.37 = (bf16[2,4,128,384]{3,2,1,0:T(8,128)(2,1)S(1)}, bf16[2,4,128,384]{3,2,1,0:T(8,128)(2,1)S(1)}, u32[]{:S(2)}, u32[]{:S(2)}) collective-permute-start(bf16[2,4,128,384]{3,2,1,0:T(8,128)(2,1)S(1)} %get-tuple-element.169), channel_id=1, source_target_pairs={{0,4},{2,6},{4,0},{6,2},{8,12},{10,14},{12,8},{14,10},{16,20},{18,... | collective-permute-start | bytes 2359304 | tf_op jit(solution)/shard_map/over_inputs_1/ppermute | solution.py:236
  161.8 22.4 %collective-permute-start.38 = (bf16[2,4,128,384]{3,2,1,0:T(8,128)(2,1)S(1)}, bf16[2,4,128,384]{3,2,1,0:T(8,128)(2,1)S(1)}, u32[]{:S(2)}, u32[]{:S(2)}) collective-permute-start(bf16[2,4,128,384]{3,2,1,0:T(8,128)(2,1)S(1)} %get-tuple-element.170), channel_id=1, source_target_pairs={{0,1},{1,0},{2,3},{3,2},{4,5},{5,4},{6,7},{7,6},{8,9},{9,8},{10,11... | collective-permute-start | bytes 2359304 | tf_op jit(solution)/shard_map/over_inputs_1/ppermute | solution.py:239
  169.2 13.1 %collective-permute-start.41 = (bf16[2,128,512]{2,1,0:T(8,128)(2,1)S(1)}, bf16[2,128,512]{2,1,0:T(8,128)(2,1)S(1)}, u32[]{:S(2)}, u32[]{:S(2)}) collective-permute-start(bf16[2,128,512]{2,1,0:T(8,128)(2,1)S(1)} %get-tuple-element.234), channel_id=1, source_target_pairs={{0,24},{2,26},{4,28},{6,30},{8,0},{10,2},{12,4},{14,6},{16,8},{18,... | collective-permute-start | bytes 786440 | tf_op jit(solution)/shard_map/column_mixed/ppermute | solution.py:242
  171.4 11.0 %collective-permute-start.42 = (bf16[2,128,512]{2,1,0:T(8,128)(2,1)S(1)}, bf16[2,128,512]{2,1,0:T(8,128)(2,1)S(1)}, u32[]{:S(2)}, u32[]{:S(2)}) collective-permute-start(bf16[2,128,512]{2,1,0:T(8,128)(2,1)S(1)} %get-tuple-element.233), channel_id=1, source_target_pairs={{0,8},{2,10},{4,12},{6,14},{8,16},{10,18},{12,20},{14,22},{16,24},... | collective-permute-start | bytes 786440 | tf_op jit(solution)/shard_map/column_mixed/ppermute | solution.py:242
  184.5 14.7 %collective-permute-start.45 = (bf16[4,128,384]{2,1,0:T(8,128)(2,1)S(1)}, bf16[4,128,384]{2,1,0:T(8,128)(2,1)S(1)}, u32[]{:S(2)}, u32[]{:S(2)}) collective-permute-start(bf16[4,128,384]{2,1,0:T(8,128)(2,1)S(1)} %get-tuple-element.223), channel_id=1, source_target_pairs={{0,1},{1,0},{2,3},{3,2},{4,5},{5,4},{6,7},{7,6},{8,9},{9,8},{10,11... | collective-permute-start | bytes 1179656 | tf_op jit(solution)/shard_map/across_inputs_1/ppermute | solution.py:239
  185.8 13.4 %collective-permute-start.46 = (bf16[4,128,384]{2,1,0:T(8,128)(2,1)S(1)}, bf16[4,128,384]{2,1,0:T(8,128)(2,1)S(1)}, u32[]{:S(2)}, u32[]{:S(2)}) collective-permute-start(bf16[4,128,384]{2,1,0:T(8,128)(2,1)S(1)} %get-tuple-element.222), channel_id=1, source_target_pairs={{0,4},{2,6},{4,0},{6,2},{8,12},{10,14},{12,8},{14,10},{16,20},{18,... | collective-permute-start | bytes 1179656 | tf_op jit(solution)/shard_map/across_inputs_1/ppermute | solution.py:236
  186.1 13.1 %collective-permute-start.47 = (bf16[2,128,512]{2,1,0:T(8,128)(2,1)S(1)}, bf16[2,128,512]{2,1,0:T(8,128)(2,1)S(1)}, u32[]{:S(2)}, u32[]{:S(2)}) collective-permute-start(bf16[2,128,512]{2,1,0:T(8,128)(2,1)S(1)} %get-tuple-element.232), channel_id=1, source_target_pairs={{0,16},{2,18},{4,20},{6,22},{8,24},{10,26},{12,28},{14,30},{16,0},... | collective-permute-start | bytes 786440 | tf_op jit(solution)/shard_map/column_mixed/ppermute | solution.py:242
  186.5 15.3 %collective-permute-start.43 = (bf16[2,4,128,128]{3,2,1,0:T(8,128)(2,1)S(1)}, bf16[2,4,128,128]{3,2,1,0:T(8,128)(2,1)S(1)}, u32[]{:S(2)}, u32[]{:S(2)}) collective-permute-start(bf16[2,4,128,128]{3,2,1,0:T(8,128)(2,1)S(1)} %get-tuple-element.181), channel_id=1, source_target_pairs={{0,4},{2,6},{4,0},{6,2},{8,12},{10,14},{12,8},{14,10},{16,20},{18,... | collective-permute-start | bytes 786440 | tf_op jit(solution)/shard_map/over_inputs_2/ppermute | solution.py:236
  188.1 13.7 %collective-permute-start.44 = (bf16[2,4,128,128]{3,2,1,0:T(8,128)(2,1)S(1)}, bf16[2,4,128,128]{3,2,1,0:T(8,128)(2,1)S(1)}, u32[]{:S(2)}, u32[]{:S(2)}) collective-permute-start(bf16[2,4,128,128]{3,2,1,0:T(8,128)(2,1)S(1)} %get-tuple-element.182), channel_id=1, source_target_pairs={{0,1},{1,0},{2,3},{3,2},{4,5},{5,4},{6,7},{7,6},{8,9},{9,8},{10,11... | collective-permute-start | bytes 786440 | tf_op jit(solution)/shard_map/over_inputs_2/ppermute | solution.py:239
  199.6 19.5 %collective-permute-start.53 = (bf16[2,128,384]{2,1,0:T(8,128)(2,1)S(1)}, bf16[2,128,384]{2,1,0:T(8,128)(2,1)S(1)}, u32[]{:S(2)}, u32[]{:S(2)}) collective-permute-start(bf16[2,128,384]{2,1,0:T(8,128)(2,1)S(1)} %get-tuple-element.235), channel_id=1, source_target_pairs={{0,24},{2,26},{4,28},{6,30},{8,0},{10,2},{12,4},{14,6},{16,8},{18,... | collective-permute-start | bytes 589832 | tf_op jit(solution)/shard_map/column_inputs_1/ppermute | solution.py:242
  201.0 19.3 %collective-permute-start.54 = (bf16[2,128,384]{2,1,0:T(8,128)(2,1)S(1)}, bf16[2,128,384]{2,1,0:T(8,128)(2,1)S(1)}, u32[]{:S(2)}, u32[]{:S(2)}) collective-permute-start(bf16[2,128,384]{2,1,0:T(8,128)(2,1)S(1)} %get-tuple-element.237), channel_id=1, source_target_pairs={{0,16},{2,18},{4,20},{6,22},{8,24},{10,26},{12,28},{14,30},{16,0},... | collective-permute-start | bytes 589832 | tf_op jit(solution)/shard_map/column_inputs_1/ppermute | solution.py:242
  201.1 19.2 %collective-permute-start.55 = (bf16[2,128,384]{2,1,0:T(8,128)(2,1)S(1)}, bf16[2,128,384]{2,1,0:T(8,128)(2,1)S(1)}, u32[]{:S(2)}, u32[]{:S(2)}) collective-permute-start(bf16[2,128,384]{2,1,0:T(8,128)(2,1)S(1)} %get-tuple-element.236), channel_id=1, source_target_pairs={{0,8},{2,10},{4,12},{6,14},{8,16},{10,18},{12,20},{14,22},{16,24},... | collective-permute-start | bytes 589832 | tf_op jit(solution)/shard_map/column_inputs_1/ppermute | solution.py:242
  209.2 12.0 %all-to-all-start = ((f32[16,1,128]{2,1,0:T(1,128)}), f32[16,1,128]{2,1,0:T(1,128)S(1)}, u32[]{:S(2)}, u32[]{:S(2)}) async-start(f32[16,1,128]{2,1,0:T(1,128)} %bitcast.94), calls=%async_computation | async-start | bytes 16384 | tf_op jit(solution)/shard_map/gates/all_to_all | solution.py:302
  215.4 6.5 %collective-permute-start.50 = (bf16[2,128,128]{2,1,0:T(8,128)(2,1)}, bf16[2,128,128]{2,1,0:T(8,128)(2,1)S(1)}, u32[]{:S(2)}, u32[]{:S(2)}) collective-permute-start(bf16[2,128,128]{2,1,0:T(8,128)(2,1)} %get-tuple-element.246), channel_id=1, source_target_pairs={{0,24},{2,26},{4,28},{6,30},{8,0},{10,2},{12,4},{14,6},{16,8},{18,... | collective-permute-start | bytes 196616 | tf_op jit(solution)/shard_map/column_inputs_2/ppermute | solution.py:242
  219.1 7.1 %collective-permute-start.51 = (bf16[2,128,128]{2,1,0:T(8,128)(2,1)}, bf16[2,128,128]{2,1,0:T(8,128)(2,1)S(1)}, u32[]{:S(2)}, u32[]{:S(2)}) collective-permute-start(bf16[2,128,128]{2,1,0:T(8,128)(2,1)} %get-tuple-element.245), channel_id=1, source_target_pairs={{0,16},{2,18},{4,20},{6,22},{8,24},{10,26},{12,28},{14,30},{16,0},... | collective-permute-start | bytes 196616 | tf_op jit(solution)/shard_map/column_inputs_2/ppermute | solution.py:242
  219.1 7.1 %collective-permute-start.52 = (bf16[2,128,128]{2,1,0:T(8,128)(2,1)}, bf16[2,128,128]{2,1,0:T(8,128)(2,1)S(1)}, u32[]{:S(2)}, u32[]{:S(2)}) collective-permute-start(bf16[2,128,128]{2,1,0:T(8,128)(2,1)} %get-tuple-element.244), channel_id=1, source_target_pairs={{0,8},{2,10},{4,12},{6,14},{8,16},{10,18},{12,20},{14,22},{16,24},... | collective-permute-start | bytes 196616 | tf_op jit(solution)/shard_map/column_inputs_2/ppermute | solution.py:242
  (30 other events, 227.2 us)

commit v6 on v5

--- a/solution.py
+++ b/solution.py
@@ -488,12 +488,15 @@
     with jax.named_scope("over_inputs_1"):
         first_1 = over(*send_1)
     with jax.named_scope("column_mixed"):
+        grad_gate_pre, send_1 = together(grad_gate_pre, send_1)
+        (grad_gate,) = weight_grads(rows, grad_gate_pre)
+        mix_second, grad_gate = together(mix_second, grad_gate)
         mix_both = sent_column(mix_own, mix_core, mix_first, mix_second)
         mix_received = from_column(mix_both)
-    grad_gate_pre, mix_both = together(grad_gate_pre, mix_both)
-    grad_gate, grad_up = weight_grads(rows, grad_gate_pre, grad_up_pre)
-    first_1, send_2, mix_received[::2], grad_gate, grad_up = together(
-        first_1, send_2, mix_received[::2], grad_gate, grad_up
+    grad_up_pre, mix_both = together(grad_up_pre, mix_both)
+    (grad_up,) = weight_grads(rows, grad_up_pre)
+    first_1, send_2, mix_received[1:], grad_gate, grad_up = together(
+        first_1, send_2, mix_received[1:], grad_gate, grad_up
     )
     with jax.named_scope("across_inputs_1"):
         send_1 = sent_second(own_1, core_1, first_1)

time: 228 us -> 230 us (level)
  waiting for transfers between devices: 80.3 us -> 84.2 us
    ppermute x17, waiting for transfers between devices: 43 us -> 49.1 us  [shift(): lax.ppermute(value, 'expert', [(e, (e + 4 * step) % expert_count) for e i...]
    pallas_call x2 -> x3, Pallas kernels: 14.1 us -> 16.1 us  [weight_grads(): pl.pallas_call(functools.partial(weight_kernel, len(lefts)), out_shape=[s...]
  transfers between devices with their start and end apart: 57 -> 57, of which waited for: 28 -> 30; matrix products, arithmetic and copies ran while one was open for 8% -> 8% of each run, Pallas kernels for 24% -> 25%
where the time goes in v6:
time: 230 us
  waiting for transfers between devices  84.2 us (37%)
  starting transfers between devices  60.4 us (26%)
  Pallas kernels  57.6 us (25%)
  other arithmetic  14.5 us (6%)
  local copies, waits for them, and re-layouts  9.91 us (4%)
    ppermute x17, waiting for transfers between devices, shift(): lax.ppermute(value, 'expert', [(e, (e + 4 * step) % expert_count) for e i...  49.1 us
    ppermute x17, starting transfers between devices, shift(): lax.ppermute(value, 'expert', [(e, (e + 4 * step) % expert_count) for e i...  23.3 us
    pallas_call x3, Pallas kernels, weight_grads(): pl.pallas_call(functools.partial(weight_kernel, len(lefts)), out_shape=[s...  16.1 us
    pallas_call x1, Pallas kernels, gather_body(): kernel(up_kernel, [table, table] + [piece_of(piece) for piece in pieces]...  13.5 us
    pallas_call x2, Pallas kernels, input_terms(): kernel(input_kernel, [table, rows_of(hidden), rows_of(hidden)] + blocks *...  13 us
    ppermute x12, starting transfers between devices, swap_side(): return lax.ppermute(value, 'tensor', [(0, 1), (1, 0)])  12.9 us
    ppermute x11, starting transfers between devices, swap_pair(): return lax.ppermute(value, 'expert', chip_pairs)  12.8 us
    ppermute x12, waiting for transfers between devices, swap_side(): return lax.ppermute(value, 'tensor', [(0, 1), (1, 0)])  10.9 us
  transfers between devices with their start and end apart: 57, of which 30 were waited for; matrix products, arithmetic and copies ran while one was open for 8% of the time, Pallas kernels for 25%

profile of v6, /device:TPU:0, one launch (start us, length us, event | category | flops | bytes accessed | tf_op | source)
XLA Modules:
  0.0 229.8 jit_solution(11676133327775329839)
XLA Ops:
  3.1 3.1 %collective-permute-start = (bf16[264,512]{1,0:T(8,128)(2,1)S(1)}, bf16[264,512]{1,0:T(8,128)(2,1)S(1)}, u32[]{:S(2)}, u32[]{:S(2)}) collective-permute-start(bf16[264,512]{1,0:T(8,128)(2,1)S(1)} %pad_maximum_fusion.11), channel_id=1, source_target_pairs={{0,8},{2,10},{4,12},{6,14},{8,16},{10,18},{12,20},{14,22},{16,24},... | collective-permute-start | bytes 811016 | tf_op jit(solution)/shard_map/column_tokens/ppermute | solution.py:242
  6.2 2.1 collective-permute-start.2
  8.3 2.9 %collective-permute-start.1 = (bf16[264,512]{1,0:T(8,128)(2,1)S(1)}, bf16[264,512]{1,0:T(8,128)(2,1)S(1)}, u32[]{:S(2)}, u32[]{:S(2)}) collective-permute-start(bf16[264,512]{1,0:T(8,128)(2,1)S(1)} %pad_maximum_fusion.11), channel_id=1, source_target_pairs={{0,16},{2,18},{4,20},{6,22},{24,8},{26,10},{28,12},{30,14},{1,17},... | collective-permute-start | bytes 811016 | tf_op jit(solution)/shard_map/column_tokens/ppermute | solution.py:262
  11.2 4.4 %collective-permute-done = bf16[264,512]{1,0:T(8,128)(2,1)S(1)} collective-permute-done((bf16[264,512]{1,0:T(8,128)(2,1)S(1)}, bf16[264,512]{1,0:T(8,128)(2,1)S(1)}, u32[]{:S(2)}, u32[]{:S(2)}) %collective-permute-start) | collective-permute-done | bytes 270368 | tf_op jit(solution)/shard_map/column_tokens/ppermute | solution.py:242
  15.6 4.4 %collective-permute-done.2 = bf16[264,512]{1,0:T(8,128)(2,1)S(1)} collective-permute-done((bf16[264,512]{1,0:T(8,128)(2,1)S(1)}, bf16[264,512]{1,0:T(8,128)(2,1)S(1)}, u32[]{:S(2)}, u32[]{:S(2)}) %collective-permute-start.2) | collective-permute-done | bytes 270368 | tf_op jit(solution)/shard_map/column_tokens/ppermute | solution.py:242
  20.0 1.3 collective-permute-start.3
  21.4 2.2 collective-permute-done.1
  23.6 6.1 %collective-permute-done.3 = bf16[264,512]{1,0:T(8,128)(2,1)S(1)} collective-permute-done((bf16[264,512]{1,0:T(8,128)(2,1)S(1)}, bf16[264,512]{1,0:T(8,128)(2,1)S(1)}, u32[]{:S(2)}, u32[]{:S(2)}) %collective-permute-start.3) | collective-permute-done | bytes 270368 | tf_op jit(solution)/shard_map/column_tokens/ppermute | solution.py:264
  30.0 1.8 collective-permute-start.5
  32.7 1.5 collective-permute-start.4
  34.8 5.9 %collective-permute-start.7 = (bf16[2,128,256]{2,1,0:T(8,128)(2,1)S(1)}, bf16[2,128,256]{2,1,0:T(8,128)(2,1)S(1)}, u32[]{:S(2)}, u32[]{:S(2)}) collective-permute-start(bf16[2,128,256]{2,1,0:T(8,128)(2,1)S(1)} %get-tuple-element.125), channel_id=1, source_target_pairs={{0,16},{2,18},{4,20},{6,22},{8,24},{10,26},{12,28},{14,30},{16,0},... | collective-permute-start | bytes 393224 | tf_op jit(solution)/shard_map/across_tokens/ppermute | solution.py:242
  41.2 2.1 collective-permute-done.6
  43.2 3.3 %collective-permute-done.7 = bf16[2,128,256]{2,1,0:T(8,128)(2,1)S(1)} collective-permute-done((bf16[2,128,256]{2,1,0:T(8,128)(2,1)S(1)}, bf16[2,128,256]{2,1,0:T(8,128)(2,1)S(1)}, u32[]{:S(2)}, u32[]{:S(2)}) %collective-permute-start.7) | collective-permute-done | bytes 131104 | tf_op jit(solution)/shard_map/across_tokens/ppermute | solution.py:242
  54.7 5.0 %collective-permute-done.13 = bf16[2,128,256]{2,1,0:T(8,128)(2,1)} collective-permute-done((bf16[2,128,256]{2,1,0:T(8,128)(2,1)S(1)}, bf16[2,128,256]{2,1,0:T(8,128)(2,1)}, u32[]{:S(2)}, u32[]{:S(2)}) %collective-permute-start.13) | collective-permute-done | bytes 131104 | tf_op jit(solution)/shard_map/over_tokens/ppermute | solution.py:242
  61.0 5.9 %collective-permute-done.14 = bf16[2,128,256]{2,1,0:T(8,128)(2,1)} collective-permute-done((bf16[2,128,256]{2,1,0:T(8,128)(2,1)S(1)}, bf16[2,128,256]{2,1,0:T(8,128)(2,1)}, u32[]{:S(2)}, u32[]{:S(2)}) %collective-permute-start.14) | collective-permute-done | bytes 131104 | tf_op jit(solution)/shard_map/over_tokens/ppermute | solution.py:242
  68.1 1.5 fusion.pos
  69.6 2.6 %collective-permute-done.15 = bf16[2,128,256]{2,1,0:T(8,128)(2,1)S(1)} collective-permute-done((bf16[2,128,256]{2,1,0:T(8,128)(2,1)S(1)}, bf16[2,128,256]{2,1,0:T(8,128)(2,1)S(1)}, u32[]{:S(2)}, u32[]{:S(2)}) %collective-permute-start.15) | collective-permute-done | bytes 131104 | tf_op jit(solution)/shard_map/over_tokens/ppermute | solution.py:242
  72.3 2.6 %collective-permute-done.9.refs_1_ = bf16[2,4,128,512]{3,2,1,0:T(8,128)(2,1)} collective-permute-done((bf16[2,4,128,512]{3,2,1,0:T(8,128)(2,1)S(1)}, bf16[2,4,128,512]{3,2,1,0:T(8,128)(2,1)}, u32[]{:S(2)}, u32[]{:S(2)}) %collective-permute-start.9) | collective-permute-done | bytes 1048608 | tf_op jit(solution)/shard_map/over_tokens/ppermute | solution.py:236
  78.7 1.3 collective-permute-start.19
  80.6 13.5 %shard_map.118 = (bf16[1024,2048]{1,0:T(8,128)(2,1)}, f32[1024,704]{1,0:T(8,128)}, f32[1024,704]{1,0:T(8,128)}, bf16[1024,704]{1,0:T(8,128)(2,1)}) custom-call(s32[1]{0:T(128)} %bitcast.side, f32[4,4,128]{2,1,0:T(4,128)} %fusion.pos, f32[4,4,128]{2,1,0:T(4,128)} %copy.49.gate, bf16[2,4,128,512]{3,2,1,0:T(8,128)(2,1)} %copy-done.10, ...), custom_call_target="tpu_custom_call" | custom-call | flops 1048576 | bytes 65536 | tf_op jit(solution)/shard_map/pallas_call | solution.py:417
  96.0 1.8 collective-permute-start.21
  97.7 7.2 %shard_map.119 = (bf16[2,2,2,4,128,512]{5,4,3,2,1,0:T(8,128)(2,1)S(1)}, bf16[2,2,2,4,128,512]{5,4,3,2,1,0:T(8,128)(2,1)S(1)}) custom-call(s32[1]{0:T(128)} %bitcast.side, f32[4,4,128]{2,1,0:T(4,128)S(1)} %copy-done.7, bf16[1024,704]{1,0:T(8,128)(2,1)S(1)} %copy-done.4, bf16[704,2048]{1,0:T(8,128)(2,1)S(1)} %bitcast.252), custom_call_target="tpu_custom_call" | custom-call | flops 1048576 | bytes 65536 | tf_op jit(solution)/shard_map/pallas_call | solution.py:429
  104.9 4.1 %collective-permute-done.22.refs_5_ = bf16[2,4,128,256]{3,2,1,0:T(8,128)(2,1)S(1)} collective-permute-done((bf16[2,4,128,256]{3,2,1,0:T(8,128)(2,1)S(1)}, bf16[2,4,128,256]{3,2,1,0:T(8,128)(2,1)S(1)}, u32[]{:S(2)}, u32[]{:S(2)}) %collective-permute-start.22) | collective-permute-done | bytes 524320 | tf_op jit(solution)/shard_map/over_grads_1/ppermute | solution.py:239
  110.2 1.8 collective-permute-start.28
  113.3 3.4 %collective-permute-done.27 = bf16[2,2,2,4,128,512]{5,4,3,2,1,0:T(8,128)(2,1)S(1)} collective-permute-done((bf16[2,2,2,4,128,512]{5,4,3,2,1,0:T(8,128)(2,1)S(1)}, bf16[2,2,2,4,128,512]{5,4,3,2,1,0:T(8,128)(2,1)S(1)}, u32[]{:S(2)}, u32[]{:S(2)}) %collective-permute-start.27) | collective-permute-done | bytes 4194336 | tf_op jit(solution)/shard_map/cores_mixed/ppermute | solution.py:233
  117.5 1.4 copy-done.11
  118.9 1.8 collective-permute-start.32
  121.9 3.1 %collective-permute-done.28.refs_9_ = bf16[2,4,128,256]{3,2,1,0:T(8,128)(2,1)S(1)} collective-permute-done((bf16[2,4,128,256]{3,2,1,0:T(8,128)(2,1)S(1)}, bf16[2,4,128,256]{3,2,1,0:T(8,128)(2,1)S(1)}, u32[]{:S(2)}, u32[]{:S(2)}) %collective-permute-start.28) | collective-permute-done | bytes 524320 | tf_op jit(solution)/shard_map/over_grads_2/ppermute | solution.py:236
  125.0 1.9 collective-permute-done.29.refs_13_
  129.6 7.9 %shard_map.120 = (bf16[1024,2048]{1,0:T(8,128)(2,1)S(1)}, bf16[1024,704]{1,0:T(8,128)(2,1)S(1)}, bf16[1024,704]{1,0:T(8,128)(2,1)S(1)}, f32[4,4,128]{2,1,0:T(4,128)S(1)}) custom-call(s32[1]{0:T(128)} %bitcast.side, f32[4,4,128]{2,1,0:T(4,128)S(1)} %copy-done.7, f32[4,4,128]{2,1,0:T(4,128)S(1)} %copy-done.8, ...), custom_call_target="tpu_custom_call" | custom-call | flops 1048576 | bytes 65536 | tf_op jit(solution)/shard_map/pallas_call | solution.py:453
  137.4 1.3 collective-permute-start.34
  138.7 3.8 %shard_map.121 = (bf16[2,2,2,4,128,128]{5,4,3,2,1,0:T(8,128)(2,1)S(1)}, bf16[2,2,2,4,128,128]{5,4,3,2,1,0:T(8,128)(2,1)S(1)}) custom-call(s32[1]{0:T(128)} %bitcast.side, f32[4,4,128]{2,1,0:T(4,128)S(1)} %copy-done.7, bf16[1024,704]{1,0:T(8,128)(2,1)S(1)} %get-tuple-element.175.grad_gate_pre.refs_0_, ...), custom_call_target="tpu_custom_call" | custom-call | flops 1048576 | bytes 65536 | tf_op jit(solution)/shard_map/pallas_call | solution.py:467
  142.6 9.1 %shard_map.122 = (bf16[2,2,2,4,128,384]{5,4,3,2,1,0:T(8,128)(2,1)S(1)}, bf16[2,2,2,4,128,384]{5,4,3,2,1,0:T(8,128)(2,1)S(1)}) custom-call(s32[1]{0:T(128)} %bitcast.side, f32[4,4,128]{2,1,0:T(4,128)S(1)} %copy-done.7, bf16[1024,704]{1,0:T(8,128)(2,1)S(1)} %get-tuple-element.175.grad_gate_pre.refs_0_, ...), custom_call_target="tpu_custom_call" | custom-call | flops 1048576 | bytes 65536 | tf_op jit(solution)/shard_map/pallas_call | solution.py:467
  154.0 5.4 %shard_map.123 = bf16[704,2048]{1,0:T(8,128)(2,1)} custom-call(bf16[1024,704]{1,0:T(8,128)(2,1)S(1)} %copy-done.4, bf16[1024,2048]{1,0:T(8,128)(2,1)S(1)} %get-tuple-element.170.refs_1_), custom_call_target="tpu_custom_call" | custom-call | flops 1048576 | bytes 65536 | tf_op jit(solution)/shard_map/pallas_call | solution.py:366
  160.0 1.8 collective-permute-start.37
  163.0 5.4 %column_mixed.1 = bf16[704,2048]{1,0:T(8,128)(2,1)} custom-call(bf16[1024,704]{1,0:T(8,128)(2,1)S(1)} %get-tuple-element.175.grad_gate_pre.refs_0_, bf16[1024,2048]{1,0:T(8,128)(2,1)S(1)} %copy-done.2), custom_call_target="tpu_custom_call" | custom-call | flops 1048576 | bytes 65536 | tf_op jit(solution)/shard_map/column_mixed/pallas_call | solution.py:366
  169.6 2.2 collective-permute-start.42
  172.0 5.4 %shard_map.124 = bf16[704,2048]{1,0:T(8,128)(2,1)} custom-call(bf16[1024,704]{1,0:T(8,128)(2,1)S(1)} %get-tuple-element.180.grad_up_pre.refs_0_, bf16[1024,2048]{1,0:T(8,128)(2,1)S(1)} %copy-done.2), custom_call_target="tpu_custom_call" | custom-call | flops 1048576 | bytes 65536 | tf_op jit(solution)/shard_map/pallas_call | solution.py:366
  177.4 11.1 %collective-permute-done.41 = bf16[2,128,512]{2,1,0:T(8,128)(2,1)S(1)} collective-permute-done((bf16[2,128,512]{2,1,0:T(8,128)(2,1)S(1)}, bf16[2,128,512]{2,1,0:T(8,128)(2,1)S(1)}, u32[]{:S(2)}, u32[]{:S(2)}) %collective-permute-start.41) | collective-permute-done | bytes 262176 | tf_op jit(solution)/shard_map/column_mixed/ppermute | solution.py:242
  189.7 1.3 collective-permute-start.46
  193.1 4.8 %collective-permute-done.47 = bf16[2,128,512]{2,1,0:T(8,128)(2,1)S(1)} collective-permute-done((bf16[2,128,512]{2,1,0:T(8,128)(2,1)S(1)}, bf16[2,128,512]{2,1,0:T(8,128)(2,1)S(1)}, u32[]{:S(2)}, u32[]{:S(2)}) %collective-permute-start.47) | collective-permute-done | bytes 262176 | tf_op jit(solution)/shard_map/column_mixed/ppermute | solution.py:242
  197.9 3.1 %collective-permute-done.45 = bf16[4,128,384]{2,1,0:T(8,128)(2,1)S(1)} collective-permute-done((bf16[4,128,384]{2,1,0:T(8,128)(2,1)S(1)}, bf16[4,128,384]{2,1,0:T(8,128)(2,1)S(1)}, u32[]{:S(2)}, u32[]{:S(2)}) %collective-permute-start.45) | collective-permute-done | bytes 393248 | tf_op jit(solution)/shard_map/across_inputs_1/ppermute | solution.py:239
  202.7 1.9 collective-permute-start.55
  205.4 1.3 collective-permute-start.48
  208.5 1.9 collective-permute-done.48
  213.0 3.9 %all-to-all-start = ((f32[16,1,128]{2,1,0:T(1,128)}), f32[16,1,128]{2,1,0:T(1,128)S(1)}, u32[]{:S(2)}, u32[]{:S(2)}) async-start(f32[16,1,128]{2,1,0:T(1,128)} %bitcast.94), calls=%async_computation | async-start | bytes 16384 | tf_op jit(solution)/shard_map/gates/all_to_all | solution.py:302
  217.6 3.7 %collective-permute-start.50 = (bf16[2,128,128]{2,1,0:T(8,128)(2,1)}, bf16[2,128,128]{2,1,0:T(8,128)(2,1)S(1)}, u32[]{:S(2)}, u32[]{:S(2)}) collective-permute-start(bf16[2,128,128]{2,1,0:T(8,128)(2,1)} %get-tuple-element.250), channel_id=1, source_target_pairs={{0,24},{2,26},{4,28},{6,30},{8,0},{10,2},{12,4},{14,6},{16,8},{18,... | collective-permute-start | bytes 196616 | tf_op jit(solution)/shard_map/column_inputs_2/ppermute | solution.py:242
  224.1 4.3 %collective-permute-done.51 = bf16[2,128,128]{2,1,0:T(8,128)(2,1)S(1)} collective-permute-done((bf16[2,128,128]{2,1,0:T(8,128)(2,1)}, bf16[2,128,128]{2,1,0:T(8,128)(2,1)S(1)}, u32[]{:S(2)}, u32[]{:S(2)}) %collective-permute-start.51) | collective-permute-done | bytes 65568 | tf_op jit(solution)/shard_map/column_inputs_2/ppermute | solution.py:242
  (205 shorter events, 48.9 us)
Async XLA Ops:
  3.1 12.5 %collective-permute-start = (bf16[264,512]{1,0:T(8,128)(2,1)S(1)}, bf16[264,512]{1,0:T(8,128)(2,1)S(1)}, u32[]{:S(2)}, u32[]{:S(2)}) collective-permute-start(bf16[264,512]{1,0:T(8,128)(2,1)S(1)} %pad_maximum_fusion.11), channel_id=1, source_target_pairs={{0,8},{2,10},{4,12},{6,14},{8,16},{10,18},{12,20},{14,22},{16,24},... | collective-permute-start | bytes 811016 | tf_op jit(solution)/shard_map/column_tokens/ppermute | solution.py:242
  6.2 13.7 %collective-permute-start.2 = (bf16[264,512]{1,0:T(8,128)(2,1)S(1)}, bf16[264,512]{1,0:T(8,128)(2,1)S(1)}, u32[]{:S(2)}, u32[]{:S(2)}) collective-permute-start(bf16[264,512]{1,0:T(8,128)(2,1)S(1)} %pad_maximum_fusion.11), channel_id=1, source_target_pairs={{0,24},{2,26},{4,28},{6,30},{8,0},{10,2},{12,4},{14,6},{16,8},{18,... | collective-permute-start | bytes 811016 | tf_op jit(solution)/shard_map/column_tokens/ppermute | solution.py:242
  8.3 15.3 %collective-permute-start.1 = (bf16[264,512]{1,0:T(8,128)(2,1)S(1)}, bf16[264,512]{1,0:T(8,128)(2,1)S(1)}, u32[]{:S(2)}, u32[]{:S(2)}) collective-permute-start(bf16[264,512]{1,0:T(8,128)(2,1)S(1)} %pad_maximum_fusion.11), channel_id=1, source_target_pairs={{0,16},{2,18},{4,20},{6,22},{24,8},{26,10},{28,12},{30,14},{1,17},... | collective-permute-start | bytes 811016 | tf_op jit(solution)/shard_map/column_tokens/ppermute | solution.py:262
  20.0 9.8 %collective-permute-start.3 = (bf16[264,512]{1,0:T(8,128)(2,1)S(1)}, bf16[264,512]{1,0:T(8,128)(2,1)S(1)}, u32[]{:S(2)}, u32[]{:S(2)}) collective-permute-start(bf16[264,512]{1,0:T(8,128)(2,1)S(1)} %broadcast_select_fusion), channel_id=1, source_target_pairs={{8,0},{10,2},{12,4},{14,6},{16,24},{18,26},{20,28},{22,30},{9,1},{... | collective-permute-start | bytes 811016 | tf_op jit(solution)/shard_map/column_tokens/ppermute | solution.py:264
  30.0 17.0 %collective-permute-start.5 = (bf16[4,136,512]{2,1,0:T(8,128)(2,1)S(1)}, bf16[4,136,512]{2,1,0:T(8,128)(2,1)S(1)}, u32[]{:S(2)}, u32[]{:S(2)}) collective-permute-start(bf16[4,136,512]{2,1,0:T(8,128)(2,1)S(1)} %pad_maximum_fusion.6), channel_id=1, source_target_pairs={{0,4},{2,6},{4,0},{6,2},{8,12},{10,14},{12,8},{14,10},{16,20},{18,... | collective-permute-start | bytes 1671176 | tf_op jit(solution)/shard_map/across_tokens/ppermute | solution.py:236
  32.7 14.3 %collective-permute-start.4 = (bf16[4,128,512]{2,1,0:T(8,128)(2,1)S(1)}, bf16[4,128,512]{2,1,0:T(8,128)(2,1)S(1)}, u32[]{:S(2)}, u32[]{:S(2)}) collective-permute-start(bf16[4,128,512]{2,1,0:T(8,128)(2,1)S(1)} %get-tuple-element.247), channel_id=1, source_target_pairs={{0,1},{1,0},{2,3},{3,2},{4,5},{5,4},{6,7},{7,6},{8,9},{9,8},{10,11... | collective-permute-start | bytes 1572872 | tf_op jit(solution)/shard_map/across_tokens/ppermute | solution.py:239
  34.8 8.4 %collective-permute-start.6 = (bf16[2,128,256]{2,1,0:T(8,128)(2,1)S(1)}, bf16[2,128,256]{2,1,0:T(8,128)(2,1)S(1)}, u32[]{:S(2)}, u32[]{:S(2)}) collective-permute-start(bf16[2,128,256]{2,1,0:T(8,128)(2,1)S(1)} %get-tuple-element.125), channel_id=1, source_target_pairs={{0,8},{2,10},{4,12},{6,14},{8,16},{10,18},{12,20},{14,22},{16,24},... | collective-permute-start | bytes 393224 | tf_op jit(solution)/shard_map/across_tokens/ppermute | solution.py:242
  34.8 11.7 %collective-permute-start.7 = (bf16[2,128,256]{2,1,0:T(8,128)(2,1)S(1)}, bf16[2,128,256]{2,1,0:T(8,128)(2,1)S(1)}, u32[]{:S(2)}, u32[]{:S(2)}) collective-permute-start(bf16[2,128,256]{2,1,0:T(8,128)(2,1)S(1)} %get-tuple-element.125), channel_id=1, source_target_pairs={{0,16},{2,18},{4,20},{6,22},{8,24},{10,26},{12,28},{14,30},{16,0},... | collective-permute-start | bytes 393224 | tf_op jit(solution)/shard_map/across_tokens/ppermute | solution.py:242
  48.0 24.3 %collective-permute-start.10 = (bf16[2,4,128,512]{3,2,1,0:T(8,128)(2,1)S(1)}, bf16[2,4,128,512]{3,2,1,0:T(8,128)(2,1)}, u32[]{:S(2)}, u32[]{:S(2)}) collective-permute-start(bf16[2,4,128,512]{3,2,1,0:T(8,128)(2,1)S(1)} %pad_maximum_fusion.5.refs_4_), channel_id=1, source_target_pairs={{0,1},{1,0},{2,3},{3,2},{4,5},{5,4},{6,7},{7,6},{8,9},{9,8},{10,11... | collective-permute-start | bytes 3145736 | tf_op jit(solution)/shard_map/over_tokens/ppermute | solution.py:239
  48.1 24.2 %collective-permute-start.12 = (bf16[2,4,128,512]{3,2,1,0:T(8,128)(2,1)S(1)}, bf16[2,4,128,512]{3,2,1,0:T(8,128)(2,1)S(1)}, u32[]{:S(2)}, u32[]{:S(2)}) collective-permute-start(bf16[2,4,128,512]{3,2,1,0:T(8,128)(2,1)S(1)} %pad_maximum_fusion.5.refs_4_), channel_id=1, source_target_pairs={{0,2},{2,0},{4,6},{6,4},{8,10},{10,8},{12,14},{14,12},{16,18},{18,... | collective-permute-start | bytes 3145736 | tf_op jit(solution)/shard_map/over_tokens/ppermute | solution.py:233
  49.1 23.2 %collective-permute-start.11 = (bf16[2,4,128,512]{3,2,1,0:T(8,128)(2,1)S(1)}, bf16[2,4,128,512]{3,2,1,0:T(8,128)(2,1)}, u32[]{:S(2)}, u32[]{:S(2)}) collective-permute-start(bf16[2,4,128,512]{3,2,1,0:T(8,128)(2,1)S(1)} %pad_maximum_fusion.4.refs_0_), channel_id=1, source_target_pairs={{0,2},{2,0},{4,6},{6,4},{8,10},{10,8},{12,14},{14,12},{16,18},{18,... | collective-permute-start | bytes 3145736 | tf_op jit(solution)/shard_map/over_tokens/ppermute | solution.py:233
  49.2 25.7 %collective-permute-start.9 = (bf16[2,4,128,512]{3,2,1,0:T(8,128)(2,1)S(1)}, bf16[2,4,128,512]{3,2,1,0:T(8,128)(2,1)}, u32[]{:S(2)}, u32[]{:S(2)}) collective-permute-start(bf16[2,4,128,512]{3,2,1,0:T(8,128)(2,1)S(1)} %pad_maximum_fusion.4.refs_0_), channel_id=1, source_target_pairs={{0,4},{2,6},{4,0},{6,2},{8,12},{10,14},{12,8},{14,10},{16,20},{18,... | collective-permute-start | bytes 3145736 | tf_op jit(solution)/shard_map/over_tokens/ppermute | solution.py:236
  52.0 7.7 %collective-permute-start.13 = (bf16[2,128,256]{2,1,0:T(8,128)(2,1)S(1)}, bf16[2,128,256]{2,1,0:T(8,128)(2,1)}, u32[]{:S(2)}, u32[]{:S(2)}) collective-permute-start(bf16[2,128,256]{2,1,0:T(8,128)(2,1)S(1)} %get-tuple-element.129), channel_id=1, source_target_pairs={{0,8},{2,10},{4,12},{6,14},{8,16},{10,18},{12,20},{14,22},{16,24},... | collective-permute-start | bytes 393224 | tf_op jit(solution)/shard_map/over_tokens/ppermute | solution.py:242
  59.7 7.2 %collective-permute-start.14 = (bf16[2,128,256]{2,1,0:T(8,128)(2,1)S(1)}, bf16[2,128,256]{2,1,0:T(8,128)(2,1)}, u32[]{:S(2)}, u32[]{:S(2)}) collective-permute-start(bf16[2,128,256]{2,1,0:T(8,128)(2,1)S(1)} %get-tuple-element.129), channel_id=1, source_target_pairs={{0,16},{2,18},{4,20},{6,22},{8,24},{10,26},{12,28},{14,30},{16,0},... | collective-permute-start | bytes 393224 | tf_op jit(solution)/shard_map/over_tokens/ppermute | solution.py:242
  78.3 15.8 %collective-permute-start.20 = (bf16[2,4,128,256]{3,2,1,0:T(8,128)(2,1)S(1)}, bf16[2,4,128,256]{3,2,1,0:T(8,128)(2,1)S(1)}, u32[]{:S(2)}, u32[]{:S(2)}) collective-permute-start(bf16[2,4,128,256]{3,2,1,0:T(8,128)(2,1)S(1)} %get-tuple-element.243), channel_id=1, source_target_pairs={{0,4},{2,6},{4,0},{6,2},{8,12},{10,14},{12,8},{14,10},{16,20},{18,... | collective-permute-start | bytes 1572872 | tf_op jit(solution)/shard_map/across_grads/ppermute | solution.py:236
  78.7 15.4 %collective-permute-start.19 = (bf16[2,4,128,256]{3,2,1,0:T(8,128)(2,1)S(1)}, bf16[2,4,128,256]{3,2,1,0:T(8,128)(2,1)S(1)}, u32[]{:S(2)}, u32[]{:S(2)}) collective-permute-start(bf16[2,4,128,256]{3,2,1,0:T(8,128)(2,1)S(1)} %get-tuple-element.244), channel_id=1, source_target_pairs={{0,1},{1,0},{2,3},{3,2},{4,5},{5,4},{6,7},{7,6},{8,9},{9,8},{10,11... | collective-permute-start | bytes 1572872 | tf_op jit(solution)/shard_map/across_grads/ppermute | solution.py:239
  94.2 15.4 %collective-permute-start.24 = (bf16[2,2,4,128,256]{4,3,2,1,0:T(8,128)(2,1)S(1)}, bf16[2,2,4,128,256]{4,3,2,1,0:T(8,128)(2,1)S(1)}, u32[]{:S(2)}, u32[]{:S(2)}) collective-permute-start(bf16[2,2,4,128,256]{4,3,2,1,0:T(8,128)(2,1)S(1)} %pad_maximum_fusion.3.refs_4_.refs_12_), channel_id=1, source_target_pairs={{0,2},{2,0},{4,6},{6,4},{8,10},{10,8},{12,14},{14,12},{16,18},{18,... | collective-permute-start | bytes 3145736 | tf_op jit(solution)/shard_map/over_grads_1/ppermute | solution.py:233
  94.4 15.1 %collective-permute-start.23 = (bf16[2,2,4,128,256]{4,3,2,0,1:T(8,128)(2,1)S(1)}, bf16[2,2,4,128,256]{4,3,2,0,1:T(8,128)(2,1)S(1)}, u32[]{:S(2)}, u32[]{:S(2)}) collective-permute-start(bf16[2,2,4,128,256]{4,3,2,0,1:T(8,128)(2,1)S(1)} %pad_maximum_fusion.2), channel_id=1, source_target_pairs={{0,2},{2,0},{4,6},{6,4},{8,10},{10,8},{12,14},{14,12},{16,18},{18,... | collective-permute-start | bytes 3145736 | tf_op jit(solution)/shard_map/over_grads_1/ppermute | solution.py:233
  95.1 13.9 %collective-permute-start.22 = (bf16[2,4,128,256]{3,2,1,0:T(8,128)(2,1)S(1)}, bf16[2,4,128,256]{3,2,1,0:T(8,128)(2,1)S(1)}, u32[]{:S(2)}, u32[]{:S(2)}) collective-permute-start(bf16[2,4,128,256]{3,2,1,0:T(8,128)(2,1)S(1)} %fusion.18), channel_id=1, source_target_pairs={{0,1},{1,0},{2,3},{3,2},{4,5},{5,4},{6,7},{7,6},{8,9},{9,8},{10,11... | collective-permute-start | bytes 1572872 | tf_op jit(solution)/shard_map/over_grads_1/ppermute | solution.py:239
  96.0 13.6 %collective-permute-start.21 = (bf16[2,4,128,256]{3,2,1,0:T(8,128)(2,1)S(1)}, bf16[2,4,128,256]{3,2,1,0:T(8,128)(2,1)S(1)}, u32[]{:S(2)}, u32[]{:S(2)}) collective-permute-start(bf16[2,4,128,256]{3,2,1,0:T(8,128)(2,1)S(1)} %fusion.20), channel_id=1, source_target_pairs={{0,4},{2,6},{4,0},{6,2},{8,12},{10,14},{12,8},{14,10},{16,20},{18,... | collective-permute-start | bytes 1572872 | tf_op jit(solution)/shard_map/over_grads_1/ppermute | solution.py:236
  109.6 7.2 %collective-permute-start.27 = (bf16[2,2,2,4,128,512]{5,4,3,2,1,0:T(8,128)(2,1)S(1)}, bf16[2,2,2,4,128,512]{5,4,3,2,1,0:T(8,128)(2,1)S(1)}, u32[]{:S(2)}, u32[]{:S(2)}) collective-permute-start(bf16[2,2,2,4,128,512]{5,4,3,2,1,0:T(8,128)(2,1)S(1)} %get-tuple-element.147), channel_id=1, source_target_pairs={{0,2},{2,0},{4,6},{6,4},{8,10},{10,8},{12,14},{14,12},{16,18},{18,... | collective-permute-start | bytes 12582920 | tf_op jit(solution)/shard_map/cores_mixed/ppermute | solution.py:233
  109.6 9.3 %collective-permute-start.25 = (bf16[2,4,128,256]{3,2,1,0:T(8,128)(2,1)S(1)}, bf16[2,4,128,256]{3,2,1,0:T(8,128)(2,1)S(1)}, u32[]{:S(2)}, u32[]{:S(2)}) collective-permute-start(bf16[2,4,128,256]{3,2,1,0:T(8,128)(2,1)S(1)} %collective-permute-done.21.refs_1_), channel_id=1, source_target_pairs={{0,2},{2,0},{4,6},{6,4},{8,10},{10,8},{12,14},{14,12},{16,18},{18,... | collective-permute-start | bytes 1572872 | tf_op jit(solution)/shard_map/cores_mixed/ppermute | solution.py:233
  110.1 8.8 %collective-permute-start.26 = (bf16[2,4,128,256]{3,2,1,0:T(8,128)(2,1)S(1)}, bf16[2,4,128,256]{3,2,1,0:T(8,128)(2,1)S(1)}, u32[]{:S(2)}, u32[]{:S(2)}) collective-permute-start(bf16[2,4,128,256]{3,2,1,0:T(8,128)(2,1)S(1)} %collective-permute-done.22.refs_5_), channel_id=1, source_target_pairs={{0,2},{2,0},{4,6},{6,4},{8,10},{10,8},{12,14},{14,12},{16,18},{18,... | collective-permute-start | bytes 1572872 | tf_op jit(solution)/shard_map/cores_mixed/ppermute | solution.py:233
  110.2 14.8 %collective-permute-start.28 = (bf16[2,4,128,256]{3,2,1,0:T(8,128)(2,1)S(1)}, bf16[2,4,128,256]{3,2,1,0:T(8,128)(2,1)S(1)}, u32[]{:S(2)}, u32[]{:S(2)}) collective-permute-start(bf16[2,4,128,256]{3,2,1,0:T(8,128)(2,1)S(1)} %slice_bitcast_fusion.2), channel_id=1, source_target_pairs={{0,4},{2,6},{4,0},{6,2},{8,12},{10,14},{12,8},{14,10},{16,20},{18,... | collective-permute-start | bytes 1572872 | tf_op jit(solution)/shard_map/over_grads_2/ppermute | solution.py:236
  112.0 14.8 %collective-permute-start.29 = (bf16[2,4,128,256]{3,2,1,0:T(8,128)(2,1)S(1)}, bf16[2,4,128,256]{3,2,1,0:T(8,128)(2,1)S(1)}, u32[]{:S(2)}, u32[]{:S(2)}) collective-permute-start(bf16[2,4,128,256]{3,2,1,0:T(8,128)(2,1)S(1)} %slice_bitcast_fusion.1), channel_id=1, source_target_pairs={{0,1},{1,0},{2,3},{3,2},{4,5},{5,4},{6,7},{7,6},{8,9},{9,8},{10,11... | collective-permute-start | bytes 1572872 | tf_op jit(solution)/shard_map/over_grads_2/ppermute | solution.py:239
  118.9 32.8 %collective-permute-start.32 = (bf16[2,4,128,512]{3,2,1,0:T(8,128)(2,1)S(1)}, bf16[2,4,128,512]{3,2,1,0:T(8,128)(2,1)S(1)}, u32[]{:S(2)}, u32[]{:S(2)}) collective-permute-start(bf16[2,4,128,512]{3,2,1,0:T(8,128)(2,1)S(1)} %get-tuple-element.152), channel_id=1, source_target_pairs={{0,4},{2,6},{4,0},{6,2},{8,12},{10,14},{12,8},{14,10},{16,20},{18,... | collective-permute-start | bytes 3145736 | tf_op jit(solution)/shard_map/over_mixed/ppermute | solution.py:236
  120.7 31.1 %collective-permute-start.33 = (bf16[2,4,128,512]{3,2,1,0:T(8,128)(2,1)S(1)}, bf16[2,4,128,512]{3,2,1,0:T(8,128)(2,1)S(1)}, u32[]{:S(2)}, u32[]{:S(2)}) collective-permute-start(bf16[2,4,128,512]{3,2,1,0:T(8,128)(2,1)S(1)} %get-tuple-element.153), channel_id=1, source_target_pairs={{0,1},{1,0},{2,3},{3,2},{4,5},{5,4},{6,7},{7,6},{8,9},{9,8},{10,11... | collective-permute-start | bytes 3145736 | tf_op jit(solution)/shard_map/over_mixed/ppermute | solution.py:239
  137.4 14.3 %collective-permute-start.34 = (f32[4,4,128]{2,1,0:T(4,128)S(1)}, f32[4,4,128]{2,1,0:T(4,128)S(1)}, u32[]{:S(2)}, u32[]{:S(2)}) collective-permute-start(f32[4,4,128]{2,1,0:T(4,128)S(1)} %get-tuple-element.163), channel_id=1, source_target_pairs={{0,1},{1,0},{2,3},{3,2},{4,5},{5,4},{6,7},{7,6},{8,9},{9,8},{10,11... | collective-permute-start | bytes 24584 | tf_op jit(solution)/shard_map/gates/ppermute | solution.py:239
  151.8 7.7 %collective-permute-start.36 = (bf16[2,2,2,4,128,384]{5,4,3,2,1,0:T(8,128)(2,1)S(1)}, bf16[2,2,2,4,128,384]{5,4,3,2,1,0:T(8,128)(2,1)S(1)}, u32[]{:S(2)}, u32[]{:S(2)}) collective-permute-start(bf16[2,2,2,4,128,384]{5,4,3,2,1,0:T(8,128)(2,1)S(1)} %get-tuple-element.166), channel_id=1, source_target_pairs={{0,2},{2,0},{4,6},{6,4},{8,10},{10,8},{12,14},{14,12},{16,18},{18,... | collective-permute-start | bytes 9437192 | tf_op jit(solution)/shard_map/cores_inputs/ppermute | solution.py:233
  151.8 7.5 %collective-permute-start.35 = (bf16[2,2,2,4,128,128]{5,4,3,2,1,0:T(8,128)(2,1)S(1)}, bf16[2,2,2,4,128,128]{5,4,3,2,1,0:T(8,128)(2,1)S(1)}, u32[]{:S(2)}, u32[]{:S(2)}) collective-permute-start(bf16[2,2,2,4,128,128]{5,4,3,2,1,0:T(8,128)(2,1)S(1)} %get-tuple-element.164), channel_id=1, source_target_pairs={{0,2},{2,0},{4,6},{6,4},{8,10},{10,8},{12,14},{14,12},{16,18},{18,... | collective-permute-start | bytes 3145736 | tf_op jit(solution)/shard_map/cores_inputs/ppermute | solution.py:233
  152.8 15.6 %collective-permute-start.39 = (bf16[4,128,512]{2,1,0:T(8,128)(2,1)S(1)}, bf16[4,128,512]{2,1,0:T(8,128)(2,1)S(1)}, u32[]{:S(2)}, u32[]{:S(2)}) collective-permute-start(bf16[4,128,512]{2,1,0:T(8,128)(2,1)S(1)} %get-tuple-element.221), channel_id=1, source_target_pairs={{0,1},{1,0},{2,3},{3,2},{4,5},{5,4},{6,7},{7,6},{8,9},{9,8},{10,11... | collective-permute-start | bytes 1572872 | tf_op jit(solution)/shard_map/across_mixed/ppermute | solution.py:239
  153.7 14.8 %collective-permute-start.40 = (bf16[4,128,512]{2,1,0:T(8,128)(2,1)S(1)}, bf16[4,128,512]{2,1,0:T(8,128)(2,1)S(1)}, u32[]{:S(2)}, u32[]{:S(2)}) collective-permute-start(bf16[4,128,512]{2,1,0:T(8,128)(2,1)S(1)} %get-tuple-element.220), channel_id=1, source_target_pairs={{0,4},{2,6},{4,0},{6,2},{8,12},{10,14},{12,8},{14,10},{16,20},{18,... | collective-permute-start | bytes 1572872 | tf_op jit(solution)/shard_map/across_mixed/ppermute | solution.py:236
  160.0 28.5 %collective-permute-start.37 = (bf16[2,4,128,384]{3,2,1,0:T(8,128)(2,1)S(1)}, bf16[2,4,128,384]{3,2,1,0:T(8,128)(2,1)S(1)}, u32[]{:S(2)}, u32[]{:S(2)}) collective-permute-start(bf16[2,4,128,384]{3,2,1,0:T(8,128)(2,1)S(1)} %get-tuple-element.171), channel_id=1, source_target_pairs={{0,4},{2,6},{4,0},{6,2},{8,12},{10,14},{12,8},{14,10},{16,20},{18,... | collective-permute-start | bytes 2359304 | tf_op jit(solution)/shard_map/over_inputs_1/ppermute | solution.py:236
  161.8 26.7 %collective-permute-start.38 = (bf16[2,4,128,384]{3,2,1,0:T(8,128)(2,1)S(1)}, bf16[2,4,128,384]{3,2,1,0:T(8,128)(2,1)S(1)}, u32[]{:S(2)}, u32[]{:S(2)}) collective-permute-start(bf16[2,4,128,384]{3,2,1,0:T(8,128)(2,1)S(1)} %get-tuple-element.172), channel_id=1, source_target_pairs={{0,1},{1,0},{2,3},{3,2},{4,5},{5,4},{6,7},{7,6},{8,9},{9,8},{10,11... | collective-permute-start | bytes 2359304 | tf_op jit(solution)/shard_map/over_inputs_1/ppermute | solution.py:239
  169.2 19.3 %collective-permute-start.41 = (bf16[2,128,512]{2,1,0:T(8,128)(2,1)S(1)}, bf16[2,128,512]{2,1,0:T(8,128)(2,1)S(1)}, u32[]{:S(2)}, u32[]{:S(2)}) collective-permute-start(bf16[2,128,512]{2,1,0:T(8,128)(2,1)S(1)} %get-tuple-element.238), channel_id=1, source_target_pairs={{0,16},{2,18},{4,20},{6,22},{8,24},{10,26},{12,28},{14,30},{16,0},... | collective-permute-start | bytes 786440 | tf_op jit(solution)/shard_map/column_mixed/ppermute | solution.py:242
  169.6 18.9 %collective-permute-start.42 = (bf16[2,128,512]{2,1,0:T(8,128)(2,1)S(1)}, bf16[2,128,512]{2,1,0:T(8,128)(2,1)S(1)}, u32[]{:S(2)}, u32[]{:S(2)}) collective-permute-start(bf16[2,128,512]{2,1,0:T(8,128)(2,1)S(1)} %get-tuple-element.237), channel_id=1, source_target_pairs={{0,8},{2,10},{4,12},{6,14},{8,16},{10,18},{12,20},{14,22},{16,24},... | collective-permute-start | bytes 786440 | tf_op jit(solution)/shard_map/column_mixed/ppermute | solution.py:242
  188.8 12.1 %collective-permute-start.45 = (bf16[4,128,384]{2,1,0:T(8,128)(2,1)S(1)}, bf16[4,128,384]{2,1,0:T(8,128)(2,1)S(1)}, u32[]{:S(2)}, u32[]{:S(2)}) collective-permute-start(bf16[4,128,384]{2,1,0:T(8,128)(2,1)S(1)} %get-tuple-element.227), channel_id=1, source_target_pairs={{0,1},{1,0},{2,3},{3,2},{4,5},{5,4},{6,7},{7,6},{8,9},{9,8},{10,11... | collective-permute-start | bytes 1179656 | tf_op jit(solution)/shard_map/across_inputs_1/ppermute | solution.py:239
  189.7 12.1 %collective-permute-start.46 = (bf16[4,128,384]{2,1,0:T(8,128)(2,1)S(1)}, bf16[4,128,384]{2,1,0:T(8,128)(2,1)S(1)}, u32[]{:S(2)}, u32[]{:S(2)}) collective-permute-start(bf16[4,128,384]{2,1,0:T(8,128)(2,1)S(1)} %get-tuple-element.226), channel_id=1, source_target_pairs={{0,4},{2,6},{4,0},{6,2},{8,12},{10,14},{12,8},{14,10},{16,20},{18,... | collective-permute-start | bytes 1179656 | tf_op jit(solution)/shard_map/across_inputs_1/ppermute | solution.py:236
  191.1 6.8 %collective-permute-start.47 = (bf16[2,128,512]{2,1,0:T(8,128)(2,1)S(1)}, bf16[2,128,512]{2,1,0:T(8,128)(2,1)S(1)}, u32[]{:S(2)}, u32[]{:S(2)}) collective-permute-start(bf16[2,128,512]{2,1,0:T(8,128)(2,1)S(1)} %get-tuple-element.236), channel_id=1, source_target_pairs={{0,24},{2,26},{4,28},{6,30},{8,0},{10,2},{12,4},{14,6},{16,8},{18,... | collective-permute-start | bytes 786440 | tf_op jit(solution)/shard_map/column_mixed/ppermute | solution.py:242
  191.1 14.1 %collective-permute-start.43 = (bf16[2,4,128,128]{3,2,1,0:T(8,128)(2,1)S(1)}, bf16[2,4,128,128]{3,2,1,0:T(8,128)(2,1)S(1)}, u32[]{:S(2)}, u32[]{:S(2)}) collective-permute-start(bf16[2,4,128,128]{3,2,1,0:T(8,128)(2,1)S(1)} %get-tuple-element.185), channel_id=1, source_target_pairs={{0,4},{2,6},{4,0},{6,2},{8,12},{10,14},{12,8},{14,10},{16,20},{18,... | collective-permute-start | bytes 786440 | tf_op jit(solution)/shard_map/over_inputs_2/ppermute | solution.py:236
  191.9 13.4 %collective-permute-start.44 = (bf16[2,4,128,128]{3,2,1,0:T(8,128)(2,1)S(1)}, bf16[2,4,128,128]{3,2,1,0:T(8,128)(2,1)S(1)}, u32[]{:S(2)}, u32[]{:S(2)}) collective-permute-start(bf16[2,4,128,128]{3,2,1,0:T(8,128)(2,1)S(1)} %get-tuple-element.186), channel_id=1, source_target_pairs={{0,1},{1,0},{2,3},{3,2},{4,5},{5,4},{6,7},{7,6},{8,9},{9,8},{10,11... | collective-permute-start | bytes 786440 | tf_op jit(solution)/shard_map/over_inputs_2/ppermute | solution.py:239
  202.3 19.0 %collective-permute-start.53 = (bf16[2,128,384]{2,1,0:T(8,128)(2,1)S(1)}, bf16[2,128,384]{2,1,0:T(8,128)(2,1)S(1)}, u32[]{:S(2)}, u32[]{:S(2)}) collective-permute-start(bf16[2,128,384]{2,1,0:T(8,128)(2,1)S(1)} %get-tuple-element.239), channel_id=1, source_target_pairs={{0,24},{2,26},{4,28},{6,30},{8,0},{10,2},{12,4},{14,6},{16,8},{18,... | collective-permute-start | bytes 589832 | tf_op jit(solution)/shard_map/column_inputs_1/ppermute | solution.py:242
  202.3 20.1 %collective-permute-start.54 = (bf16[2,128,384]{2,1,0:T(8,128)(2,1)S(1)}, bf16[2,128,384]{2,1,0:T(8,128)(2,1)S(1)}, u32[]{:S(2)}, u32[]{:S(2)}) collective-permute-start(bf16[2,128,384]{2,1,0:T(8,128)(2,1)S(1)} %get-tuple-element.241), channel_id=1, source_target_pairs={{0,16},{2,18},{4,20},{6,22},{8,24},{10,26},{12,28},{14,30},{16,0},... | collective-permute-start | bytes 589832 | tf_op jit(solution)/shard_map/column_inputs_1/ppermute | solution.py:242
  202.7 19.7 %collective-permute-start.55 = (bf16[2,128,384]{2,1,0:T(8,128)(2,1)S(1)}, bf16[2,128,384]{2,1,0:T(8,128)(2,1)S(1)}, u32[]{:S(2)}, u32[]{:S(2)}) collective-permute-start(bf16[2,128,384]{2,1,0:T(8,128)(2,1)S(1)} %get-tuple-element.240), channel_id=1, source_target_pairs={{0,8},{2,10},{4,12},{6,14},{8,16},{10,18},{12,20},{14,22},{16,24},... | collective-permute-start | bytes 589832 | tf_op jit(solution)/shard_map/column_inputs_1/ppermute | solution.py:242
  213.0 10.4 %all-to-all-start = ((f32[16,1,128]{2,1,0:T(1,128)}), f32[16,1,128]{2,1,0:T(1,128)S(1)}, u32[]{:S(2)}, u32[]{:S(2)}) async-start(f32[16,1,128]{2,1,0:T(1,128)} %bitcast.94), calls=%async_computation | async-start | bytes 16384 | tf_op jit(solution)/shard_map/gates/all_to_all | solution.py:302
  217.6 6.5 %collective-permute-start.50 = (bf16[2,128,128]{2,1,0:T(8,128)(2,1)}, bf16[2,128,128]{2,1,0:T(8,128)(2,1)S(1)}, u32[]{:S(2)}, u32[]{:S(2)}) collective-permute-start(bf16[2,128,128]{2,1,0:T(8,128)(2,1)} %get-tuple-element.250), channel_id=1, source_target_pairs={{0,24},{2,26},{4,28},{6,30},{8,0},{10,2},{12,4},{14,6},{16,8},{18,... | collective-permute-start | bytes 196616 | tf_op jit(solution)/shard_map/column_inputs_2/ppermute | solution.py:242
  221.3 7.1 %collective-permute-start.51 = (bf16[2,128,128]{2,1,0:T(8,128)(2,1)}, bf16[2,128,128]{2,1,0:T(8,128)(2,1)S(1)}, u32[]{:S(2)}, u32[]{:S(2)}) collective-permute-start(bf16[2,128,128]{2,1,0:T(8,128)(2,1)} %get-tuple-element.249), channel_id=1, source_target_pairs={{0,16},{2,18},{4,20},{6,22},{8,24},{10,26},{12,28},{14,30},{16,0},... | collective-permute-start | bytes 196616 | tf_op jit(solution)/shard_map/column_inputs_2/ppermute | solution.py:242
  221.3 7.1 %collective-permute-start.52 = (bf16[2,128,128]{2,1,0:T(8,128)(2,1)}, bf16[2,128,128]{2,1,0:T(8,128)(2,1)S(1)}, u32[]{:S(2)}, u32[]{:S(2)}) collective-permute-start(bf16[2,128,128]{2,1,0:T(8,128)(2,1)} %get-tuple-element.248), channel_id=1, source_target_pairs={{0,8},{2,10},{4,12},{6,14},{8,16},{10,18},{12,20},{14,22},{16,24},... | collective-permute-start | bytes 196616 | tf_op jit(solution)/shard_map/column_inputs_2/ppermute | solution.py:242
  (30 other events, 226.8 us)
